TPU v7x, 128 devices: a whole 4x4x4 slice. The times are simulated.
128 devices in a mesh: blk: 16 (over x, y_hi, core), rep: 8 (over y_lo, z).
Axes of the slice: x: 4, y: 4 (y_hi: 2, y_lo: 2; y = y_hi * 2 + y_lo), z: 4, core: 2. Of those that a mesh axis runs over, the one named last changes fastest.
Arguments:
- user_factors: float32 [131072, 256], P(('blk', 'rep')), may hold values from -1.5 to 1.5
- user_first: float32 [131072, 256], P(('blk', 'rep')), may hold values from -6 to 6
- user_second: float32 [131072, 256], P(('blk', 'rep')), may hold values from 0.5 to 20
- item_factors: float32 [8192, 256], P(('blk', 'rep')), may hold values from -1.5 to 1.5
- item_first: float32 [8192, 256], P(('blk', 'rep')), may hold values from -6 to 6
- item_second: float32 [8192, 256], P(('blk', 'rep')), may hold values from 0.5 to 20
- block_rows: int32 [16, 8, 8, 8], P('blk', 'rep'), may hold values from 0 to 7, as said below
- block_cols: int32 [16, 8, 8, 8], P('blk', 'rep'), may hold values from 0 to 3
- live_slots: int32 [16, 8, 8], P('blk', 'rep'), may hold values from 2 to 8, as said below
- teacher: bfloat16 [16, 8, 8, 8, 128, 128], P('blk', 'rep'), may hold values from -6 to 6
Outputs:
- user_values: float32 [131072, 256], P(('blk', 'rep'))
- user_moment_one: float32 [131072, 256], P(('blk', 'rep'))
- user_moment_two: float32 [131072, 256], P(('blk', 'rep'))
- item_values: float32 [8192, 256], P(('blk', 'rep'))
- item_moment_one: float32 [8192, 256], P(('blk', 'rep'))
- item_moment_two: float32 [8192, 256], P(('blk', 'rep'))
Inputs may be any that keep to these rules, and one draw needn't show every extreme that they name: For each (g, q, s) the 8 pairs (block_rows, block_cols) are distinct. `live_slots`: some entry equals 8 in every draw.
All inputs are finite; a program needn't handle non-finite values.
Results may differ from a plain program's by a relative error of at most 0.0034.
Values may be sent and summed in bfloat16 or wider, within the bound.
No kernel may reach another device: no remote copies, remote signals or barrier semaphores. Data moves between devices by JAX's collectives and lax.ppermute only.
A program may use at most 64 MiB of HBM per device.

v0:
```python
import jax
import jax.numpy as jnp
from jax import lax
from jax.sharding import PartitionSpec as P

learn_rate = 0.01
adam_eps = 1e-08


def shifted(value, axis, steps):
    count = lax.axis_size(axis)
    pairs = [(source, (source + steps) % count) for source in range(count)]
    return lax.ppermute(value, axis, pairs)


def adam_stack(stacked, gradient):
    moment_one = 0.9 * stacked[1] + 0.1 * gradient
    moment_two = 0.99 * stacked[2] + 0.01 * gradient * gradient
    values = stacked[0] - learn_rate * moment_one / (jnp.sqrt(moment_two) + adam_eps)
    return jnp.stack([values, moment_one, moment_two])


def stratum_grads(user_bf, panel_bf, row_ids, col_ids, live_count, scores):
    block_edge = scores.shape[-1]
    rank_width = user_bf.shape[1]
    user_count = user_bf.shape[0] // block_edge
    item_count = panel_bf.shape[0] // block_edge
    slot_count = row_ids.shape[0]
    user_blocks = jnp.take(user_bf.reshape(user_count, block_edge, rank_width), row_ids, axis=0)
    item_blocks = jnp.take(panel_bf.reshape(item_count, block_edge, rank_width), col_ids, axis=0)
    predicted = jnp.einsum(
        "sur,sir->sui", user_blocks, item_blocks, preferred_element_type=jnp.float32
    )
    active = (jnp.arange(slot_count) < live_count)[:, None, None]
    residual = jnp.where(active, predicted - scores.astype(jnp.float32), 0.0).astype(jnp.bfloat16)
    user_terms = jnp.einsum(
        "sui,sir->sur", residual, item_blocks, preferred_element_type=jnp.float32
    )
    item_terms = jnp.einsum(
        "sui,sur->sir", residual, user_blocks, preferred_element_type=jnp.float32
    )
    row_hot = (row_ids[None, :] == jnp.arange(user_count)[:, None]).astype(jnp.float32)
    col_hot = (col_ids[None, :] == jnp.arange(item_count)[:, None]).astype(jnp.float32)
    user_grad = jnp.einsum("bs,sur->bur", row_hot, user_terms, precision=lax.Precision.HIGHEST)
    item_grad = jnp.einsum("cs,sir->cir", col_hot, item_terms, precision=lax.Precision.HIGHEST)
    return (
        user_grad.reshape(user_bf.shape[0], rank_width),
        item_grad.reshape(panel_bf.shape[0], rank_width),
    )


def on_device(
    user_factors,
    user_first,
    user_second,
    item_factors,
    item_first,
    item_second,
    block_rows,
    block_cols,
    live_slots,
    teacher,
):
    shard_rows = item_factors.shape[0]
    user_state = jnp.stack([user_factors, user_first, user_second])
    item_state = jnp.stack([item_factors, item_first, item_second])
    strata_count = block_rows.shape[2]
    item_state = lax.all_gather(item_state, "rep", axis=1, tiled=True)
    for stratum in range(strata_count):
        user_bf = user_state[0].astype(jnp.bfloat16)
        panel_bf = item_state[0].astype(jnp.bfloat16)
        user_grad, item_grad = stratum_grads(
            user_bf,
            panel_bf,
            block_rows[0, 0, stratum],
            block_cols[0, 0, stratum],
            live_slots[0, 0, stratum],
            teacher[0, 0, stratum],
        )
        item_grad = lax.psum(item_grad, "rep")
        user_state = adam_stack(user_state, user_grad)
        item_state = adam_stack(item_state, item_grad)
        item_state = shifted(item_state, "blk", -1)
    offset = lax.axis_index("rep") * shard_rows
    item_state = lax.dynamic_slice_in_dim(item_state, offset, shard_rows, 1)
    return (
        user_state[0],
        user_state[1],
        user_state[2],
        item_state[0],
        item_state[1],
        item_state[2],
    )


def solution(mesh):
    in_specs = (
        P(("blk", "rep"), None),
        P(("blk", "rep"), None),
        P(("blk", "rep"), None),
        P(("blk", "rep"), None),
        P(("blk", "rep"), None),
        P(("blk", "rep"), None),
        P("blk", "rep", None, None),
        P("blk", "rep", None, None),
        P("blk", "rep", None),
        P("blk", "rep", None, None, None, None),
    )
    out_specs = (
        P(("blk", "rep"), None),
        P(("blk", "rep"), None),
        P(("blk", "rep"), None),
        P(("blk", "rep"), None),
        P(("blk", "rep"), None),
        P(("blk", "rep"), None),
    )
    return jax.shard_map(
        on_device, mesh=mesh, in_specs=in_specs, out_specs=out_specs, check_vma=False
    )
```

profile of v0, /device:TPU:1, one launch (start us, length us, event | category | flops | bytes accessed | tf_op | source)
XLA Modules:
  0.0 892.8 jit_solution(7296742571262334292)
XLA Ops:
  12.2 35.8 %all-gather.2.cloned.1.call-done = f32[3,512,256]{2,1,0:T(8,128)} async-done(((f32[3,64,256]{2,1,0:T(8,128)}), f32[3,512,256]{2,1,0:T(8,128)}) %all-gather.2.cloned.1.call-update) | async-done | bytes 1572880 | tf_op jit(solution)/shard_map/all_gather | solution.py:68
  53.5 75.6 %all-reduce.9.cloned.1.call-done = f32[512,256]{1,0:T(8,128)} async-done(((f32[512,256]{1,0:T(8,128)}), f32[512,256]{1,0:T(8,128)}) %all-reduce.9.cloned.1.call-update) | async-done | bytes 524304 | tf_op jit(solution)/shard_map/psum | solution.py:80
  131.8 5.7 collective-permute-start
  143.6 14.7 %collective-permute-done = f32[3,512,256]{2,1,0:T(8,128)} collective-permute-done((f32[3,512,256]{2,1,0:T(8,128)}, f32[3,512,256]{2,1,0:T(8,128)}, u32[]{:S(2)}, u32[]{:S(2)}) %collective-permute-start) | collective-permute-done | bytes 1572896 | tf_op jit(solution)/shard_map/ppermute | solution.py:13
  163.7 68.1 %all-reduce.11.cloned.1.call-done = f32[512,256]{1,0:T(8,128)} async-done(((f32[512,256]{1,0:T(8,128)}), f32[512,256]{1,0:T(8,128)}) %all-reduce.11.cloned.1.call-update) | async-done | bytes 524304 | tf_op jit(solution)/shard_map/psum | solution.py:80
  234.9 5.9 collective-permute-start.1
  249.1 12.5 %collective-permute-done.1 = f32[3,512,256]{2,1,0:T(8,128)} collective-permute-done((f32[3,512,256]{2,1,0:T(8,128)}, f32[3,512,256]{2,1,0:T(8,128)}, u32[]{:S(2)}, u32[]{:S(2)}) %collective-permute-start.1) | collective-permute-done | bytes 1572896 | tf_op jit(solution)/shard_map/ppermute | solution.py:13
  268.0 68.1 %all-reduce.13.cloned.1.call-done = f32[512,256]{1,0:T(8,128)} async-done(((f32[512,256]{1,0:T(8,128)}), f32[512,256]{1,0:T(8,128)}) %all-reduce.13.cloned.1.call-update) | async-done | bytes 524304 | tf_op jit(solution)/shard_map/psum | solution.py:80
  339.2 5.7 collective-permute-start.2
  352.3 13.4 %collective-permute-done.2 = f32[3,512,256]{2,1,0:T(8,128)} collective-permute-done((f32[3,512,256]{2,1,0:T(8,128)}, f32[3,512,256]{2,1,0:T(8,128)}, u32[]{:S(2)}, u32[]{:S(2)}) %collective-permute-start.2) | collective-permute-done | bytes 1572896 | tf_op jit(solution)/shard_map/ppermute | solution.py:13
  371.2 68.1 %all-reduce.15.cloned.1.call-done = f32[512,256]{1,0:T(8,128)} async-done(((f32[512,256]{1,0:T(8,128)}), f32[512,256]{1,0:T(8,128)}) %all-reduce.15.cloned.1.call-update) | async-done | bytes 524304 | tf_op jit(solution)/shard_map/psum | solution.py:80
  442.3 5.9 collective-permute-start.3
  455.4 13.6 %collective-permute-done.3 = f32[3,512,256]{2,1,0:T(8,128)} collective-permute-done((f32[3,512,256]{2,1,0:T(8,128)}, f32[3,512,256]{2,1,0:T(8,128)}, u32[]{:S(2)}, u32[]{:S(2)}) %collective-permute-start.3) | collective-permute-done | bytes 1572896 | tf_op jit(solution)/shard_map/ppermute | solution.py:13
  474.5 68.1 %all-reduce.17.cloned.1.call-done = f32[512,256]{1,0:T(8,128)} async-done(((f32[512,256]{1,0:T(8,128)}), f32[512,256]{1,0:T(8,128)}) %all-reduce.17.cloned.1.call-update) | async-done | bytes 524304 | tf_op jit(solution)/shard_map/psum | solution.py:80
  545.7 5.7 collective-permute-start.4
  559.5 12.6 %collective-permute-done.4 = f32[3,512,256]{2,1,0:T(8,128)} collective-permute-done((f32[3,512,256]{2,1,0:T(8,128)}, f32[3,512,256]{2,1,0:T(8,128)}, u32[]{:S(2)}, u32[]{:S(2)}) %collective-permute-start.4) | collective-permute-done | bytes 1572896 | tf_op jit(solution)/shard_map/ppermute | solution.py:13
  578.8 68.1 %all-reduce.19.cloned.1.call-done = f32[512,256]{1,0:T(8,128)} async-done(((f32[512,256]{1,0:T(8,128)}), f32[512,256]{1,0:T(8,128)}) %all-reduce.19.cloned.1.call-update) | async-done | bytes 524304 | tf_op jit(solution)/shard_map/psum | solution.py:80
  650.0 6.1 collective-permute-start.5
  663.3 13.6 %collective-permute-done.5 = f32[3,512,256]{2,1,0:T(8,128)} collective-permute-done((f32[3,512,256]{2,1,0:T(8,128)}, f32[3,512,256]{2,1,0:T(8,128)}, u32[]{:S(2)}, u32[]{:S(2)}) %collective-permute-start.5) | collective-permute-done | bytes 1572896 | tf_op jit(solution)/shard_map/ppermute | solution.py:13
  682.4 68.1 %all-reduce.21.cloned.1.call-done = f32[512,256]{1,0:T(8,128)} async-done(((f32[512,256]{1,0:T(8,128)}), f32[512,256]{1,0:T(8,128)}) %all-reduce.21.cloned.1.call-update) | async-done | bytes 524304 | tf_op jit(solution)/shard_map/psum | solution.py:80
  767.7 12.3 %collective-permute-done.6 = f32[3,512,256]{2,1,0:T(8,128)} collective-permute-done((f32[3,512,256]{2,1,0:T(8,128)}, f32[3,512,256]{2,1,0:T(8,128)}, u32[]{:S(2)}, u32[]{:S(2)}) %collective-permute-start.6) | collective-permute-done | bytes 1572896 | tf_op jit(solution)/shard_map/ppermute | solution.py:13
  786.6 68.1 %all-reduce.23.cloned.1.call-done = f32[512,256]{1,0:T(8,128)} async-done(((f32[512,256]{1,0:T(8,128)}), f32[512,256]{1,0:T(8,128)}) %all-reduce.23.cloned.1.call-update) | async-done | bytes 524304 | tf_op jit(solution)/shard_map/psum | solution.py:80
  857.9 5.9 collective-permute-start.7
  869.8 14.7 %collective-permute-done.7 = f32[3,512,256]{2,1,0:T(8,128)} collective-permute-done((f32[3,512,256]{2,1,0:T(8,128)}, f32[3,512,256]{2,1,0:T(8,128)}, u32[]{:S(2)}, u32[]{:S(2)}) %collective-permute-start.7) | collective-permute-done | bytes 1572896 | tf_op jit(solution)/shard_map/ppermute | solution.py:13
  (210 shorter events, 141.5 us)
Async XLA Ops:
  7.2 3.0 copy-start.26
  7.2 40.8 %all-gather.2.cloned.1.call-start = ((), (), s32[]{:S(2)}) async-start(), calls=%async_computation | async-start | bytes 1769472 | tf_op jit(solution)/shard_map/all_gather | solution.py:68
  7.2 3.6 copy-start.25
  8.9 120.3 %all-reduce.9.cloned.1.call-start = ((), (), s32[]{:S(2)}) async-start(), calls=%async_computation.1 | async-start | bytes 1048576 | tf_op jit(solution)/shard_map/psum | solution.py:80
  51.4 77.7 %copy-start.18 = (f32[3,512,256]{2,1,0:T(8,128)S(1)}, f32[3,512,256]{2,1,0:T(8,128)}, u32[]{:S(2)}) copy-start(f32[3,512,256]{2,1,0:T(8,128)} %all-gather.2.cloned.1.call-done) | copy-start | bytes 4718596
  53.5 178.3 %all-reduce.11.cloned.1.call-start = ((), (), s32[]{:S(2)}) async-start(), calls=%async_computation.2 | async-start | bytes 1048576 | tf_op jit(solution)/shard_map/psum | solution.py:80
  131.8 26.5 %collective-permute-start = (f32[3,512,256]{2,1,0:T(8,128)}, f32[3,512,256]{2,1,0:T(8,128)}, u32[]{:S(2)}, u32[]{:S(2)}) collective-permute-start(f32[3,512,256]{2,1,0:T(8,128)} %pad_maximum_fusion), channel_id=1, source_target_pairs={{0,120},{8,0},{16,8},{24,16},{32,24},{40,32},{48,40},{56,48},{64,5... | collective-permute-start | bytes 4718600 | tf_op jit(solution)/shard_map/ppermute | solution.py:13
  163.7 172.4 %all-reduce.13.cloned.1.call-start = ((), (), s32[]{:S(2)}) async-start(), calls=%async_computation.3 | async-start | bytes 1048576 | tf_op jit(solution)/shard_map/psum | solution.py:80
  234.9 26.6 %collective-permute-start.1 = (f32[3,512,256]{2,1,0:T(8,128)}, f32[3,512,256]{2,1,0:T(8,128)}, u32[]{:S(2)}, u32[]{:S(2)}) collective-permute-start(f32[3,512,256]{2,1,0:T(8,128)} %pad_maximum_fusion.1), channel_id=1, source_target_pairs={{0,120},{8,0},{16,8},{24,16},{32,24},{40,32},{48,40},{56,48},{64,5... | collective-permute-start | bytes 4718600 | tf_op jit(solution)/shard_map/ppermute | solution.py:13
  246.3 101.3 %copy-start = (f32[1024,256]{1,0:T(8,128)}, f32[1024,256]{1,0:T(8,128)S(1)}, u32[]{:S(2)}) copy-start(f32[1024,256]{1,0:T(8,128)S(1)} %get-tuple-element.49) | copy-start | bytes 3145732
  268.0 171.3 %all-reduce.15.cloned.1.call-start = ((), (), s32[]{:S(2)}) async-start(), calls=%async_computation.4 | async-start | bytes 1048576 | tf_op jit(solution)/shard_map/psum | solution.py:80
  337.9 7.7 copy-start.20
  339.2 26.5 %collective-permute-start.2 = (f32[3,512,256]{2,1,0:T(8,128)}, f32[3,512,256]{2,1,0:T(8,128)}, u32[]{:S(2)}, u32[]{:S(2)}) collective-permute-start(f32[3,512,256]{2,1,0:T(8,128)} %pad_maximum_fusion.2), channel_id=1, source_target_pairs={{0,120},{8,0},{16,8},{24,16},{32,24},{40,32},{48,40},{56,48},{64,5... | collective-permute-start | bytes 4718600 | tf_op jit(solution)/shard_map/ppermute | solution.py:13
  347.6 3.1 copy-start.2
  371.1 171.5 %all-reduce.17.cloned.1.call-start = ((), (), s32[]{:S(2)}) async-start(), calls=%async_computation.5 | async-start | bytes 1048576 | tf_op jit(solution)/shard_map/psum | solution.py:80
  442.3 26.7 %collective-permute-start.3 = (f32[3,512,256]{2,1,0:T(8,128)}, f32[3,512,256]{2,1,0:T(8,128)}, u32[]{:S(2)}, u32[]{:S(2)}) collective-permute-start(f32[3,512,256]{2,1,0:T(8,128)} %pad_maximum_fusion.3), channel_id=1, source_target_pairs={{0,120},{8,0},{16,8},{24,16},{32,24},{40,32},{48,40},{56,48},{64,5... | collective-permute-start | bytes 4718600 | tf_op jit(solution)/shard_map/ppermute | solution.py:13
  474.5 172.4 %all-reduce.19.cloned.1.call-start = ((), (), s32[]{:S(2)}) async-start(), calls=%async_computation.6 | async-start | bytes 1048576 | tf_op jit(solution)/shard_map/psum | solution.py:80
  545.7 26.5 %collective-permute-start.4 = (f32[3,512,256]{2,1,0:T(8,128)}, f32[3,512,256]{2,1,0:T(8,128)}, u32[]{:S(2)}, u32[]{:S(2)}) collective-permute-start(f32[3,512,256]{2,1,0:T(8,128)} %pad_maximum_fusion.4), channel_id=1, source_target_pairs={{0,120},{8,0},{16,8},{24,16},{32,24},{40,32},{48,40},{56,48},{64,5... | collective-permute-start | bytes 4718600 | tf_op jit(solution)/shard_map/ppermute | solution.py:13
  578.8 171.7 %all-reduce.21.cloned.1.call-start = ((), (), s32[]{:S(2)}) async-start(), calls=%async_computation.7 | async-start | bytes 1048576 | tf_op jit(solution)/shard_map/psum | solution.py:80
  648.7 8.0 copy-start.21
  650.0 26.9 %collective-permute-start.5 = (f32[3,512,256]{2,1,0:T(8,128)}, f32[3,512,256]{2,1,0:T(8,128)}, u32[]{:S(2)}, u32[]{:S(2)}) collective-permute-start(f32[3,512,256]{2,1,0:T(8,128)} %pad_maximum_fusion.5), channel_id=1, source_target_pairs={{0,120},{8,0},{16,8},{24,16},{32,24},{40,32},{48,40},{56,48},{64,5... | collective-permute-start | bytes 4718600 | tf_op jit(solution)/shard_map/ppermute | solution.py:13
  682.3 172.4 %all-reduce.23.cloned.1.call-start = ((), (), s32[]{:S(2)}) async-start(), calls=%async_computation.8 | async-start | bytes 1048576 | tf_op jit(solution)/shard_map/psum | solution.py:80
  753.5 26.5 %collective-permute-start.6 = (f32[3,512,256]{2,1,0:T(8,128)}, f32[3,512,256]{2,1,0:T(8,128)}, u32[]{:S(2)}, u32[]{:S(2)}) collective-permute-start(f32[3,512,256]{2,1,0:T(8,128)} %pad_maximum_fusion.6), channel_id=1, source_target_pairs={{0,120},{8,0},{16,8},{24,16},{32,24},{40,32},{48,40},{56,48},{64,5... | collective-permute-start | bytes 4718600 | tf_op jit(solution)/shard_map/ppermute | solution.py:13
  857.9 26.6 %collective-permute-start.7 = (f32[3,512,256]{2,1,0:T(8,128)}, f32[3,512,256]{2,1,0:T(8,128)}, u32[]{:S(2)}, u32[]{:S(2)}) collective-permute-start(f32[3,512,256]{2,1,0:T(8,128)} %pad_maximum_fusion.7), channel_id=1, source_target_pairs={{0,120},{8,0},{16,8},{24,16},{32,24},{40,32},{48,40},{56,48},{64,5... | collective-permute-start | bytes 4718600 | tf_op jit(solution)/shard_map/ppermute | solution.py:13
  (21 other events, 31.8 us)
Sparse Core Ops, SparseCore 0:
  10.2 37.7 all-gather.1
  53.6 75.4 all-reduce.8
  163.8 67.9 all-reduce.10
  268.1 67.9 all-reduce.12
  371.3 67.9 all-reduce.14
  474.6 67.9 all-reduce.16
  578.9 67.9 all-reduce.18
  682.4 67.9 all-reduce.20
  786.8 67.9 all-reduce.22
where the time goes:
time: 901 us; the launch traced here: 893 us
  waiting for transfers between devices  695 us (77%)
  local copies, waits for them, and re-layouts  49.5 us (5%)
  other arithmetic  48.6 us (5%)
  starting transfers between devices  47.1 us (5%)
  matrix products  37.1 us (4%)
  between operations  15.1 us (2%)
    psum x8, waiting for transfers between devices, on_device(): item_grad = lax.psum(item_grad, 'rep')  552 us
    ppermute x8, waiting for transfers between devices, shifted(): return lax.ppermute(value, axis, pairs)  107 us
    ppermute x8, starting transfers between devices, shifted(): return lax.ppermute(value, axis, pairs)  46.7 us
    all_gather x1, waiting for transfers between devices, on_device(): item_state = lax.all_gather(item_state, 'rep', axis=1, tiled=True)  35.8 us
    another operation x16, other arithmetic, adam_stack(): return jnp.stack([values, moment_one, moment_two])  24.3 us
  transfers between devices with their start and end apart: 17, of which 17 were waited for; matrix products, arithmetic and copies ran while one was open for 6% of the time, Pallas kernels for 0%

commit v1 on v0

v1 whole, which is shorter than its diff:
```python
import functools

import jax
import jax.numpy as jnp
from jax import lax
from jax.experimental import pallas as pl
from jax.experimental.pallas import tpu as pltpu
from jax.sharding import PartitionSpec as P

learn_rate = 0.01
adam_eps = 1e-08
EDGE = 128
VMEM = pltpu.VMEM
F32 = jnp.float32
BF16 = jnp.bfloat16


def adam(values, moment_one, moment_two, gradient):
    moment_one = 0.9 * moment_one + 0.1 * gradient
    moment_two = 0.99 * moment_two + 0.01 * gradient * gradient
    values = values - learn_rate * moment_one / (jnp.sqrt(moment_two) + adam_eps)
    return values, moment_one, moment_two


def block_at(index):
    return pl.ds(pl.multiple_of(index * EDGE, EDGE), EDGE)


def item_grad_kernel(stratum, slots, meta, items, users, teacher, grad, residual):
    grad[...] = jnp.zeros_like(grad)
    live = meta[stratum, 2 * slots]
    for slot in range(slots):
        user_block = users[block_at(meta[stratum, slot]), :]
        col = block_at(meta[stratum, slots + slot])
        predicted = lax.dot_general(
            user_block, items[col, :], (((1,), (1,)), ((), ())), preferred_element_type=F32
        )
        left = jnp.where(slot < live, predicted - teacher[stratum, slot].astype(F32), 0.0).astype(BF16)
        residual[slot] = left
        grad[col, :] += lax.dot_general(
            left, user_block, (((0,), (0,)), ((), ())), preferred_element_type=F32
        )


def user_grads(stratum, slots, meta, items, residual, grad):
    grad[...] = jnp.zeros_like(grad)
    for slot in range(slots):
        col = block_at(meta[stratum, slots + slot])
        grad[meta[stratum, slot]] += jnp.dot(residual[slot], items[col, :], preferred_element_type=F32)


def user_kernel(stratum, slots, meta, items, residual, values, one, two, values_out, one_out, two_out, rounded, grad):
    user_grads(stratum, slots, meta, items, residual, grad)

    def one_block(at, carry):
        rows = block_at(at)
        new, first, second = adam(values[rows, :], one[rows, :], two[rows, :], grad[at])
        values_out[rows, :] = new
        one_out[rows, :] = first
        two_out[rows, :] = second
        rounded[rows, :] = new.astype(BF16)
        return carry

    lax.fori_loop(0, grad.shape[0], one_block, 0)


def last_user_kernel(stratum, slots, meta, items, residual, values, one, two, values_out, one_out, two_out, grad):
    at = pl.program_id(0)

    @pl.when(at == 0)
    def _():
        user_grads(stratum, slots, meta, items, residual, grad)

    values_out[...], one_out[...], two_out[...] = adam(values[...], one[...], two[...], grad[at])


def owner_kernel(parts, values, moments, values_out, moments_out):
    total = parts[0]
    for part in range(1, parts.shape[0]):
        total += parts[part]
    values_out[...], moments_out[0], moments_out[1] = adam(values[...], moments[0], moments[1], total)


def vmem_specs(count):
    return [pl.BlockSpec(memory_space=VMEM)] * count


def in_vmem(*arrays):
    return [pltpu.with_memory_space_constraint(a, VMEM) for a in arrays]


LIMIT = pltpu.CompilerParams(vmem_limit_bytes=6 * 1024 * 1024)

USER_COST = pl.CostEstimate(flops=300_000_000, bytes_accessed=8_000_000, transcendentals=600_000)


def on_device(
    user_factors,
    user_first,
    user_second,
    item_factors,
    item_first,
    item_second,
    block_rows,
    block_cols,
    live_slots,
    teacher,
):
    strata, slots = block_rows.shape[2], block_rows.shape[3]
    user_rows, rank = user_factors.shape
    shard = item_factors.shape[0]
    groups, reps = lax.axis_size("blk"), lax.axis_size("rep")
    half = reps // 2
    item_rows = shard * reps

    def owner(group, rep):
        return rep if group % 2 else (rep + half) % reps

    moves = [
        (group * reps + rep, ((group - 1) % groups) * reps + owner(group, rep))
        for group in range(groups)
        for rep in range(reps)
    ]

    def shifted(value):
        return lax.ppermute(value, ("blk", "rep"), moves)

    parity = lax.axis_index("blk") % 2
    turned = jnp.array(
        [[sum((p + hop) % 2 == 0 for hop in range(1, s + 1)) % 2 for s in range(strata)] for p in range(2)], jnp.int32
    )[parity]
    item_blocks = item_rows // EDGE
    cols = (block_cols[0, 0] + turned[:, None] * (item_blocks // 2)) % item_blocks
    meta = jnp.concatenate([block_rows[0, 0], cols, live_slots[0, 0][:, None]], axis=1)
    smem = pl.BlockSpec(memory_space=pltpu.SMEM)

    scores = teacher[0, 0]
    values, moments = item_factors, jnp.stack([item_first, item_second])
    users = (user_factors, user_first, user_second)
    user_bf = user_factors.astype(BF16)

    for stratum in range(strata):
        last = stratum == strata - 1
        copies = jnp.broadcast_to(values.astype(BF16)[None], (reps, shard, rank))
        items = lax.all_to_all(copies, "rep", 0, 0).reshape(item_rows, rank)
        grad, residual = pl.pallas_call(
            functools.partial(item_grad_kernel, stratum, slots),
            in_specs=[smem] + vmem_specs(3),
            out_specs=vmem_specs(2),
            out_shape=[VMEM((item_rows, rank), F32), VMEM((slots, EDGE, EDGE), BF16)],
            compiler_params=LIMIT,
            name="item_grad",
        )(meta, *in_vmem(items, user_bf, scores))
        parts = lax.all_to_all(grad.reshape(reps, shard, rank), "rep", 0, 0)
        values, moments = pl.pallas_call(
            owner_kernel,
            in_specs=vmem_specs(3),
            out_specs=vmem_specs(2),
            out_shape=[VMEM((shard, rank), F32), VMEM((2, shard, rank), F32)],
            compiler_params=LIMIT,
            name="owner_adam",
        )(*in_vmem(parts, values, moments))
        residual, values, moments = lax.optimization_barrier((residual, values, moments))
        values, moments = shifted(values), shifted(moments)
        operands = (meta, *in_vmem(items, residual))
        scratch = [VMEM((user_rows // EDGE, EDGE, rank), F32)]
        if last:
            by_block = pl.BlockSpec((EDGE, rank), lambda at: (at, 0))
            users = pl.pallas_call(
                functools.partial(last_user_kernel, stratum, slots),
                grid=(user_rows // EDGE,),
                in_specs=[smem] + vmem_specs(2) + [by_block] * 3,
                out_specs=[by_block] * 3,
                out_shape=[jax.ShapeDtypeStruct((user_rows, rank), F32)] * 3,
                scratch_shapes=scratch,
                compiler_params=LIMIT,
                cost_estimate=USER_COST,
                name="last_user_adam",
            )(*operands, *users)
        else:
            *users, user_bf = pl.pallas_call(
                functools.partial(user_kernel, stratum, slots),
                in_specs=[smem] + vmem_specs(5),
                out_specs=vmem_specs(4),
                out_shape=[VMEM((user_rows, rank), kind) for kind in (F32, F32, F32, BF16)],
                scratch_shapes=scratch,
                compiler_params=LIMIT,
                cost_estimate=USER_COST,
                name="user_adam",
            )(*operands, *in_vmem(*users))
            values, moments, user_bf = lax.optimization_barrier((values, moments, user_bf))

    return (*users, values, moments[0], moments[1])


def solution(mesh):
    rows = P(("blk", "rep"), None)
    in_specs = (rows,) * 6 + (
        P("blk", "rep", None, None),
        P("blk", "rep", None, None),
        P("blk", "rep", None),
        P("blk", "rep", None, None, None, None),
    )
    return jax.shard_map(on_device, mesh=mesh, in_specs=in_specs, out_specs=(rows,) * 6, check_vma=False)
```

time: 901 us -> 252 us (0.28)
  waiting for transfers between devices: 695 us -> 11.6 us
  blocking collectives: 0 us -> 130 us
  other arithmetic: 48.6 us -> 4.15 us
  local copies, waits for them, and re-layouts: 49.5 us -> 9.66 us
  matrix products: 37.1 us -> 0 us
  Pallas kernels: 0 us -> 28.9 us
  starting transfers between devices: 47.1 us -> 65.9 us
  between operations: 15.1 us -> 1.01 us
    psum x8 -> x0, waiting for transfers between devices: 552 us -> none  [on_device(): item_grad = lax.psum(item_grad, 'rep')]
    all_to_all x0 -> x14, blocking collectives: none -> 130 us  [the longest x7 69.3 us: on_device(): parts = lax.all_to_all(grad.reshape(reps, shard, rank), 'rep', 0, 0)]
    ppermute x8 -> x16, waiting for transfers between devices: 107 us -> 2.14 us  [shifted(): return lax.ppermute(value, ('blk', 'rep'), moves)]
    dot_general x40 -> x0, matrix products: 37.1 us -> none  [the longest x8 11.6 us: stratum_grads(): jnp.einsum('sur,sir->sui', user_blocks, item_blocks, preferred_element_ty...]
    all_gather x1 -> x0, waiting for transfers between devices: 35.8 us -> none  [on_device(): item_state = lax.all_gather(item_state, 'rep', axis=1, tiled=True)]
    pallas_call x0 -> x24, Pallas kernels: none -> 28.9 us  [the longest x7 11.9 us: on_device(): pl.pallas_call(functools.partial(user_kernel, stratum, slots), in_specs=[...]
    another operation x17 -> x1, other arithmetic: 25.9 us -> 0.88 us  [on_device(): values, moments = (item_factors, jnp.stack([item_first, item_second]))]
    gather x16 -> x0, local copies, waits for them, and re-layouts: 19.8 us -> none  [the longest x8 13.6 us: stratum_grads(): jnp.take(user_bf.reshape(user_count, block_edge, rank_width), row_ids, ax...]
  transfers between devices with their start and end apart: 17 -> 18, of which waited for: 17 -> 5; matrix products, arithmetic and copies ran while one was open for 6% -> 2% of each run, Pallas kernels for 0% -> 6%
where the time goes in v1:
time: 252 us; the launch traced here: 251 us
  blocking collectives  130 us (52%)
  starting transfers between devices  65.9 us (26%)
  Pallas kernels  28.9 us (11%)
  waiting for transfers between devices  11.6 us (5%)
  local copies, waits for them, and re-layouts  9.66 us (4%)
  other arithmetic  4.15 us (2%)
    all_to_all x7, blocking collectives, on_device(): parts = lax.all_to_all(grad.reshape(reps, shard, rank), 'rep', 0, 0)  69.3 us
    all_to_all x7, blocking collectives, on_device(): items = lax.all_to_all(copies, 'rep', 0, 0).reshape(item_rows, rank)  60.8 us
    ppermute x16, starting transfers between devices, shifted(): return lax.ppermute(value, ('blk', 'rep'), moves)  54.9 us
    pallas_call x7, Pallas kernels, on_device(): pl.pallas_call(functools.partial(user_kernel, stratum, slots), in_specs=[...  11.9 us
    pallas_call x8, Pallas kernels, on_device(): pl.pallas_call(functools.partial(item_grad_kernel, stratum, slots), in_sp...  11.1 us
    unnamed x25, local copies, waits for them, and re-layouts  7.42 us
    all_to_all x1, starting transfers between devices, on_device(): items = lax.all_to_all(copies, 'rep', 0, 0).reshape(item_rows, rank)  6.88 us
    all_to_all x1, waiting for transfers between devices, on_device(): parts = lax.all_to_all(grad.reshape(reps, shard, rank), 'rep', 0, 0)  6.3 us
  transfers between devices with their start and end apart: 18, of which 5 were waited for; matrix products, arithmetic and copies ran while one was open for 2% of the time, Pallas kernels for 6%

profile of v1, /device:TPU:1, one launch (start us, length us, event | category | flops | bytes accessed | tf_op | source)
XLA Modules:
  0.0 251.3 jit_solution(16551588091809564723)
XLA Ops:
  2.4 6.9 %all-to-all-start = ((bf16[8,64,256]{2,1,0:T(8,128)(2,1)}), bf16[8,64,256]{2,1,0:T(8,128)(2,1)S(1)}, u32[]{:S(2)}, u32[]{:S(2)}) async-start(bf16[8,64,256]{2,1,0:T(8,128)(2,1)} %broadcast_in_dim.16), calls=%async_computation | async-start | bytes 524288 | tf_op jit(solution)/shard_map/all_to_all | solution.py:145
  19.3 4.2 %all-to-all-start.1 = ((f32[8,64,256]{2,1,0:T(8,128)}), f32[8,64,256]{2,1,0:T(8,128)}, u32[]{:S(2)}, u32[]{:S(2)}) async-start(f32[8,64,256]{2,1,0:T(8,128)} %bitcast.57), calls=%async_computation.1 | async-start | bytes 1048576 | tf_op jit(solution)/shard_map/all_to_all | solution.py:154
  24.4 6.3 %all-to-all-done.1.parts = f32[8,64,256]{2,1,0:T(8,128)} async-done(((f32[8,64,256]{2,1,0:T(8,128)}), f32[8,64,256]{2,1,0:T(8,128)}, u32[]{:S(2)}, u32[]{:S(2)}) %all-to-all-start.1) | async-done | bytes 524320 | tf_op jit(solution)/shard_map/all_to_all | solution.py:154
  43.2 9.7 %all_to_all.80 = bf16[8,64,256]{2,1,0:T(8,128)(2,1)S(1)} all-to-all(bf16[8,64,256]{2,1,0:T(8,128)(2,1)S(1)} %broadcast_in_dim.17), channel_id=1, replica_groups=mesh['blk'=16,'rep'=8] {'rep'}, dimensions={0} | all-to-all | bytes 524288 | tf_op jit(solution)/shard_map/all_to_all | solution.py:145
  54.3 9.9 %all_to_all.81.parts = f32[8,64,256]{2,1,0:T(8,128)S(1)} all-to-all(f32[8,64,256]{2,1,0:T(8,128)S(1)} %bitcast.58), channel_id=1, replica_groups=mesh['blk'=16,'rep'=8] {'rep'}, dimensions={0} | all-to-all | bytes 1048576 | tf_op jit(solution)/shard_map/all_to_all | solution.py:154
  64.2 4.3 %collective-permute-start.3 = (f32[2,64,256]{2,1,0:T(8,128)S(1)}, f32[2,64,256]{2,1,0:T(8,128)S(1)}, u32[]{:S(2)}, u32[]{:S(2)}) collective-permute-start(f32[2,64,256]{2,1,0:T(8,128)S(1)} %get-tuple-element.130), channel_id=1, source_target_pairs={{0,124},{1,125},{2,126},{3,127},{4,120},{5,121},{6,122},{7,123},{8... | collective-permute-start | bytes 393224 | tf_op jit(solution)/shard_map/ppermute | solution.py:126
  73.5 8.5 %all_to_all.82 = bf16[8,64,256]{2,1,0:T(8,128)(2,1)S(1)} all-to-all(bf16[8,64,256]{2,1,0:T(8,128)(2,1)S(1)} %broadcast_in_dim.18), channel_id=1, replica_groups=mesh['blk'=16,'rep'=8] {'rep'}, dimensions={0} | all-to-all | bytes 524288 | tf_op jit(solution)/shard_map/all_to_all | solution.py:145
  83.4 9.9 %all_to_all.83.parts = f32[8,64,256]{2,1,0:T(8,128)S(1)} all-to-all(f32[8,64,256]{2,1,0:T(8,128)S(1)} %bitcast.59), channel_id=1, replica_groups=mesh['blk'=16,'rep'=8] {'rep'}, dimensions={0} | all-to-all | bytes 1048576 | tf_op jit(solution)/shard_map/all_to_all | solution.py:154
  102.1 8.5 %all_to_all.84 = bf16[8,64,256]{2,1,0:T(8,128)(2,1)S(1)} all-to-all(bf16[8,64,256]{2,1,0:T(8,128)(2,1)S(1)} %broadcast_in_dim.19), channel_id=1, replica_groups=mesh['blk'=16,'rep'=8] {'rep'}, dimensions={0} | all-to-all | bytes 524288 | tf_op jit(solution)/shard_map/all_to_all | solution.py:145
  112.0 9.9 %all_to_all.85.parts = f32[8,64,256]{2,1,0:T(8,128)S(1)} all-to-all(f32[8,64,256]{2,1,0:T(8,128)S(1)} %bitcast.60), channel_id=1, replica_groups=mesh['blk'=16,'rep'=8] {'rep'}, dimensions={0} | all-to-all | bytes 1048576 | tf_op jit(solution)/shard_map/all_to_all | solution.py:154
  122.0 4.1 %collective-permute-start.7 = (f32[2,64,256]{2,1,0:T(8,128)S(1)}, f32[2,64,256]{2,1,0:T(8,128)S(1)}, u32[]{:S(2)}, u32[]{:S(2)}) collective-permute-start(f32[2,64,256]{2,1,0:T(8,128)S(1)} %get-tuple-element.158), channel_id=1, source_target_pairs={{0,124},{1,125},{2,126},{3,127},{4,120},{5,121},{6,122},{7,123},{8... | collective-permute-start | bytes 393224 | tf_op jit(solution)/shard_map/ppermute | solution.py:126
  131.1 8.5 %all_to_all.86 = bf16[8,64,256]{2,1,0:T(8,128)(2,1)S(1)} all-to-all(bf16[8,64,256]{2,1,0:T(8,128)(2,1)S(1)} %broadcast_in_dim.20), channel_id=1, replica_groups=mesh['blk'=16,'rep'=8] {'rep'}, dimensions={0} | all-to-all | bytes 524288 | tf_op jit(solution)/shard_map/all_to_all | solution.py:145
  141.0 9.9 %all_to_all.87.parts = f32[8,64,256]{2,1,0:T(8,128)S(1)} all-to-all(f32[8,64,256]{2,1,0:T(8,128)S(1)} %bitcast.61), channel_id=1, replica_groups=mesh['blk'=16,'rep'=8] {'rep'}, dimensions={0} | all-to-all | bytes 1048576 | tf_op jit(solution)/shard_map/all_to_all | solution.py:154
  154.5 3.9 %collective-permute-start.8 = (f32[64,256]{1,0:T(8,128)S(1)}, f32[64,256]{1,0:T(8,128)S(1)}, u32[]{:S(2)}, u32[]{:S(2)}) collective-permute-start(f32[64,256]{1,0:T(8,128)S(1)} %get-tuple-element.171), channel_id=1, source_target_pairs={{0,124},{1,125},{2,126},{3,127},{4,120},{5,121},{6,122},{7,123},{8... | collective-permute-start | bytes 196616 | tf_op jit(solution)/shard_map/ppermute | solution.py:126
  160.2 8.5 %all_to_all.88 = bf16[8,64,256]{2,1,0:T(8,128)(2,1)S(1)} all-to-all(bf16[8,64,256]{2,1,0:T(8,128)(2,1)S(1)} %broadcast_in_dim.21), channel_id=1, replica_groups=mesh['blk'=16,'rep'=8] {'rep'}, dimensions={0} | all-to-all | bytes 524288 | tf_op jit(solution)/shard_map/all_to_all | solution.py:145
  170.1 9.9 %all_to_all.89.parts = f32[8,64,256]{2,1,0:T(8,128)S(1)} all-to-all(f32[8,64,256]{2,1,0:T(8,128)S(1)} %bitcast.62), channel_id=1, replica_groups=mesh['blk'=16,'rep'=8] {'rep'}, dimensions={0} | all-to-all | bytes 1048576 | tf_op jit(solution)/shard_map/all_to_all | solution.py:154
  180.1 4.1 %collective-permute-start.11 = (f32[2,64,256]{2,1,0:T(8,128)S(1)}, f32[2,64,256]{2,1,0:T(8,128)S(1)}, u32[]{:S(2)}, u32[]{:S(2)}) collective-permute-start(f32[2,64,256]{2,1,0:T(8,128)S(1)} %get-tuple-element.186), channel_id=1, source_target_pairs={{0,124},{1,125},{2,126},{3,127},{4,120},{5,121},{6,122},{7,123},{8... | collective-permute-start | bytes 393224 | tf_op jit(solution)/shard_map/ppermute | solution.py:126
  189.1 8.5 %all_to_all.90 = bf16[8,64,256]{2,1,0:T(8,128)(2,1)S(1)} all-to-all(bf16[8,64,256]{2,1,0:T(8,128)(2,1)S(1)} %broadcast_in_dim.22), channel_id=1, replica_groups=mesh['blk'=16,'rep'=8] {'rep'}, dimensions={0} | all-to-all | bytes 524288 | tf_op jit(solution)/shard_map/all_to_all | solution.py:145
  199.0 9.9 %all_to_all.91.parts = f32[8,64,256]{2,1,0:T(8,128)S(1)} all-to-all(f32[8,64,256]{2,1,0:T(8,128)S(1)} %bitcast.63), channel_id=1, replica_groups=mesh['blk'=16,'rep'=8] {'rep'}, dimensions={0} | all-to-all | bytes 1048576 | tf_op jit(solution)/shard_map/all_to_all | solution.py:154
  212.9 4.3 %collective-permute-start.12 = (f32[64,256]{1,0:T(8,128)S(1)}, f32[64,256]{1,0:T(8,128)S(1)}, u32[]{:S(2)}, u32[]{:S(2)}) collective-permute-start(f32[64,256]{1,0:T(8,128)S(1)} %get-tuple-element.199), channel_id=1, source_target_pairs={{0,124},{1,125},{2,126},{3,127},{4,120},{5,121},{6,122},{7,123},{8... | collective-permute-start | bytes 196616 | tf_op jit(solution)/shard_map/ppermute | solution.py:126
  218.9 8.5 %all_to_all.92 = bf16[8,64,256]{2,1,0:T(8,128)(2,1)S(1)} all-to-all(bf16[8,64,256]{2,1,0:T(8,128)(2,1)S(1)} %broadcast_in_dim.23), channel_id=1, replica_groups=mesh['blk'=16,'rep'=8] {'rep'}, dimensions={0} | all-to-all | bytes 524288 | tf_op jit(solution)/shard_map/all_to_all | solution.py:145
  228.8 9.9 %all_to_all.93.parts = f32[8,64,256]{2,1,0:T(8,128)S(1)} all-to-all(f32[8,64,256]{2,1,0:T(8,128)S(1)} %bitcast.64), channel_id=1, replica_groups=mesh['blk'=16,'rep'=8] {'rep'}, dimensions={0} | all-to-all | bytes 1048576 | tf_op jit(solution)/shard_map/all_to_all | solution.py:154
  238.8 4.1 %collective-permute-start.15 = (f32[2,64,256]{2,1,0:T(8,128)S(1)}, f32[2,64,256]{2,1,0:T(8,128)S(1)}, u32[]{:S(2)}, u32[]{:S(2)}) collective-permute-start(f32[2,64,256]{2,1,0:T(8,128)S(1)} %get-tuple-element.221), channel_id=1, source_target_pairs={{0,124},{1,125},{2,126},{3,127},{4,120},{5,121},{6,122},{7,123},{8... | collective-permute-start | bytes 393224 | tf_op jit(solution)/shard_map/ppermute | solution.py:126
  245.8 4.2 %last_user_adam.1 = (f32[1024,256]{1,0:T(8,128)}, f32[1024,256]{1,0:T(8,128)}, f32[1024,256]{1,0:T(8,128)}) custom-call(s32[8,17]{1,0:T(8,128)S(1)} %pad_add_fusion.meta, bf16[512,256]{1,0:T(8,128)(2,1)S(1)} %bitcast.56, bf16[8,128,128]{2,1,0:T(8,128)(2,1)S(1)} %get-tuple-element.213.residual, f32[1024,256]{1,0:T(8,128)S(1)} %get-tuple-element.214.values, ...), custom_call_target="tpu_custom_call" | custom-call | flops 300000000 | bytes 8000000 | tf_op jit(solution)/shard_map/last_user_adam/pallas_call | solution.py:169
  (98 shorter events, 73.8 us)
Async XLA Ops:
  0.6 11.4 %copy-start.11 = (s32[2,8]{1,0:T(2,128)S(1)}, s32[2,8]{1,0:T(2,128)}, u32[]{:S(2)}) copy-start(s32[2,8]{1,0:T(2,128)} %constant.37.clone) | copy-start | bytes 196
  0.6 11.4 %copy-start.9 = (s32[1,1,8,8]{3,2,1,0:T(8,128)S(1)}, s32[1,1,8,8]{3,2,1,0:T(8,128)}, u32[]{:S(2)}) copy-start(s32[1,1,8,8]{3,2,1,0:T(8,128)} %param.18) | copy-start | bytes 772
  0.7 11.5 %copy-start.10 = (s32[1,1,8,8]{3,2,1,0:T(8,128)S(1)}, s32[1,1,8,8]{3,2,1,0:T(8,128)}, u32[]{:S(2)}) copy-start(s32[1,1,8,8]{3,2,1,0:T(8,128)} %param.17) | copy-start | bytes 772
  0.7 14.7 %copy-start = (bf16[1,1,8,8,128,128]{5,4,3,2,1,0:T(8,128)(2,1)S(1)}, bf16[1,1,8,8,128,128]{5,4,3,2,1,0:T(8,128)(2,1)}, u32[]{:S(2)}) copy-start(bf16[1,1,8,8,128,128]{5,4,3,2,1,0:T(8,128)(2,1)} %param.20) | copy-start | bytes 6291460
  2.4 13.0 %all-to-all-start = ((bf16[8,64,256]{2,1,0:T(8,128)(2,1)}), bf16[8,64,256]{2,1,0:T(8,128)(2,1)S(1)}, u32[]{:S(2)}, u32[]{:S(2)}) async-start(bf16[8,64,256]{2,1,0:T(8,128)(2,1)} %broadcast_in_dim.16), calls=%async_computation | async-start | bytes 524288 | tf_op jit(solution)/shard_map/all_to_all | solution.py:145
  16.4 21.6 %copy-start.1 = (f32[1024,256]{1,0:T(8,128)S(1)}, f32[1024,256]{1,0:T(8,128)}, u32[]{:S(2)}) copy-start(f32[1024,256]{1,0:T(8,128)} %values.3) | copy-start | bytes 3145732
  19.3 11.4 %all-to-all-start.1 = ((f32[8,64,256]{2,1,0:T(8,128)}), f32[8,64,256]{2,1,0:T(8,128)}, u32[]{:S(2)}, u32[]{:S(2)}) async-start(f32[8,64,256]{2,1,0:T(8,128)} %bitcast.57), calls=%async_computation.1 | async-start | bytes 1048576 | tf_op jit(solution)/shard_map/all_to_all | solution.py:154
  32.6 10.5 %collective-permute-start.1 = (f32[2,64,256]{2,1,0:T(8,128)S(1)}, f32[2,64,256]{2,1,0:T(8,128)S(1)}, u32[]{:S(2)}, u32[]{:S(2)}) collective-permute-start(f32[2,64,256]{2,1,0:T(8,128)S(1)} %get-tuple-element.119), channel_id=1, source_target_pairs={{0,124},{1,125},{2,126},{3,127},{4,120},{5,121},{6,122},{7,123},{8... | collective-permute-start | bytes 393224 | tf_op jit(solution)/shard_map/ppermute | solution.py:126
  36.2 7.0 %collective-permute-start = (f32[64,256]{1,0:T(8,128)S(1)}, f32[64,256]{1,0:T(8,128)S(1)}, u32[]{:S(2)}, u32[]{:S(2)}) collective-permute-start(f32[64,256]{1,0:T(8,128)S(1)} %get-tuple-element.118), channel_id=1, source_target_pairs={{0,124},{1,125},{2,126},{3,127},{4,120},{5,121},{6,122},{7,123},{8... | collective-permute-start | bytes 196616 | tf_op jit(solution)/shard_map/ppermute | solution.py:126
  38.0 1.2 copy-start.3
  64.2 9.2 %collective-permute-start.3 = (f32[2,64,256]{2,1,0:T(8,128)S(1)}, f32[2,64,256]{2,1,0:T(8,128)S(1)}, u32[]{:S(2)}, u32[]{:S(2)}) collective-permute-start(f32[2,64,256]{2,1,0:T(8,128)S(1)} %get-tuple-element.130), channel_id=1, source_target_pairs={{0,124},{1,125},{2,126},{3,127},{4,120},{5,121},{6,122},{7,123},{8... | collective-permute-start | bytes 393224 | tf_op jit(solution)/shard_map/ppermute | solution.py:126
  68.5 4.9 %collective-permute-start.2 = (f32[64,256]{1,0:T(8,128)S(1)}, f32[64,256]{1,0:T(8,128)S(1)}, u32[]{:S(2)}, u32[]{:S(2)}) collective-permute-start(f32[64,256]{1,0:T(8,128)S(1)} %get-tuple-element.129), channel_id=1, source_target_pairs={{0,124},{1,125},{2,126},{3,127},{4,120},{5,121},{6,122},{7,123},{8... | collective-permute-start | bytes 196616 | tf_op jit(solution)/shard_map/ppermute | solution.py:126
  93.4 8.7 %collective-permute-start.5 = (f32[2,64,256]{2,1,0:T(8,128)S(1)}, f32[2,64,256]{2,1,0:T(8,128)S(1)}, u32[]{:S(2)}, u32[]{:S(2)}) collective-permute-start(f32[2,64,256]{2,1,0:T(8,128)S(1)} %get-tuple-element.144), channel_id=1, source_target_pairs={{0,124},{1,125},{2,126},{3,127},{4,120},{5,121},{6,122},{7,123},{8... | collective-permute-start | bytes 393224 | tf_op jit(solution)/shard_map/ppermute | solution.py:126
  97.1 5.0 %collective-permute-start.4 = (f32[64,256]{1,0:T(8,128)S(1)}, f32[64,256]{1,0:T(8,128)S(1)}, u32[]{:S(2)}, u32[]{:S(2)}) collective-permute-start(f32[64,256]{1,0:T(8,128)S(1)} %get-tuple-element.143), channel_id=1, source_target_pairs={{0,124},{1,125},{2,126},{3,127},{4,120},{5,121},{6,122},{7,123},{8... | collective-permute-start | bytes 196616 | tf_op jit(solution)/shard_map/ppermute | solution.py:126
  122.0 9.0 %collective-permute-start.7 = (f32[2,64,256]{2,1,0:T(8,128)S(1)}, f32[2,64,256]{2,1,0:T(8,128)S(1)}, u32[]{:S(2)}, u32[]{:S(2)}) collective-permute-start(f32[2,64,256]{2,1,0:T(8,128)S(1)} %get-tuple-element.158), channel_id=1, source_target_pairs={{0,124},{1,125},{2,126},{3,127},{4,120},{5,121},{6,122},{7,123},{8... | collective-permute-start | bytes 393224 | tf_op jit(solution)/shard_map/ppermute | solution.py:126
  126.1 4.9 %collective-permute-start.6 = (f32[64,256]{1,0:T(8,128)S(1)}, f32[64,256]{1,0:T(8,128)S(1)}, u32[]{:S(2)}, u32[]{:S(2)}) collective-permute-start(f32[64,256]{1,0:T(8,128)S(1)} %get-tuple-element.157), channel_id=1, source_target_pairs={{0,124},{1,125},{2,126},{3,127},{4,120},{5,121},{6,122},{7,123},{8... | collective-permute-start | bytes 196616 | tf_op jit(solution)/shard_map/ppermute | solution.py:126
  151.0 9.2 %collective-permute-start.9 = (f32[2,64,256]{2,1,0:T(8,128)S(1)}, f32[2,64,256]{2,1,0:T(8,128)S(1)}, u32[]{:S(2)}, u32[]{:S(2)}) collective-permute-start(f32[2,64,256]{2,1,0:T(8,128)S(1)} %get-tuple-element.172), channel_id=1, source_target_pairs={{0,124},{1,125},{2,126},{3,127},{4,120},{5,121},{6,122},{7,123},{8... | collective-permute-start | bytes 393224 | tf_op jit(solution)/shard_map/ppermute | solution.py:126
  154.5 5.6 %collective-permute-start.8 = (f32[64,256]{1,0:T(8,128)S(1)}, f32[64,256]{1,0:T(8,128)S(1)}, u32[]{:S(2)}, u32[]{:S(2)}) collective-permute-start(f32[64,256]{1,0:T(8,128)S(1)} %get-tuple-element.171), channel_id=1, source_target_pairs={{0,124},{1,125},{2,126},{3,127},{4,120},{5,121},{6,122},{7,123},{8... | collective-permute-start | bytes 196616 | tf_op jit(solution)/shard_map/ppermute | solution.py:126
  180.1 9.0 %collective-permute-start.11 = (f32[2,64,256]{2,1,0:T(8,128)S(1)}, f32[2,64,256]{2,1,0:T(8,128)S(1)}, u32[]{:S(2)}, u32[]{:S(2)}) collective-permute-start(f32[2,64,256]{2,1,0:T(8,128)S(1)} %get-tuple-element.186), channel_id=1, source_target_pairs={{0,124},{1,125},{2,126},{3,127},{4,120},{5,121},{6,122},{7,123},{8... | collective-permute-start | bytes 393224 | tf_op jit(solution)/shard_map/ppermute | solution.py:126
  184.2 4.9 %collective-permute-start.10 = (f32[64,256]{1,0:T(8,128)S(1)}, f32[64,256]{1,0:T(8,128)S(1)}, u32[]{:S(2)}, u32[]{:S(2)}) collective-permute-start(f32[64,256]{1,0:T(8,128)S(1)} %get-tuple-element.185), channel_id=1, source_target_pairs={{0,124},{1,125},{2,126},{3,127},{4,120},{5,121},{6,122},{7,123},{8... | collective-permute-start | bytes 196616 | tf_op jit(solution)/shard_map/ppermute | solution.py:126
  209.0 9.9 %collective-permute-start.13 = (f32[2,64,256]{2,1,0:T(8,128)S(1)}, f32[2,64,256]{2,1,0:T(8,128)S(1)}, u32[]{:S(2)}, u32[]{:S(2)}) collective-permute-start(f32[2,64,256]{2,1,0:T(8,128)S(1)} %get-tuple-element.200), channel_id=1, source_target_pairs={{0,124},{1,125},{2,126},{3,127},{4,120},{5,121},{6,122},{7,123},{8... | collective-permute-start | bytes 393224 | tf_op jit(solution)/shard_map/ppermute | solution.py:126
  212.9 6.0 %collective-permute-start.12 = (f32[64,256]{1,0:T(8,128)S(1)}, f32[64,256]{1,0:T(8,128)S(1)}, u32[]{:S(2)}, u32[]{:S(2)}) collective-permute-start(f32[64,256]{1,0:T(8,128)S(1)} %get-tuple-element.199), channel_id=1, source_target_pairs={{0,124},{1,125},{2,126},{3,127},{4,120},{5,121},{6,122},{7,123},{8... | collective-permute-start | bytes 196616 | tf_op jit(solution)/shard_map/ppermute | solution.py:126
  238.8 11.2 %collective-permute-start.15 = (f32[2,64,256]{2,1,0:T(8,128)S(1)}, f32[2,64,256]{2,1,0:T(8,128)S(1)}, u32[]{:S(2)}, u32[]{:S(2)}) collective-permute-start(f32[2,64,256]{2,1,0:T(8,128)S(1)} %get-tuple-element.221), channel_id=1, source_target_pairs={{0,124},{1,125},{2,126},{3,127},{4,120},{5,121},{6,122},{7,123},{8... | collective-permute-start | bytes 393224 | tf_op jit(solution)/shard_map/ppermute | solution.py:126
  242.9 7.1 %collective-permute-start.14 = (f32[64,256]{1,0:T(8,128)S(1)}, f32[64,256]{1,0:T(8,128)S(1)}, u32[]{:S(2)}, u32[]{:S(2)}) collective-permute-start(f32[64,256]{1,0:T(8,128)S(1)} %get-tuple-element.220), channel_id=1, source_target_pairs={{0,124},{1,125},{2,126},{3,127},{4,120},{5,121},{6,122},{7,123},{8... | collective-permute-start | bytes 196616 | tf_op jit(solution)/shard_map/ppermute | solution.py:126
  (6 other events, 5.6 us)

commit v2 on v1

v2 whole, which is shorter than its diff:
```python
import functools

import jax
import jax.numpy as jnp
from jax import lax
from jax.experimental import pallas as pl
from jax.experimental.pallas import tpu as pltpu
from jax.sharding import PartitionSpec as P

learn_rate = 0.01
adam_eps = 1e-08
EDGE = 128
OWNERS = 4
VMEM = pltpu.VMEM
F32 = jnp.float32
BF16 = jnp.bfloat16


def adam(values, moment_one, moment_two, gradient):
    moment_one = 0.9 * moment_one + 0.1 * gradient
    moment_two = 0.99 * moment_two + 0.01 * gradient * gradient
    values = values - learn_rate * moment_one / (jnp.sqrt(moment_two) + adam_eps)
    return values, moment_one, moment_two


def block_at(index):
    return pl.ds(pl.multiple_of(index * EDGE, EDGE), EDGE)


def slot_grads(stratum, slots, meta, items, users, teacher, residual, grad):
    grad[...] = jnp.zeros_like(grad)
    live = meta[stratum, 2 * slots]
    for slot in range(slots):
        user_block = users[block_at(meta[stratum, slot]), :]
        col = block_at(meta[stratum, slots + slot])
        predicted = lax.dot_general(
            user_block, items[col, :], (((1,), (1,)), ((), ())), preferred_element_type=F32
        )
        left = jnp.where(slot < live, predicted - teacher[stratum, slot].astype(F32), 0.0).astype(BF16)
        residual[slot] = left
        grad[col, :] += lax.dot_general(
            left, user_block, (((0,), (0,)), ((), ())), preferred_element_type=F32
        )


def spread_parts(grad, parts):
    shard = parts.shape[1] // 2
    for owner in range(OWNERS):
        for side in range(2):
            at = (side * OWNERS + owner) * shard
            rows = grad[at : at + shard, :].astype(BF16)
            for copy in range(parts.shape[0] // OWNERS):
                parts[copy * OWNERS + owner, side * shard : (side + 1) * shard, :] = rows


def first_item_kernel(stratum, slots, meta, items, users, teacher, parts, residual, grad):
    slot_grads(stratum, slots, meta, items, users, teacher, residual, grad)
    spread_parts(grad, parts)


def item_kernel(stratum, slots, meta, *refs):
    got = refs[:OWNERS]
    users, teacher, parts, residual, items, grad = refs[OWNERS:]
    shard = got[0].shape[0] // 2
    place = meta[stratum, 2 * slots + 1]
    for hop in range(OWNERS):
        start = pl.multiple_of((place ^ hop) * shard, shard)
        items[pl.ds(start, shard), :] = got[hop][:shard, :]
        items[pl.ds(start + OWNERS * shard, shard), :] = got[hop][shard:, :]
    slot_grads(stratum, slots, meta, items, users, teacher, residual, grad)
    spread_parts(grad, parts)


def user_grads(stratum, slots, meta, items, residual, grad):
    grad[...] = jnp.zeros_like(grad)
    for slot in range(slots):
        col = block_at(meta[stratum, slots + slot])
        grad[meta[stratum, slot]] += jnp.dot(residual[slot], items[col, :], preferred_element_type=F32)


def user_kernel(stratum, slots, meta, items, residual, values, one, two, values_out, one_out, two_out, rounded, grad):
    user_grads(stratum, slots, meta, items, residual, grad)

    def one_block(at, carry):
        rows = block_at(at)
        new, first, second = adam(values[rows, :], one[rows, :], two[rows, :], grad[at])
        values_out[rows, :] = new
        one_out[rows, :] = first
        two_out[rows, :] = second
        rounded[rows, :] = new.astype(BF16)
        return carry

    lax.fori_loop(0, grad.shape[0], one_block, 0)


def last_user_kernel(stratum, slots, meta, items, residual, values, one, two, values_out, one_out, two_out, grad):
    at = pl.program_id(0)

    @pl.when(at == 0)
    def _():
        user_grads(stratum, slots, meta, items, residual, grad)

    values_out[...], one_out[...], two_out[...] = adam(
        values[...], one[...], two[...], grad[pl.ds(at * 2, 2)].reshape(values.shape)
    )


def owner_kernel(parts, state, state_out, rounded):
    total = parts[0].astype(F32)
    for part in range(1, parts.shape[0]):
        total += parts[part].astype(F32)
    new, state_out[1], state_out[2] = adam(state[0], state[1], state[2], total)
    state_out[0] = new
    rounded[...] = new.astype(BF16)


def first_owner_kernel(slots, meta, parts, own, other, state_out, rounded):
    total = parts[0].astype(F32)
    for part in range(1, parts.shape[0]):
        total += parts[part].astype(F32)

    def update(low, high):
        columns = [jnp.concatenate([low[term], high[term]], axis=0) for term in range(3)]
        new, state_out[1], state_out[2] = adam(*columns, total)
        state_out[0] = new
        rounded[...] = new.astype(BF16)

    side = meta[0, 2 * slots + 3]

    @pl.when(side == 0)
    def _():
        update(own, other)

    @pl.when(side == 1)
    def _():
        update(other, own)


def last_owner_kernel(stratum, slots, meta, parts, state, state_out):
    shard = state.shape[1] // 2
    rows = pl.ds(pl.multiple_of(meta[stratum, 2 * slots + 2] * shard, shard), shard)
    total = parts[0, rows, :].astype(F32)
    for part in range(1, parts.shape[0]):
        total += parts[part, rows, :].astype(F32)
    state_out[0], state_out[1], state_out[2] = adam(state[0, rows, :], state[1, rows, :], state[2, rows, :], total)


def start_kernel(values, one, two, own, arrived):
    moves = [
        pltpu.make_async_copy(source, own.at[term], arrived.at[term]) for term, source in enumerate((values, one, two))
    ]
    for move in moves:
        move.start()
    for move in moves:
        move.wait()


def finish_kernel(state, values, one, two, sent):
    moves = [
        pltpu.make_async_copy(state.at[term], target, sent.at[term]) for term, target in enumerate((values, one, two))
    ]
    for move in moves:
        move.start()
    for move in moves:
        move.wait()


def vmem_specs(count):
    return [pl.BlockSpec(memory_space=VMEM)] * count


def in_vmem(*arrays):
    return [pltpu.with_memory_space_constraint(a, VMEM) for a in arrays]


LIMIT = pltpu.CompilerParams(vmem_limit_bytes=6 * 1024 * 1024)
USER_COST = pl.CostEstimate(flops=300_000_000, bytes_accessed=8_000_000, transcendentals=600_000)


def on_device(
    user_factors,
    user_first,
    user_second,
    item_factors,
    item_first,
    item_second,
    block_rows,
    block_cols,
    live_slots,
    teacher,
):
    strata, slots = block_rows.shape[2], block_rows.shape[3]
    user_rows, rank = user_factors.shape
    shard = item_factors.shape[0]
    groups, reps = lax.axis_size("blk"), lax.axis_size("rep")
    item_rows = shard * reps

    def moves(hop):
        return [
            (group * reps + rep, ((group - 1) % groups) * reps + (rep ^ hop ^ (0 if group % 2 else OWNERS)))
            for group in range(groups)
            for rep in range(reps)
        ]

    def shifted(value, hop=0):
        return lax.ppermute(value, ("blk", "rep"), moves(hop))

    rep = lax.axis_index("rep")
    side = rep // OWNERS
    keep = (side + 1 - lax.axis_index("blk") % 2) % 2
    places = jnp.broadcast_to(jnp.stack([rep % OWNERS, keep, side]), (strata, 3))
    meta = jnp.concatenate([block_rows[0, 0], block_cols[0, 0], live_slots[0, 0][:, None], places], axis=1)
    smem = pl.BlockSpec(memory_space=pltpu.SMEM)

    scores = teacher[0, 0]
    users = (user_factors, user_first, user_second)
    user_bf = user_factors.astype(BF16)

    anywhere = pl.BlockSpec(memory_space=pl.ANY)
    own = pl.pallas_call(
        start_kernel,
        in_specs=[anywhere] * 3,
        out_specs=vmem_specs(1)[0],
        out_shape=VMEM((3, shard, rank), F32),
        scratch_shapes=[pltpu.SemaphoreType.DMA((3,))],
        compiler_params=LIMIT,
        name="start",
    )(*[pltpu.with_memory_space_constraint(a, pltpu.HBM) for a in (item_factors, item_first, item_second)])
    other = lax.ppermute(own, "rep", [(at, at ^ OWNERS) for at in range(reps)])
    copies = jnp.broadcast_to(own[0].astype(BF16)[None], (reps, shard, rank))
    items = lax.all_to_all(copies, "rep", 0, 0).reshape(item_rows, rank)
    items, own, other, user_bf, meta = lax.optimization_barrier((items, own, other, user_bf, meta))

    parts_shape = VMEM((reps, 2 * shard, rank), BF16)
    residual_shape = VMEM((slots, EDGE, EDGE), BF16)
    item_scratch = [VMEM((item_rows, rank), F32)]
    for stratum in range(strata):
        last = stratum == strata - 1
        if stratum == 0:
            parts, residual = pl.pallas_call(
                functools.partial(first_item_kernel, stratum, slots),
                in_specs=[smem] + vmem_specs(3),
                out_specs=vmem_specs(2),
                out_shape=[parts_shape, residual_shape],
                scratch_shapes=item_scratch,
                compiler_params=LIMIT,
                name="item_grad",
            )(meta, *in_vmem(items, user_bf, scores))
        else:
            parts, residual, items = pl.pallas_call(
                functools.partial(item_kernel, stratum, slots),
                in_specs=[smem] + vmem_specs(OWNERS + 2),
                out_specs=vmem_specs(3),
                out_shape=[parts_shape, residual_shape, VMEM((item_rows, rank), BF16)],
                scratch_shapes=item_scratch,
                compiler_params=LIMIT,
                name="item_grad",
            )(meta, *in_vmem(*got, user_bf, scores))
        if stratum > 0:
            parts, state = lax.optimization_barrier((parts, state))
        parts = lax.all_to_all(parts, "rep", 0, 0)
        scratch = [VMEM((user_rows // EDGE, EDGE, rank), F32)]
        if last:
            state = pl.pallas_call(
                functools.partial(last_owner_kernel, stratum, slots),
                in_specs=[smem] + vmem_specs(2),
                out_specs=vmem_specs(1)[0],
                out_shape=VMEM((3, shard, rank), F32),
                compiler_params=LIMIT,
                name="owner_adam",
            )(meta, *in_vmem(parts, state))
            residual, state = lax.optimization_barrier((residual, state))
            state = shifted(state)
            by_block = pl.BlockSpec((2 * EDGE, rank), lambda at: (at, 0))
            users = pl.pallas_call(
                functools.partial(last_user_kernel, stratum, slots),
                grid=(user_rows // (2 * EDGE),),
                in_specs=[smem] + vmem_specs(2) + [by_block] * 3,
                out_specs=[by_block] * 3,
                out_shape=[jax.ShapeDtypeStruct((user_rows, rank), F32)] * 3,
                scratch_shapes=scratch,
                compiler_params=LIMIT,
                cost_estimate=USER_COST,
                name="last_user_adam",
            )(meta, *in_vmem(items, residual), *users)
        else:
            first = stratum == 0
            state, rounded = pl.pallas_call(
                functools.partial(first_owner_kernel, slots) if first else owner_kernel,
                in_specs=[smem] * first + vmem_specs(3 if first else 2),
                out_specs=vmem_specs(2),
                out_shape=[VMEM((3, 2 * shard, rank), F32), VMEM((2 * shard, rank), BF16)],
                compiler_params=LIMIT,
                name="owner_adam",
            )(*[meta] * first, *in_vmem(parts, *((own, other) if first else (state,))))
            residual, rounded, state = lax.optimization_barrier((residual, rounded, state))
            state = shifted(state)
            got = [shifted(rounded, hop) for hop in reversed(range(OWNERS))][::-1]
            *users, user_bf = pl.pallas_call(
                functools.partial(user_kernel, stratum, slots),
                in_specs=[smem] + vmem_specs(5),
                out_specs=vmem_specs(4),
                out_shape=[VMEM((user_rows, rank), kind) for kind in (F32, F32, F32, BF16)],
                scratch_shapes=scratch,
                compiler_params=LIMIT,
                cost_estimate=USER_COST,
                name="user_adam",
            )(meta, *in_vmem(items, residual, *users))

    items = pl.pallas_call(
        finish_kernel,
        in_specs=vmem_specs(1),
        out_specs=[anywhere] * 3,
        out_shape=[pltpu.HBM((shard, rank), F32)] * 3,
        scratch_shapes=[pltpu.SemaphoreType.DMA((3,))],
        compiler_params=LIMIT,
        name="finish",
    )(*in_vmem(state))
    return (*users, *items)


def solution(mesh):
    rows = P(("blk", "rep"), None)
    in_specs = (rows,) * 6 + (
        P("blk", "rep", None, None),
        P("blk", "rep", None, None),
        P("blk", "rep", None),
        P("blk", "rep", None, None, None, None),
    )
    return jax.shard_map(on_device, mesh=mesh, in_specs=in_specs, out_specs=(rows,) * 6, check_vma=False)
```

time: 252 us -> 218 us (0.87)
  blocking collectives: 130 us -> 92.9 us
  waiting for transfers between devices: 11.6 us -> 28 us
  local copies, waits for them, and re-layouts: 9.66 us -> 1.56 us
  starting transfers between devices: 65.9 us -> 61.9 us
  other arithmetic: 4.15 us -> 1.43 us
    all_to_all x14 -> x8, blocking collectives: 130 us -> 92.9 us  [on_device(): parts = lax.all_to_all(parts, 'rep', 0, 0)]
    ppermute x16 -> x37, waiting for transfers between devices: 2.14 us -> 24.1 us  [the longest x36 24.1 us: shifted(): return lax.ppermute(value, ('blk', 'rep'), moves(hop))]
    unnamed x25 -> x12, local copies, waits for them, and re-layouts: 7.42 us -> 0.02 us
    all_to_all x1 -> x0, waiting for transfers between devices: 6.3 us -> none  [on_device(): parts = lax.all_to_all(grad.reshape(reps, shard, rank), 'rep', 0, 0)]
    all_to_all x1 -> x0, starting transfers between devices: 4.16 us -> none  [on_device(): parts = lax.all_to_all(grad.reshape(reps, shard, rank), 'rep', 0, 0)]
    pallas_call x16 -> x18, Pallas kernels: 12.8 us -> 15.7 us  [the longest x7 10.1 us: on_device(): pl.pallas_call(functools.partial(item_kernel, stratum, slots), in_specs=[...]
    ppermute x16 -> x37, starting transfers between devices: 54.9 us -> 56.8 us  [the longest x36 54.6 us: shifted(): return lax.ppermute(value, ('blk', 'rep'), moves(hop))]
  transfers between devices with their start and end apart: 18 -> 38, of which waited for: 5 -> 21; matrix products, arithmetic and copies ran while one was open for 2% -> 1% of each run, Pallas kernels for 6% -> 12%
where the time goes in v2:
time: 218 us
  blocking collectives  92.9 us (43%)
  starting transfers between devices  61.9 us (28%)
  Pallas kernels  30.7 us (14%)
  waiting for transfers between devices  28 us (13%)
    all_to_all x8, blocking collectives, on_device(): parts = lax.all_to_all(parts, 'rep', 0, 0)  92.9 us
    ppermute x36, starting transfers between devices, shifted(): return lax.ppermute(value, ('blk', 'rep'), moves(hop))  54.6 us
    ppermute x36, waiting for transfers between devices, shifted(): return lax.ppermute(value, ('blk', 'rep'), moves(hop))  24.1 us
    pallas_call x7, Pallas kernels, on_device(): pl.pallas_call(functools.partial(user_kernel, stratum, slots), in_specs=[...  11.9 us
    pallas_call x7, Pallas kernels, on_device(): pl.pallas_call(functools.partial(item_kernel, stratum, slots), in_specs=[...  10.1 us
    all_to_all x1, starting transfers between devices, on_device(): items = lax.all_to_all(copies, 'rep', 0, 0).reshape(item_rows, rank)  5.03 us
  transfers between devices with their start and end apart: 38, of which 21 were waited for; matrix products, arithmetic and copies ran while one was open for 1% of the time, Pallas kernels for 12%

profile of v2, /device:TPU:1, one launch (start us, length us, event | category | flops | bytes accessed | tf_op | source)
XLA Modules:
  0.0 217.6 jit_solution(13322982437625756652)
XLA Ops:
  4.7 5.0 %all-to-all-start = ((bf16[8,64,256]{2,1,0:T(8,128)(2,1)}), bf16[8,64,256]{2,1,0:T(8,128)(2,1)S(1)}, u32[]{:S(2)}, u32[]{:S(2)}) async-start(bf16[8,64,256]{2,1,0:T(8,128)(2,1)} %broadcast_in_dim.12), calls=%async_computation | async-start | bytes 524288 | tf_op jit(solution)/shard_map/all_to_all | solution.py:231
  12.0 3.9 %all-to-all-done = bf16[8,64,256]{2,1,0:T(8,128)(2,1)S(1)} async-done(((bf16[8,64,256]{2,1,0:T(8,128)(2,1)}), bf16[8,64,256]{2,1,0:T(8,128)(2,1)S(1)}, u32[]{:S(2)}, u32[]{:S(2)}) %all-to-all-start) | async-done | bytes 262176 | tf_op jit(solution)/shard_map/all_to_all | solution.py:231
  17.3 9.9 %all_to_all.45.parts = bf16[8,128,256]{2,1,0:T(8,128)(2,1)S(1)} all-to-all(bf16[8,128,256]{2,1,0:T(8,128)(2,1)S(1)} %get-tuple-element.123), channel_id=1, replica_groups=mesh['blk'=16,'rep'=8] {'rep'}, dimensions={0} | all-to-all | bytes 1048576 | tf_op jit(solution)/shard_map/all_to_all | solution.py:261
  28.0 3.7 %collective-permute-start.5 = (f32[3,128,256]{2,1,0:T(8,128)S(1)}, f32[3,128,256]{2,1,0:T(8,128)S(1)}, u32[]{:S(2)}, u32[]{:S(2)}) collective-permute-start(f32[3,128,256]{2,1,0:T(8,128)S(1)} %get-tuple-element.133), channel_id=1, source_target_pairs={{0,124},{1,125},{2,126},{3,127},{4,120},{5,121},{6,122},{7,123},{8... | collective-permute-start | bytes 1179656 | tf_op jit(solution)/shard_map/ppermute | solution.py:206
  33.7 4.5 %collective-permute-start.3 = (bf16[128,256]{1,0:T(8,128)(2,1)S(1)}, bf16[128,256]{1,0:T(8,128)(2,1)S(1)}, u32[]{:S(2)}, u32[]{:S(2)}) collective-permute-start(bf16[128,256]{1,0:T(8,128)(2,1)S(1)} %get-tuple-element.128), channel_id=1, source_target_pairs={{0,126},{1,127},{2,124},{3,125},{4,122},{5,123},{6,120},{7,121},{8... | collective-permute-start | bytes 196616 | tf_op jit(solution)/shard_map/ppermute | solution.py:206
  41.7 2.4 %collective-permute-done.2.refs_1_ = bf16[128,256]{1,0:T(8,128)(2,1)S(1)} collective-permute-done((bf16[128,256]{1,0:T(8,128)(2,1)S(1)}, bf16[128,256]{1,0:T(8,128)(2,1)S(1)}, u32[]{:S(2)}, u32[]{:S(2)}) %collective-permute-start.2) | collective-permute-done | bytes 65568 | tf_op jit(solution)/shard_map/ppermute | solution.py:206
  45.9 11.9 %all_to_all.46.parts = bf16[8,128,256]{2,1,0:T(8,128)(2,1)S(1)} all-to-all(bf16[8,128,256]{2,1,0:T(8,128)(2,1)S(1)} %get-tuple-element.134), channel_id=1, replica_groups=mesh['blk'=16,'rep'=8] {'rep'}, dimensions={0} | all-to-all | bytes 1048576 | tf_op jit(solution)/shard_map/all_to_all | solution.py:261
  58.0 3.2 %collective-permute-start.9 = (bf16[128,256]{1,0:T(8,128)(2,1)S(1)}, bf16[128,256]{1,0:T(8,128)(2,1)S(1)}, u32[]{:S(2)}, u32[]{:S(2)}) collective-permute-start(bf16[128,256]{1,0:T(8,128)(2,1)S(1)} %get-tuple-element.138), channel_id=1, source_target_pairs={{0,127},{1,126},{2,125},{3,124},{4,123},{5,122},{6,121},{7,120},{8... | collective-permute-start | bytes 196616 | tf_op jit(solution)/shard_map/ppermute | solution.py:206
  70.7 12.1 %all_to_all.47.parts = bf16[8,128,256]{2,1,0:T(8,128)(2,1)S(1)} all-to-all(bf16[8,128,256]{2,1,0:T(8,128)(2,1)S(1)} %get-tuple-element.148), channel_id=1, replica_groups=mesh['blk'=16,'rep'=8] {'rep'}, dimensions={0} | all-to-all | bytes 1048576 | tf_op jit(solution)/shard_map/all_to_all | solution.py:261
  83.5 2.7 %collective-permute-start.14 = (bf16[128,256]{1,0:T(8,128)(2,1)S(1)}, bf16[128,256]{1,0:T(8,128)(2,1)S(1)}, u32[]{:S(2)}, u32[]{:S(2)}) collective-permute-start(bf16[128,256]{1,0:T(8,128)(2,1)S(1)} %get-tuple-element.152), channel_id=1, source_target_pairs={{0,127},{1,126},{2,125},{3,124},{4,123},{5,122},{6,121},{7,120},{8... | collective-permute-start | bytes 196616 | tf_op jit(solution)/shard_map/ppermute | solution.py:206
  95.8 12.0 %all_to_all.48.parts = bf16[8,128,256]{2,1,0:T(8,128)(2,1)S(1)} all-to-all(bf16[8,128,256]{2,1,0:T(8,128)(2,1)S(1)} %get-tuple-element.162), channel_id=1, replica_groups=mesh['blk'=16,'rep'=8] {'rep'}, dimensions={0} | all-to-all | bytes 1048576 | tf_op jit(solution)/shard_map/all_to_all | solution.py:261
  108.2 3.2 %collective-permute-start.19 = (bf16[128,256]{1,0:T(8,128)(2,1)S(1)}, bf16[128,256]{1,0:T(8,128)(2,1)S(1)}, u32[]{:S(2)}, u32[]{:S(2)}) collective-permute-start(bf16[128,256]{1,0:T(8,128)(2,1)S(1)} %get-tuple-element.166), channel_id=1, source_target_pairs={{0,127},{1,126},{2,125},{3,124},{4,123},{5,122},{6,121},{7,120},{8... | collective-permute-start | bytes 196616 | tf_op jit(solution)/shard_map/ppermute | solution.py:206
  120.8 11.1 %all_to_all.49.parts = bf16[8,128,256]{2,1,0:T(8,128)(2,1)S(1)} all-to-all(bf16[8,128,256]{2,1,0:T(8,128)(2,1)S(1)} %get-tuple-element.176), channel_id=1, replica_groups=mesh['blk'=16,'rep'=8] {'rep'}, dimensions={0} | all-to-all | bytes 1048576 | tf_op jit(solution)/shard_map/all_to_all | solution.py:261
  132.1 2.4 %collective-permute-start.25 = (f32[3,128,256]{2,1,0:T(8,128)S(1)}, f32[3,128,256]{2,1,0:T(8,128)S(1)}, u32[]{:S(2)}, u32[]{:S(2)}) collective-permute-start(f32[3,128,256]{2,1,0:T(8,128)S(1)} %get-tuple-element.189), channel_id=1, source_target_pairs={{0,124},{1,125},{2,126},{3,127},{4,120},{5,121},{6,122},{7,123},{8... | collective-permute-start | bytes 1179656 | tf_op jit(solution)/shard_map/ppermute | solution.py:206
  134.5 3.4 %collective-permute-start.24 = (bf16[128,256]{1,0:T(8,128)(2,1)S(1)}, bf16[128,256]{1,0:T(8,128)(2,1)S(1)}, u32[]{:S(2)}, u32[]{:S(2)}) collective-permute-start(bf16[128,256]{1,0:T(8,128)(2,1)S(1)} %get-tuple-element.180), channel_id=1, source_target_pairs={{0,127},{1,126},{2,125},{3,124},{4,123},{5,122},{6,121},{7,120},{8... | collective-permute-start | bytes 196616 | tf_op jit(solution)/shard_map/ppermute | solution.py:206
  138.9 2.6 %collective-permute-start.22 = (bf16[128,256]{1,0:T(8,128)(2,1)S(1)}, bf16[128,256]{1,0:T(8,128)(2,1)S(1)}, u32[]{:S(2)}, u32[]{:S(2)}) collective-permute-start(bf16[128,256]{1,0:T(8,128)(2,1)S(1)} %get-tuple-element.180), channel_id=1, source_target_pairs={{0,125},{1,124},{2,127},{3,126},{4,121},{5,120},{6,123},{7,122},{8... | collective-permute-start | bytes 196616 | tf_op jit(solution)/shard_map/ppermute | solution.py:206
  147.9 12.1 %all_to_all.50.parts = bf16[8,128,256]{2,1,0:T(8,128)(2,1)S(1)} all-to-all(bf16[8,128,256]{2,1,0:T(8,128)(2,1)S(1)} %get-tuple-element.190), channel_id=1, replica_groups=mesh['blk'=16,'rep'=8] {'rep'}, dimensions={0} | all-to-all | bytes 1048576 | tf_op jit(solution)/shard_map/all_to_all | solution.py:261
  160.4 2.5 %collective-permute-start.29 = (bf16[128,256]{1,0:T(8,128)(2,1)S(1)}, bf16[128,256]{1,0:T(8,128)(2,1)S(1)}, u32[]{:S(2)}, u32[]{:S(2)}) collective-permute-start(bf16[128,256]{1,0:T(8,128)(2,1)S(1)} %get-tuple-element.194), channel_id=1, source_target_pairs={{0,127},{1,126},{2,125},{3,124},{4,123},{5,122},{6,121},{7,120},{8... | collective-permute-start | bytes 196616 | tf_op jit(solution)/shard_map/ppermute | solution.py:206
  172.9 11.8 %all_to_all.51.parts = bf16[8,128,256]{2,1,0:T(8,128)(2,1)S(1)} all-to-all(bf16[8,128,256]{2,1,0:T(8,128)(2,1)S(1)} %get-tuple-element.204), channel_id=1, replica_groups=mesh['blk'=16,'rep'=8] {'rep'}, dimensions={0} | all-to-all | bytes 1048576 | tf_op jit(solution)/shard_map/all_to_all | solution.py:261
  184.9 3.0 %collective-permute-start.34 = (bf16[128,256]{1,0:T(8,128)(2,1)S(1)}, bf16[128,256]{1,0:T(8,128)(2,1)S(1)}, u32[]{:S(2)}, u32[]{:S(2)}) collective-permute-start(bf16[128,256]{1,0:T(8,128)(2,1)S(1)} %get-tuple-element.208), channel_id=1, source_target_pairs={{0,127},{1,126},{2,125},{3,124},{4,123},{5,122},{6,121},{7,120},{8... | collective-permute-start | bytes 196616 | tf_op jit(solution)/shard_map/ppermute | solution.py:206
  188.9 2.4 %collective-permute-start.32 = (bf16[128,256]{1,0:T(8,128)(2,1)S(1)}, bf16[128,256]{1,0:T(8,128)(2,1)S(1)}, u32[]{:S(2)}, u32[]{:S(2)}) collective-permute-start(bf16[128,256]{1,0:T(8,128)(2,1)S(1)} %get-tuple-element.208), channel_id=1, source_target_pairs={{0,125},{1,124},{2,127},{3,126},{4,121},{5,120},{6,123},{7,122},{8... | collective-permute-start | bytes 196616 | tf_op jit(solution)/shard_map/ppermute | solution.py:206
  197.7 12.0 %all_to_all.52.parts = bf16[8,128,256]{2,1,0:T(8,128)(2,1)S(1)} all-to-all(bf16[8,128,256]{2,1,0:T(8,128)(2,1)S(1)} %get-tuple-element.219), channel_id=1, replica_groups=mesh['blk'=16,'rep'=8] {'rep'}, dimensions={0} | all-to-all | bytes 1048576 | tf_op jit(solution)/shard_map/all_to_all | solution.py:261
  210.4 3.1 %last_user_adam.1 = (f32[1024,256]{1,0:T(8,128)}, f32[1024,256]{1,0:T(8,128)}, f32[1024,256]{1,0:T(8,128)}) custom-call(s32[8,20]{1,0:T(8,128)S(1)} %add_add_fusion.meta, bf16[512,256]{1,0:T(8,128)(2,1)S(1)} %get-tuple-element.215.items, bf16[8,128,128]{2,1,0:T(8,128)(2,1)S(1)} %get-tuple-element.221.residual, f32[1024,256]{1,0:T(8,128)S(1)} %get-tuple-element.222.values, ...), custom_call_target="tpu_custom_call" | custom-call | flops 300000000 | bytes 8000000 | tf_op jit(solution)/shard_map/last_user_adam/pallas_call | solution.py:275
  213.5 3.2 %collective-permute-done.36.state = f32[3,64,256]{2,1,0:T(8,128)S(1)} collective-permute-done((f32[3,64,256]{2,1,0:T(8,128)S(1)}, f32[3,64,256]{2,1,0:T(8,128)S(1)}, u32[]{:S(2)}, u32[]{:S(2)}) %collective-permute-start.36) | collective-permute-done | bytes 196640 | tf_op jit(solution)/shard_map/ppermute | solution.py:206
  (105 shorter events, 72.4 us)
Async XLA Ops:
  1.8 10.2 %collective-permute-start = (f32[3,64,256]{2,1,0:T(8,128)S(1)}, f32[3,64,256]{2,1,0:T(8,128)S(1)}, u32[]{:S(2)}, u32[]{:S(2)}) collective-permute-start(f32[3,64,256]{2,1,0:T(8,128)S(1)} %start.1.own), channel_id=1, source_target_pairs={{0,4},{1,5},{2,6},{3,7},{4,0},{5,1},{6,2},{7,3},{8,12},{9,13},{10,... | collective-permute-start | bytes 589832 | tf_op jit(solution)/shard_map/ppermute | solution.py:229
  4.7 11.2 %all-to-all-start = ((bf16[8,64,256]{2,1,0:T(8,128)(2,1)}), bf16[8,64,256]{2,1,0:T(8,128)(2,1)S(1)}, u32[]{:S(2)}, u32[]{:S(2)}) async-start(bf16[8,64,256]{2,1,0:T(8,128)(2,1)} %broadcast_in_dim.12), calls=%async_computation | async-start | bytes 524288 | tf_op jit(solution)/shard_map/all_to_all | solution.py:231
  28.0 17.9 %collective-permute-start.5 = (f32[3,128,256]{2,1,0:T(8,128)S(1)}, f32[3,128,256]{2,1,0:T(8,128)S(1)}, u32[]{:S(2)}, u32[]{:S(2)}) collective-permute-start(f32[3,128,256]{2,1,0:T(8,128)S(1)} %get-tuple-element.133), channel_id=1, source_target_pairs={{0,124},{1,125},{2,126},{3,127},{4,120},{5,121},{6,122},{7,123},{8... | collective-permute-start | bytes 1179656 | tf_op jit(solution)/shard_map/ppermute | solution.py:206
  31.7 9.9 %collective-permute-start.4 = (bf16[128,256]{1,0:T(8,128)(2,1)S(1)}, bf16[128,256]{1,0:T(8,128)(2,1)S(1)}, u32[]{:S(2)}, u32[]{:S(2)}) collective-permute-start(bf16[128,256]{1,0:T(8,128)(2,1)S(1)} %get-tuple-element.128), channel_id=1, source_target_pairs={{0,127},{1,126},{2,125},{3,124},{4,123},{5,122},{6,121},{7,120},{8... | collective-permute-start | bytes 196616 | tf_op jit(solution)/shard_map/ppermute | solution.py:206
  33.7 8.0 %collective-permute-start.3 = (bf16[128,256]{1,0:T(8,128)(2,1)S(1)}, bf16[128,256]{1,0:T(8,128)(2,1)S(1)}, u32[]{:S(2)}, u32[]{:S(2)}) collective-permute-start(bf16[128,256]{1,0:T(8,128)(2,1)S(1)} %get-tuple-element.128), channel_id=1, source_target_pairs={{0,126},{1,127},{2,124},{3,125},{4,122},{5,123},{6,120},{7,121},{8... | collective-permute-start | bytes 196616 | tf_op jit(solution)/shard_map/ppermute | solution.py:206
  57.9 12.8 %collective-permute-start.10 = (f32[3,128,256]{2,1,0:T(8,128)S(1)}, f32[3,128,256]{2,1,0:T(8,128)S(1)}, u32[]{:S(2)}, u32[]{:S(2)}) collective-permute-start(f32[3,128,256]{2,1,0:T(8,128)S(1)} %get-tuple-element.147), channel_id=1, source_target_pairs={{0,124},{1,125},{2,126},{3,127},{4,120},{5,121},{6,122},{7,123},{8... | collective-permute-start | bytes 1179656 | tf_op jit(solution)/shard_map/ppermute | solution.py:206
  58.0 9.5 %collective-permute-start.9 = (bf16[128,256]{1,0:T(8,128)(2,1)S(1)}, bf16[128,256]{1,0:T(8,128)(2,1)S(1)}, u32[]{:S(2)}, u32[]{:S(2)}) collective-permute-start(bf16[128,256]{1,0:T(8,128)(2,1)S(1)} %get-tuple-element.138), channel_id=1, source_target_pairs={{0,127},{1,126},{2,125},{3,124},{4,123},{5,122},{6,121},{7,120},{8... | collective-permute-start | bytes 196616 | tf_op jit(solution)/shard_map/ppermute | solution.py:206
  61.2 7.3 %collective-permute-start.8 = (bf16[128,256]{1,0:T(8,128)(2,1)S(1)}, bf16[128,256]{1,0:T(8,128)(2,1)S(1)}, u32[]{:S(2)}, u32[]{:S(2)}) collective-permute-start(bf16[128,256]{1,0:T(8,128)(2,1)S(1)} %get-tuple-element.138), channel_id=1, source_target_pairs={{0,126},{1,127},{2,124},{3,125},{4,122},{5,123},{6,120},{7,121},{8... | collective-permute-start | bytes 196616 | tf_op jit(solution)/shard_map/ppermute | solution.py:206
  83.0 12.7 %collective-permute-start.15 = (f32[3,128,256]{2,1,0:T(8,128)S(1)}, f32[3,128,256]{2,1,0:T(8,128)S(1)}, u32[]{:S(2)}, u32[]{:S(2)}) collective-permute-start(f32[3,128,256]{2,1,0:T(8,128)S(1)} %get-tuple-element.161), channel_id=1, source_target_pairs={{0,124},{1,125},{2,126},{3,127},{4,120},{5,121},{6,122},{7,123},{8... | collective-permute-start | bytes 1179656 | tf_op jit(solution)/shard_map/ppermute | solution.py:206
  83.5 9.2 %collective-permute-start.14 = (bf16[128,256]{1,0:T(8,128)(2,1)S(1)}, bf16[128,256]{1,0:T(8,128)(2,1)S(1)}, u32[]{:S(2)}, u32[]{:S(2)}) collective-permute-start(bf16[128,256]{1,0:T(8,128)(2,1)S(1)} %get-tuple-element.152), channel_id=1, source_target_pairs={{0,127},{1,126},{2,125},{3,124},{4,123},{5,122},{6,121},{7,120},{8... | collective-permute-start | bytes 196616 | tf_op jit(solution)/shard_map/ppermute | solution.py:206
  86.2 7.5 %collective-permute-start.13 = (bf16[128,256]{1,0:T(8,128)(2,1)S(1)}, bf16[128,256]{1,0:T(8,128)(2,1)S(1)}, u32[]{:S(2)}, u32[]{:S(2)}) collective-permute-start(bf16[128,256]{1,0:T(8,128)(2,1)S(1)} %get-tuple-element.152), channel_id=1, source_target_pairs={{0,126},{1,127},{2,124},{3,125},{4,122},{5,123},{6,120},{7,121},{8... | collective-permute-start | bytes 196616 | tf_op jit(solution)/shard_map/ppermute | solution.py:206
  107.9 12.9 %collective-permute-start.20 = (f32[3,128,256]{2,1,0:T(8,128)S(1)}, f32[3,128,256]{2,1,0:T(8,128)S(1)}, u32[]{:S(2)}, u32[]{:S(2)}) collective-permute-start(f32[3,128,256]{2,1,0:T(8,128)S(1)} %get-tuple-element.175), channel_id=1, source_target_pairs={{0,124},{1,125},{2,126},{3,127},{4,120},{5,121},{6,122},{7,123},{8... | collective-permute-start | bytes 1179656 | tf_op jit(solution)/shard_map/ppermute | solution.py:206
  108.2 9.5 %collective-permute-start.19 = (bf16[128,256]{1,0:T(8,128)(2,1)S(1)}, bf16[128,256]{1,0:T(8,128)(2,1)S(1)}, u32[]{:S(2)}, u32[]{:S(2)}) collective-permute-start(bf16[128,256]{1,0:T(8,128)(2,1)S(1)} %get-tuple-element.166), channel_id=1, source_target_pairs={{0,127},{1,126},{2,125},{3,124},{4,123},{5,122},{6,121},{7,120},{8... | collective-permute-start | bytes 196616 | tf_op jit(solution)/shard_map/ppermute | solution.py:206
  111.4 7.3 %collective-permute-start.18 = (bf16[128,256]{1,0:T(8,128)(2,1)S(1)}, bf16[128,256]{1,0:T(8,128)(2,1)S(1)}, u32[]{:S(2)}, u32[]{:S(2)}) collective-permute-start(bf16[128,256]{1,0:T(8,128)(2,1)S(1)} %get-tuple-element.166), channel_id=1, source_target_pairs={{0,126},{1,127},{2,124},{3,125},{4,122},{5,123},{6,120},{7,121},{8... | collective-permute-start | bytes 196616 | tf_op jit(solution)/shard_map/ppermute | solution.py:206
  132.1 15.7 %collective-permute-start.25 = (f32[3,128,256]{2,1,0:T(8,128)S(1)}, f32[3,128,256]{2,1,0:T(8,128)S(1)}, u32[]{:S(2)}, u32[]{:S(2)}) collective-permute-start(f32[3,128,256]{2,1,0:T(8,128)S(1)} %get-tuple-element.189), channel_id=1, source_target_pairs={{0,124},{1,125},{2,126},{3,127},{4,120},{5,121},{6,122},{7,123},{8... | collective-permute-start | bytes 1179656 | tf_op jit(solution)/shard_map/ppermute | solution.py:206
  134.5 8.8 %collective-permute-start.24 = (bf16[128,256]{1,0:T(8,128)(2,1)S(1)}, bf16[128,256]{1,0:T(8,128)(2,1)S(1)}, u32[]{:S(2)}, u32[]{:S(2)}) collective-permute-start(bf16[128,256]{1,0:T(8,128)(2,1)S(1)} %get-tuple-element.180), channel_id=1, source_target_pairs={{0,127},{1,126},{2,125},{3,124},{4,123},{5,122},{6,121},{7,120},{8... | collective-permute-start | bytes 196616 | tf_op jit(solution)/shard_map/ppermute | solution.py:206
  137.9 7.3 %collective-permute-start.23 = (bf16[128,256]{1,0:T(8,128)(2,1)S(1)}, bf16[128,256]{1,0:T(8,128)(2,1)S(1)}, u32[]{:S(2)}, u32[]{:S(2)}) collective-permute-start(bf16[128,256]{1,0:T(8,128)(2,1)S(1)} %get-tuple-element.180), channel_id=1, source_target_pairs={{0,126},{1,127},{2,124},{3,125},{4,122},{5,123},{6,120},{7,121},{8... | collective-permute-start | bytes 196616 | tf_op jit(solution)/shard_map/ppermute | solution.py:206
  160.1 12.7 %collective-permute-start.30 = (f32[3,128,256]{2,1,0:T(8,128)S(1)}, f32[3,128,256]{2,1,0:T(8,128)S(1)}, u32[]{:S(2)}, u32[]{:S(2)}) collective-permute-start(f32[3,128,256]{2,1,0:T(8,128)S(1)} %get-tuple-element.203), channel_id=1, source_target_pairs={{0,124},{1,125},{2,126},{3,127},{4,120},{5,121},{6,122},{7,123},{8... | collective-permute-start | bytes 1179656 | tf_op jit(solution)/shard_map/ppermute | solution.py:206
  160.4 9.3 %collective-permute-start.29 = (bf16[128,256]{1,0:T(8,128)(2,1)S(1)}, bf16[128,256]{1,0:T(8,128)(2,1)S(1)}, u32[]{:S(2)}, u32[]{:S(2)}) collective-permute-start(bf16[128,256]{1,0:T(8,128)(2,1)S(1)} %get-tuple-element.194), channel_id=1, source_target_pairs={{0,127},{1,126},{2,125},{3,124},{4,123},{5,122},{6,121},{7,120},{8... | collective-permute-start | bytes 196616 | tf_op jit(solution)/shard_map/ppermute | solution.py:206
  162.9 7.8 %collective-permute-start.28 = (bf16[128,256]{1,0:T(8,128)(2,1)S(1)}, bf16[128,256]{1,0:T(8,128)(2,1)S(1)}, u32[]{:S(2)}, u32[]{:S(2)}) collective-permute-start(bf16[128,256]{1,0:T(8,128)(2,1)S(1)} %get-tuple-element.194), channel_id=1, source_target_pairs={{0,126},{1,127},{2,124},{3,125},{4,122},{5,123},{6,120},{7,121},{8... | collective-permute-start | bytes 196616 | tf_op jit(solution)/shard_map/ppermute | solution.py:206
  163.9 6.8 %collective-permute-start.27 = (bf16[128,256]{1,0:T(8,128)(2,1)S(1)}, bf16[128,256]{1,0:T(8,128)(2,1)S(1)}, u32[]{:S(2)}, u32[]{:S(2)}) collective-permute-start(bf16[128,256]{1,0:T(8,128)(2,1)S(1)} %get-tuple-element.194), channel_id=1, source_target_pairs={{0,125},{1,124},{2,127},{3,126},{4,121},{5,120},{6,123},{7,122},{8... | collective-permute-start | bytes 196616 | tf_op jit(solution)/shard_map/ppermute | solution.py:206
  184.9 12.8 %collective-permute-start.35 = (f32[3,128,256]{2,1,0:T(8,128)S(1)}, f32[3,128,256]{2,1,0:T(8,128)S(1)}, u32[]{:S(2)}, u32[]{:S(2)}) collective-permute-start(f32[3,128,256]{2,1,0:T(8,128)S(1)} %get-tuple-element.218), channel_id=1, source_target_pairs={{0,124},{1,125},{2,126},{3,127},{4,120},{5,121},{6,122},{7,123},{8... | collective-permute-start | bytes 1179656 | tf_op jit(solution)/shard_map/ppermute | solution.py:206
  184.9 9.5 %collective-permute-start.34 = (bf16[128,256]{1,0:T(8,128)(2,1)S(1)}, bf16[128,256]{1,0:T(8,128)(2,1)S(1)}, u32[]{:S(2)}, u32[]{:S(2)}) collective-permute-start(bf16[128,256]{1,0:T(8,128)(2,1)S(1)} %get-tuple-element.208), channel_id=1, source_target_pairs={{0,127},{1,126},{2,125},{3,124},{4,123},{5,122},{6,121},{7,120},{8... | collective-permute-start | bytes 196616 | tf_op jit(solution)/shard_map/ppermute | solution.py:206
  187.9 7.3 %collective-permute-start.33 = (bf16[128,256]{1,0:T(8,128)(2,1)S(1)}, bf16[128,256]{1,0:T(8,128)(2,1)S(1)}, u32[]{:S(2)}, u32[]{:S(2)}) collective-permute-start(bf16[128,256]{1,0:T(8,128)(2,1)S(1)} %get-tuple-element.208), channel_id=1, source_target_pairs={{0,126},{1,127},{2,124},{3,125},{4,122},{5,123},{6,120},{7,121},{8... | collective-permute-start | bytes 196616 | tf_op jit(solution)/shard_map/ppermute | solution.py:206
  (20 other events, 190.1 us)

commit v3 on v2

--- a/solution.py
+++ b/solution.py
@@ -23,59 +23,81 @@
     return values, moment_one, moment_two
 
 
+def words(meta, stratum):
+    return meta[stratum, 0, 0], meta[stratum, 1, 0]
+
+
+def field(word, at, bits):
+    return (word >> at) & ((1 << bits) - 1)
+
+
+def row_of(rows, slot):
+    return field(rows, 3 * slot, 3)
+
+
+def col_of(rest, slot):
+    return block_at(field(rest, 2 * slot, 2))
+
+
+def live_of(rest):
+    return field(rest, 16, 4)
+
+
+def place_of(rest):
+    return field(rest, 20, 2)
+
+
 def block_at(index):
     return pl.ds(pl.multiple_of(index * EDGE, EDGE), EDGE)
 
 
-def slot_grads(stratum, slots, meta, items, users, teacher, residual, grad):
-    grad[...] = jnp.zeros_like(grad)
-    live = meta[stratum, 2 * slots]
-    for slot in range(slots):
-        user_block = users[block_at(meta[stratum, slot]), :]
-        col = block_at(meta[stratum, slots + slot])
+def slot_grads(stratum, slots, meta, items, users, teacher, residual, parts):
+    shard = parts.shape[1] // 2
+    rows, rest = words(meta, stratum)
+    blocks = [users[block_at(row_of(rows, slot)), :] for slot in range(slots)]
+    for slot, user_block in enumerate(blocks):
         predicted = lax.dot_general(
-            user_block, items[col, :], (((1,), (1,)), ((), ())), preferred_element_type=F32
+            items[col_of(rest, slot), :], user_block, (((1,), (1,)), ((), ())), preferred_element_type=F32
         )
-        left = jnp.where(slot < live, predicted - teacher[stratum, slot].astype(F32), 0.0).astype(BF16)
-        residual[slot] = left
-        grad[col, :] += lax.dot_general(
-            left, user_block, (((0,), (0,)), ((), ())), preferred_element_type=F32
-        )
-
-
-def spread_parts(grad, parts):
-    shard = parts.shape[1] // 2
-    for owner in range(OWNERS):
-        for side in range(2):
-            at = (side * OWNERS + owner) * shard
-            rows = grad[at : at + shard, :].astype(BF16)
-            for copy in range(parts.shape[0] // OWNERS):
-                parts[copy * OWNERS + owner, side * shard : (side + 1) * shard, :] = rows
-
-
-def first_item_kernel(stratum, slots, meta, items, users, teacher, parts, residual, grad):
-    slot_grads(stratum, slots, meta, items, users, teacher, residual, grad)
-    spread_parts(grad, parts)
+        scores = teacher[stratum, slot].T.astype(F32)
+        residual[slot] = jnp.where(slot < live_of(rest), predicted - scores, 0.0).astype(BF16)
+    stacked = jnp.concatenate(blocks, axis=0)
+    for block in range(items.shape[0] // EDGE):
+        hits = [
+            jnp.where(field(rest, 2 * slot, 2) == block, residual[slot], jnp.zeros((), BF16)) for slot in range(slots)
+        ]
+        grad = jnp.dot(jnp.concatenate(hits, axis=1), stacked, preferred_element_type=F32).astype(BF16)
+        for piece in range(EDGE // shard):
+            at = block * (EDGE // shard) + piece
+            span = slice(at // OWNERS * shard, (at // OWNERS + 1) * shard)
+            for owner in range(at % OWNERS, parts.shape[0], OWNERS):
+                parts[owner, span, :] = grad[piece * shard : (piece + 1) * shard, :]
+
+
+def first_item_kernel(stratum, slots, meta, items, users, teacher, parts, residual):
+    slot_grads(stratum, slots, meta, items, users, teacher, residual, parts)
 
 
 def item_kernel(stratum, slots, meta, *refs):
     got = refs[:OWNERS]
-    users, teacher, parts, residual, items, grad = refs[OWNERS:]
+    users, teacher, parts, residual, items = refs[OWNERS:]
     shard = got[0].shape[0] // 2
-    place = meta[stratum, 2 * slots + 1]
+    place = place_of(words(meta, stratum)[1])
     for hop in range(OWNERS):
         start = pl.multiple_of((place ^ hop) * shard, shard)
         items[pl.ds(start, shard), :] = got[hop][:shard, :]
         items[pl.ds(start + OWNERS * shard, shard), :] = got[hop][shard:, :]
-    slot_grads(stratum, slots, meta, items, users, teacher, residual, grad)
-    spread_parts(grad, parts)
+    slot_grads(stratum, slots, meta, items, users, teacher, residual, parts)
 
 
 def user_grads(stratum, slots, meta, items, residual, grad):
     grad[...] = jnp.zeros_like(grad)
+    rows, rest = words(meta, stratum)
     for slot in range(slots):
-        col = block_at(meta[stratum, slots + slot])
-        grad[meta[stratum, slot]] += jnp.dot(residual[slot], items[col, :], preferred_element_type=F32)
+        col = col_of(rest, slot)
+        grad[row_of(rows, slot)] += lax.dot_general(
+            residual[slot], items[col, :], (((0,), (0,)), ((), ())), preferred_element_type=F32
+        )
 
 
 def user_kernel(stratum, slots, meta, items, residual, values, one, two, values_out, one_out, two_out, rounded, grad):
@@ -125,7 +147,7 @@
         state_out[0] = new
         rounded[...] = new.astype(BF16)
 
-    side = meta[0, 2 * slots + 3]
+    side = field(words(meta, 0)[1], 23, 1)
 
     @pl.when(side == 0)
     def _():
@@ -138,7 +160,7 @@
 
 def last_owner_kernel(stratum, slots, meta, parts, state, state_out):
     shard = state.shape[1] // 2
-    rows = pl.ds(pl.multiple_of(meta[stratum, 2 * slots + 2] * shard, shard), shard)
+    rows = pl.ds(pl.multiple_of(field(words(meta, stratum)[1], 22, 1) * shard, shard), shard)
     total = parts[0, rows, :].astype(F32)
     for part in range(1, parts.shape[0]):
         total += parts[part, rows, :].astype(F32)
@@ -208,9 +230,11 @@
     rep = lax.axis_index("rep")
     side = rep // OWNERS
     keep = (side + 1 - lax.axis_index("blk") % 2) % 2
-    places = jnp.broadcast_to(jnp.stack([rep % OWNERS, keep, side]), (strata, 3))
-    meta = jnp.concatenate([block_rows[0, 0], block_cols[0, 0], live_slots[0, 0][:, None], places], axis=1)
-    smem = pl.BlockSpec(memory_space=pltpu.SMEM)
+    slot_at = jnp.arange(slots, dtype=jnp.int32)
+    row_words = jnp.sum(block_rows[0, 0] << (3 * slot_at), axis=1)
+    col_words = jnp.sum(block_cols[0, 0] << (2 * slot_at), axis=1)
+    col_words += (live_slots[0, 0] << 16) + ((rep % OWNERS) << 20) + (keep << 22) + (side << 23)
+    meta = jnp.broadcast_to(jnp.stack([row_words, col_words], axis=1)[:, :, None], (strata, 2, EDGE))
 
     scores = teacher[0, 0]
     users = (user_factors, user_first, user_second)
@@ -233,29 +257,26 @@
 
     parts_shape = VMEM((reps, 2 * shard, rank), BF16)
     residual_shape = VMEM((slots, EDGE, EDGE), BF16)
-    item_scratch = [VMEM((item_rows, rank), F32)]
     for stratum in range(strata):
         last = stratum == strata - 1
         if stratum == 0:
             parts, residual = pl.pallas_call(
                 functools.partial(first_item_kernel, stratum, slots),
-                in_specs=[smem] + vmem_specs(3),
+                in_specs=vmem_specs(1 + 3),
                 out_specs=vmem_specs(2),
                 out_shape=[parts_shape, residual_shape],
-                scratch_shapes=item_scratch,
                 compiler_params=LIMIT,
                 name="item_grad",
-            )(meta, *in_vmem(items, user_bf, scores))
+            )(*in_vmem(meta, items, user_bf, scores))
         else:
             parts, residual, items = pl.pallas_call(
                 functools.partial(item_kernel, stratum, slots),
-                in_specs=[smem] + vmem_specs(OWNERS + 2),
+                in_specs=vmem_specs(1 + OWNERS + 2),
                 out_specs=vmem_specs(3),
                 out_shape=[parts_shape, residual_shape, VMEM((item_rows, rank), BF16)],
-                scratch_shapes=item_scratch,
                 compiler_params=LIMIT,
                 name="item_grad",
-            )(meta, *in_vmem(*got, user_bf, scores))
+            )(*in_vmem(meta, *got, user_bf, scores))
         if stratum > 0:
             parts, state = lax.optimization_barrier((parts, state))
         parts = lax.all_to_all(parts, "rep", 0, 0)
@@ -263,49 +284,49 @@
         if last:
             state = pl.pallas_call(
                 functools.partial(last_owner_kernel, stratum, slots),
-                in_specs=[smem] + vmem_specs(2),
+                in_specs=vmem_specs(1 + 2),
                 out_specs=vmem_specs(1)[0],
                 out_shape=VMEM((3, shard, rank), F32),
                 compiler_params=LIMIT,
                 name="owner_adam",
-            )(meta, *in_vmem(parts, state))
+            )(*in_vmem(meta, parts, state))
             residual, state = lax.optimization_barrier((residual, state))
             state = shifted(state)
             by_block = pl.BlockSpec((2 * EDGE, rank), lambda at: (at, 0))
             users = pl.pallas_call(
                 functools.partial(last_user_kernel, stratum, slots),
                 grid=(user_rows // (2 * EDGE),),
-                in_specs=[smem] + vmem_specs(2) + [by_block] * 3,
+                in_specs=vmem_specs(1 + 2) + [by_block] * 3,
                 out_specs=[by_block] * 3,
                 out_shape=[jax.ShapeDtypeStruct((user_rows, rank), F32)] * 3,
                 scratch_shapes=scratch,
                 compiler_params=LIMIT,
                 cost_estimate=USER_COST,
                 name="last_user_adam",
-            )(meta, *in_vmem(items, residual), *users)
+            )(*in_vmem(meta, items, residual), *users)
         else:
             first = stratum == 0
             state, rounded = pl.pallas_call(
                 functools.partial(first_owner_kernel, slots) if first else owner_kernel,
-                in_specs=[smem] * first + vmem_specs(3 if first else 2),
+                in_specs=vmem_specs(4 if first else 2),
                 out_specs=vmem_specs(2),
                 out_shape=[VMEM((3, 2 * shard, rank), F32), VMEM((2 * shard, rank), BF16)],
                 compiler_params=LIMIT,
                 name="owner_adam",
-            )(*[meta] * first, *in_vmem(parts, *((own, other) if first else (state,))))
+            )(*in_vmem(*[meta] * first, parts, *((own, other) if first else (state,))))
             residual, rounded, state = lax.optimization_barrier((residual, rounded, state))
             state = shifted(state)
             got = [shifted(rounded, hop) for hop in reversed(range(OWNERS))][::-1]
             *users, user_bf = pl.pallas_call(
                 functools.partial(user_kernel, stratum, slots),
-                in_specs=[smem] + vmem_specs(5),
+                in_specs=vmem_specs(1 + 5),
                 out_specs=vmem_specs(4),
                 out_shape=[VMEM((user_rows, rank), kind) for kind in (F32, F32, F32, BF16)],
                 scratch_shapes=scratch,
                 compiler_params=LIMIT,
                 cost_estimate=USER_COST,
                 name="user_adam",
-            )(meta, *in_vmem(items, residual, *users))
+            )(*in_vmem(meta, items, residual, *users))
 
     items = pl.pallas_call(
         finish_kernel,

time: 218 us -> 211 us (0.968)
  Pallas kernels: 30.7 us -> 19.8 us
    pallas_call x14, Pallas kernels: 22 us -> 13.4 us  [the longest x7 8.77 us: on_device(): pl.pallas_call(functools.partial(user_kernel, stratum, slots), in_specs=v...]
    ppermute x36, waiting for transfers between devices: 24.1 us -> 27.6 us  [shifted(): return lax.ppermute(value, ('blk', 'rep'), moves(hop))]
  transfers between devices with their start and end apart: 38 -> 38, of which waited for: 21 -> 22; matrix products, arithmetic and copies ran while one was open for 1% -> 2% of each run, Pallas kernels for 12% -> 8%
where the time goes in v3:
time: 211 us; the launch traced here: 210 us
  blocking collectives  93.1 us (44%)
  starting transfers between devices  61.6 us (29%)
  waiting for transfers between devices  30 us (14%)
  Pallas kernels  19.8 us (9%)
  other arithmetic  3.56 us (2%)
    all_to_all x8, blocking collectives, on_device(): parts = lax.all_to_all(parts, 'rep', 0, 0)  93.1 us
    ppermute x36, starting transfers between devices, shifted(): return lax.ppermute(value, ('blk', 'rep'), moves(hop))  54.4 us
    ppermute x36, waiting for transfers between devices, shifted(): return lax.ppermute(value, ('blk', 'rep'), moves(hop))  27.6 us
    pallas_call x7, Pallas kernels, on_device(): pl.pallas_call(functools.partial(user_kernel, stratum, slots), in_specs=v...  8.77 us
    all_to_all x1, starting transfers between devices, on_device(): items = lax.all_to_all(copies, 'rep', 0, 0).reshape(item_rows, rank)  5.03 us
    pallas_call x7, Pallas kernels, on_device(): pl.pallas_call(functools.partial(item_kernel, stratum, slots), in_specs=v...  4.64 us
  transfers between devices with their start and end apart: 38, of which 22 were waited for; matrix products, arithmetic and copies ran while one was open for 2% of the time, Pallas kernels for 8%

profile of v3, /device:TPU:1, one launch (start us, length us, event | category | flops | bytes accessed | tf_op | source)
XLA Modules:
  0.0 210.1 jit_solution(46216552220029648)
XLA Ops:
  4.7 5.0 %all-to-all-start = ((bf16[8,64,256]{2,1,0:T(8,128)(2,1)}), bf16[8,64,256]{2,1,0:T(8,128)(2,1)S(1)}, u32[]{:S(2)}, u32[]{:S(2)}) async-start(bf16[8,64,256]{2,1,0:T(8,128)(2,1)} %broadcast_in_dim.7), calls=%async_computation | async-start | bytes 524288 | tf_op jit(solution)/shard_map/all_to_all | solution.py:255
  13.4 2.4 %all-to-all-done = bf16[8,64,256]{2,1,0:T(8,128)(2,1)S(1)} async-done(((bf16[8,64,256]{2,1,0:T(8,128)(2,1)}), bf16[8,64,256]{2,1,0:T(8,128)(2,1)S(1)}, u32[]{:S(2)}, u32[]{:S(2)}) %all-to-all-start) | async-done | bytes 262176 | tf_op jit(solution)/shard_map/all_to_all | solution.py:255
  16.6 10.1 %all_to_all.45.parts = bf16[8,128,256]{2,1,0:T(8,128)(2,1)S(1)} all-to-all(bf16[8,128,256]{2,1,0:T(8,128)(2,1)S(1)} %get-tuple-element.123), channel_id=1, replica_groups=mesh['blk'=16,'rep'=8] {'rep'}, dimensions={0} | all-to-all | bytes 1048576 | tf_op jit(solution)/shard_map/all_to_all | solution.py:282
  26.9 3.6 %collective-permute-start.5 = (f32[3,128,256]{2,1,0:T(8,128)S(1)}, f32[3,128,256]{2,1,0:T(8,128)S(1)}, u32[]{:S(2)}, u32[]{:S(2)}) collective-permute-start(f32[3,128,256]{2,1,0:T(8,128)S(1)} %get-tuple-element.133), channel_id=1, source_target_pairs={{0,124},{1,125},{2,126},{3,127},{4,120},{5,121},{6,122},{7,123},{8... | collective-permute-start | bytes 1179656 | tf_op jit(solution)/shard_map/ppermute | solution.py:228
  32.6 4.4 %collective-permute-start.3 = (bf16[128,256]{1,0:T(8,128)(2,1)S(1)}, bf16[128,256]{1,0:T(8,128)(2,1)S(1)}, u32[]{:S(2)}, u32[]{:S(2)}) collective-permute-start(bf16[128,256]{1,0:T(8,128)(2,1)S(1)} %get-tuple-element.128), channel_id=1, source_target_pairs={{0,126},{1,127},{2,124},{3,125},{4,122},{5,123},{6,120},{7,121},{8... | collective-permute-start | bytes 196616 | tf_op jit(solution)/shard_map/ppermute | solution.py:228
  40.1 2.7 %collective-permute-done.2.refs_1_ = bf16[128,256]{1,0:T(8,128)(2,1)S(1)} collective-permute-done((bf16[128,256]{1,0:T(8,128)(2,1)S(1)}, bf16[128,256]{1,0:T(8,128)(2,1)S(1)}, u32[]{:S(2)}, u32[]{:S(2)}) %collective-permute-start.2) | collective-permute-done | bytes 65568 | tf_op jit(solution)/shard_map/ppermute | solution.py:228
  43.9 11.9 %all_to_all.46.parts = bf16[8,128,256]{2,1,0:T(8,128)(2,1)S(1)} all-to-all(bf16[8,128,256]{2,1,0:T(8,128)(2,1)S(1)} %get-tuple-element.134), channel_id=1, replica_groups=mesh['blk'=16,'rep'=8] {'rep'}, dimensions={0} | all-to-all | bytes 1048576 | tf_op jit(solution)/shard_map/all_to_all | solution.py:282
  56.0 3.2 %collective-permute-start.9 = (bf16[128,256]{1,0:T(8,128)(2,1)S(1)}, bf16[128,256]{1,0:T(8,128)(2,1)S(1)}, u32[]{:S(2)}, u32[]{:S(2)}) collective-permute-start(bf16[128,256]{1,0:T(8,128)(2,1)S(1)} %get-tuple-element.138), channel_id=1, source_target_pairs={{0,127},{1,126},{2,125},{3,124},{4,123},{5,122},{6,121},{7,120},{8... | collective-permute-start | bytes 196616 | tf_op jit(solution)/shard_map/ppermute | solution.py:228
  68.0 12.1 %all_to_all.47.parts = bf16[8,128,256]{2,1,0:T(8,128)(2,1)S(1)} all-to-all(bf16[8,128,256]{2,1,0:T(8,128)(2,1)S(1)} %get-tuple-element.148), channel_id=1, replica_groups=mesh['blk'=16,'rep'=8] {'rep'}, dimensions={0} | all-to-all | bytes 1048576 | tf_op jit(solution)/shard_map/all_to_all | solution.py:282
  80.8 2.7 %collective-permute-start.14 = (bf16[128,256]{1,0:T(8,128)(2,1)S(1)}, bf16[128,256]{1,0:T(8,128)(2,1)S(1)}, u32[]{:S(2)}, u32[]{:S(2)}) collective-permute-start(bf16[128,256]{1,0:T(8,128)(2,1)S(1)} %get-tuple-element.152), channel_id=1, source_target_pairs={{0,127},{1,126},{2,125},{3,124},{4,123},{5,122},{6,121},{7,120},{8... | collective-permute-start | bytes 196616 | tf_op jit(solution)/shard_map/ppermute | solution.py:228
  92.2 12.0 %all_to_all.48.parts = bf16[8,128,256]{2,1,0:T(8,128)(2,1)S(1)} all-to-all(bf16[8,128,256]{2,1,0:T(8,128)(2,1)S(1)} %get-tuple-element.162), channel_id=1, replica_groups=mesh['blk'=16,'rep'=8] {'rep'}, dimensions={0} | all-to-all | bytes 1048576 | tf_op jit(solution)/shard_map/all_to_all | solution.py:282
  104.4 3.2 %collective-permute-start.19 = (bf16[128,256]{1,0:T(8,128)(2,1)S(1)}, bf16[128,256]{1,0:T(8,128)(2,1)S(1)}, u32[]{:S(2)}, u32[]{:S(2)}) collective-permute-start(bf16[128,256]{1,0:T(8,128)(2,1)S(1)} %get-tuple-element.166), channel_id=1, source_target_pairs={{0,127},{1,126},{2,125},{3,124},{4,123},{5,122},{6,121},{7,120},{8... | collective-permute-start | bytes 196616 | tf_op jit(solution)/shard_map/ppermute | solution.py:228
  116.3 11.1 %all_to_all.49.parts = bf16[8,128,256]{2,1,0:T(8,128)(2,1)S(1)} all-to-all(bf16[8,128,256]{2,1,0:T(8,128)(2,1)S(1)} %get-tuple-element.176), channel_id=1, replica_groups=mesh['blk'=16,'rep'=8] {'rep'}, dimensions={0} | all-to-all | bytes 1048576 | tf_op jit(solution)/shard_map/all_to_all | solution.py:282
  130.0 3.4 %collective-permute-start.24 = (bf16[128,256]{1,0:T(8,128)(2,1)S(1)}, bf16[128,256]{1,0:T(8,128)(2,1)S(1)}, u32[]{:S(2)}, u32[]{:S(2)}) collective-permute-start(bf16[128,256]{1,0:T(8,128)(2,1)S(1)} %get-tuple-element.180), channel_id=1, source_target_pairs={{0,127},{1,126},{2,125},{3,124},{4,123},{5,122},{6,121},{7,120},{8... | collective-permute-start | bytes 196616 | tf_op jit(solution)/shard_map/ppermute | solution.py:228
  134.3 2.7 %collective-permute-start.22 = (bf16[128,256]{1,0:T(8,128)(2,1)S(1)}, bf16[128,256]{1,0:T(8,128)(2,1)S(1)}, u32[]{:S(2)}, u32[]{:S(2)}) collective-permute-start(bf16[128,256]{1,0:T(8,128)(2,1)S(1)} %get-tuple-element.180), channel_id=1, source_target_pairs={{0,125},{1,124},{2,127},{3,126},{4,121},{5,120},{6,123},{7,122},{8... | collective-permute-start | bytes 196616 | tf_op jit(solution)/shard_map/ppermute | solution.py:228
  142.6 12.1 %all_to_all.50.parts = bf16[8,128,256]{2,1,0:T(8,128)(2,1)S(1)} all-to-all(bf16[8,128,256]{2,1,0:T(8,128)(2,1)S(1)} %get-tuple-element.190), channel_id=1, replica_groups=mesh['blk'=16,'rep'=8] {'rep'}, dimensions={0} | all-to-all | bytes 1048576 | tf_op jit(solution)/shard_map/all_to_all | solution.py:282
  155.1 2.4 %collective-permute-start.29 = (bf16[128,256]{1,0:T(8,128)(2,1)S(1)}, bf16[128,256]{1,0:T(8,128)(2,1)S(1)}, u32[]{:S(2)}, u32[]{:S(2)}) collective-permute-start(bf16[128,256]{1,0:T(8,128)(2,1)S(1)} %get-tuple-element.194), channel_id=1, source_target_pairs={{0,127},{1,126},{2,125},{3,124},{4,123},{5,122},{6,121},{7,120},{8... | collective-permute-start | bytes 196616 | tf_op jit(solution)/shard_map/ppermute | solution.py:228
  158.5 2.4 %collective-permute-start.27 = (bf16[128,256]{1,0:T(8,128)(2,1)S(1)}, bf16[128,256]{1,0:T(8,128)(2,1)S(1)}, u32[]{:S(2)}, u32[]{:S(2)}) collective-permute-start(bf16[128,256]{1,0:T(8,128)(2,1)S(1)} %get-tuple-element.194), channel_id=1, source_target_pairs={{0,125},{1,124},{2,127},{3,126},{4,121},{5,120},{6,123},{7,122},{8... | collective-permute-start | bytes 196616 | tf_op jit(solution)/shard_map/ppermute | solution.py:228
  166.8 11.8 %all_to_all.51.parts = bf16[8,128,256]{2,1,0:T(8,128)(2,1)S(1)} all-to-all(bf16[8,128,256]{2,1,0:T(8,128)(2,1)S(1)} %get-tuple-element.204), channel_id=1, replica_groups=mesh['blk'=16,'rep'=8] {'rep'}, dimensions={0} | all-to-all | bytes 1048576 | tf_op jit(solution)/shard_map/all_to_all | solution.py:282
  178.9 2.9 %collective-permute-start.34 = (bf16[128,256]{1,0:T(8,128)(2,1)S(1)}, bf16[128,256]{1,0:T(8,128)(2,1)S(1)}, u32[]{:S(2)}, u32[]{:S(2)}) collective-permute-start(bf16[128,256]{1,0:T(8,128)(2,1)S(1)} %get-tuple-element.208), channel_id=1, source_target_pairs={{0,127},{1,126},{2,125},{3,124},{4,123},{5,122},{6,121},{7,120},{8... | collective-permute-start | bytes 196616 | tf_op jit(solution)/shard_map/ppermute | solution.py:228
  182.8 2.5 %collective-permute-start.32 = (bf16[128,256]{1,0:T(8,128)(2,1)S(1)}, bf16[128,256]{1,0:T(8,128)(2,1)S(1)}, u32[]{:S(2)}, u32[]{:S(2)}) collective-permute-start(bf16[128,256]{1,0:T(8,128)(2,1)S(1)} %get-tuple-element.208), channel_id=1, source_target_pairs={{0,125},{1,124},{2,127},{3,126},{4,121},{5,120},{6,123},{7,122},{8... | collective-permute-start | bytes 196616 | tf_op jit(solution)/shard_map/ppermute | solution.py:228
  190.8 12.0 %all_to_all.52.parts = bf16[8,128,256]{2,1,0:T(8,128)(2,1)S(1)} all-to-all(bf16[8,128,256]{2,1,0:T(8,128)(2,1)S(1)} %get-tuple-element.219), channel_id=1, replica_groups=mesh['blk'=16,'rep'=8] {'rep'}, dimensions={0} | all-to-all | bytes 1048576 | tf_op jit(solution)/shard_map/all_to_all | solution.py:282
  203.0 2.7 %last_user_adam.1 = (f32[1024,256]{1,0:T(8,128)}, f32[1024,256]{1,0:T(8,128)}, f32[1024,256]{1,0:T(8,128)}) custom-call(s32[8,2,128]{2,1,0:T(2,128)S(1)} %broadcast_in_dim.8.meta, bf16[512,256]{1,0:T(8,128)(2,1)S(1)} %get-tuple-element.215.items, bf16[8,128,128]{2,1,0:T(8,128)(2,1)S(1)} %get-tuple-element.221.residual, ...), custom_call_target="tpu_custom_call" | custom-call | flops 300000000 | bytes 8000000 | tf_op jit(solution)/shard_map/last_user_adam/pallas_call | solution.py:296
  205.7 3.6 %collective-permute-done.36.state = f32[3,64,256]{2,1,0:T(8,128)S(1)} collective-permute-done((f32[3,64,256]{2,1,0:T(8,128)S(1)}, f32[3,64,256]{2,1,0:T(8,128)S(1)}, u32[]{:S(2)}, u32[]{:S(2)}) %collective-permute-start.36) | collective-permute-done | bytes 196640 | tf_op jit(solution)/shard_map/ppermute | solution.py:228
  (105 shorter events, 66.0 us)
Async XLA Ops:
  1.7 11.6 %collective-permute-start = (f32[3,64,256]{2,1,0:T(8,128)S(1)}, f32[3,64,256]{2,1,0:T(8,128)S(1)}, u32[]{:S(2)}, u32[]{:S(2)}) collective-permute-start(f32[3,64,256]{2,1,0:T(8,128)S(1)} %start.1.own), channel_id=1, source_target_pairs={{0,4},{1,5},{2,6},{3,7},{4,0},{5,1},{6,2},{7,3},{8,12},{9,13},{10,... | collective-permute-start | bytes 589832 | tf_op jit(solution)/shard_map/ppermute | solution.py:253
  4.7 11.2 %all-to-all-start = ((bf16[8,64,256]{2,1,0:T(8,128)(2,1)}), bf16[8,64,256]{2,1,0:T(8,128)(2,1)S(1)}, u32[]{:S(2)}, u32[]{:S(2)}) async-start(bf16[8,64,256]{2,1,0:T(8,128)(2,1)} %broadcast_in_dim.7), calls=%async_computation | async-start | bytes 524288 | tf_op jit(solution)/shard_map/all_to_all | solution.py:255
  26.9 17.0 %collective-permute-start.5 = (f32[3,128,256]{2,1,0:T(8,128)S(1)}, f32[3,128,256]{2,1,0:T(8,128)S(1)}, u32[]{:S(2)}, u32[]{:S(2)}) collective-permute-start(f32[3,128,256]{2,1,0:T(8,128)S(1)} %get-tuple-element.133), channel_id=1, source_target_pairs={{0,124},{1,125},{2,126},{3,127},{4,120},{5,121},{6,122},{7,123},{8... | collective-permute-start | bytes 1179656 | tf_op jit(solution)/shard_map/ppermute | solution.py:228
  30.5 9.5 %collective-permute-start.4 = (bf16[128,256]{1,0:T(8,128)(2,1)S(1)}, bf16[128,256]{1,0:T(8,128)(2,1)S(1)}, u32[]{:S(2)}, u32[]{:S(2)}) collective-permute-start(bf16[128,256]{1,0:T(8,128)(2,1)S(1)} %get-tuple-element.128), channel_id=1, source_target_pairs={{0,127},{1,126},{2,125},{3,124},{4,123},{5,122},{6,121},{7,120},{8... | collective-permute-start | bytes 196616 | tf_op jit(solution)/shard_map/ppermute | solution.py:228
  32.6 7.5 %collective-permute-start.3 = (bf16[128,256]{1,0:T(8,128)(2,1)S(1)}, bf16[128,256]{1,0:T(8,128)(2,1)S(1)}, u32[]{:S(2)}, u32[]{:S(2)}) collective-permute-start(bf16[128,256]{1,0:T(8,128)(2,1)S(1)} %get-tuple-element.128), channel_id=1, source_target_pairs={{0,126},{1,127},{2,124},{3,125},{4,122},{5,123},{6,120},{7,121},{8... | collective-permute-start | bytes 196616 | tf_op jit(solution)/shard_map/ppermute | solution.py:228
  55.9 12.0 %collective-permute-start.10 = (f32[3,128,256]{2,1,0:T(8,128)S(1)}, f32[3,128,256]{2,1,0:T(8,128)S(1)}, u32[]{:S(2)}, u32[]{:S(2)}) collective-permute-start(f32[3,128,256]{2,1,0:T(8,128)S(1)} %get-tuple-element.147), channel_id=1, source_target_pairs={{0,124},{1,125},{2,126},{3,127},{4,120},{5,121},{6,122},{7,123},{8... | collective-permute-start | bytes 1179656 | tf_op jit(solution)/shard_map/ppermute | solution.py:228
  56.0 9.5 %collective-permute-start.9 = (bf16[128,256]{1,0:T(8,128)(2,1)S(1)}, bf16[128,256]{1,0:T(8,128)(2,1)S(1)}, u32[]{:S(2)}, u32[]{:S(2)}) collective-permute-start(bf16[128,256]{1,0:T(8,128)(2,1)S(1)} %get-tuple-element.138), channel_id=1, source_target_pairs={{0,127},{1,126},{2,125},{3,124},{4,123},{5,122},{6,121},{7,120},{8... | collective-permute-start | bytes 196616 | tf_op jit(solution)/shard_map/ppermute | solution.py:228
  59.2 7.3 %collective-permute-start.8 = (bf16[128,256]{1,0:T(8,128)(2,1)S(1)}, bf16[128,256]{1,0:T(8,128)(2,1)S(1)}, u32[]{:S(2)}, u32[]{:S(2)}) collective-permute-start(bf16[128,256]{1,0:T(8,128)(2,1)S(1)} %get-tuple-element.138), channel_id=1, source_target_pairs={{0,126},{1,127},{2,124},{3,125},{4,122},{5,123},{6,120},{7,121},{8... | collective-permute-start | bytes 196616 | tf_op jit(solution)/shard_map/ppermute | solution.py:228
  80.2 12.0 %collective-permute-start.15 = (f32[3,128,256]{2,1,0:T(8,128)S(1)}, f32[3,128,256]{2,1,0:T(8,128)S(1)}, u32[]{:S(2)}, u32[]{:S(2)}) collective-permute-start(f32[3,128,256]{2,1,0:T(8,128)S(1)} %get-tuple-element.161), channel_id=1, source_target_pairs={{0,124},{1,125},{2,126},{3,127},{4,120},{5,121},{6,122},{7,123},{8... | collective-permute-start | bytes 1179656 | tf_op jit(solution)/shard_map/ppermute | solution.py:228
  80.8 9.2 %collective-permute-start.14 = (bf16[128,256]{1,0:T(8,128)(2,1)S(1)}, bf16[128,256]{1,0:T(8,128)(2,1)S(1)}, u32[]{:S(2)}, u32[]{:S(2)}) collective-permute-start(bf16[128,256]{1,0:T(8,128)(2,1)S(1)} %get-tuple-element.152), channel_id=1, source_target_pairs={{0,127},{1,126},{2,125},{3,124},{4,123},{5,122},{6,121},{7,120},{8... | collective-permute-start | bytes 196616 | tf_op jit(solution)/shard_map/ppermute | solution.py:228
  83.4 7.5 %collective-permute-start.13 = (bf16[128,256]{1,0:T(8,128)(2,1)S(1)}, bf16[128,256]{1,0:T(8,128)(2,1)S(1)}, u32[]{:S(2)}, u32[]{:S(2)}) collective-permute-start(bf16[128,256]{1,0:T(8,128)(2,1)S(1)} %get-tuple-element.152), channel_id=1, source_target_pairs={{0,126},{1,127},{2,124},{3,125},{4,122},{5,123},{6,120},{7,121},{8... | collective-permute-start | bytes 196616 | tf_op jit(solution)/shard_map/ppermute | solution.py:228
  104.3 12.0 %collective-permute-start.20 = (f32[3,128,256]{2,1,0:T(8,128)S(1)}, f32[3,128,256]{2,1,0:T(8,128)S(1)}, u32[]{:S(2)}, u32[]{:S(2)}) collective-permute-start(f32[3,128,256]{2,1,0:T(8,128)S(1)} %get-tuple-element.175), channel_id=1, source_target_pairs={{0,124},{1,125},{2,126},{3,127},{4,120},{5,121},{6,122},{7,123},{8... | collective-permute-start | bytes 1179656 | tf_op jit(solution)/shard_map/ppermute | solution.py:228
  104.4 9.5 %collective-permute-start.19 = (bf16[128,256]{1,0:T(8,128)(2,1)S(1)}, bf16[128,256]{1,0:T(8,128)(2,1)S(1)}, u32[]{:S(2)}, u32[]{:S(2)}) collective-permute-start(bf16[128,256]{1,0:T(8,128)(2,1)S(1)} %get-tuple-element.166), channel_id=1, source_target_pairs={{0,127},{1,126},{2,125},{3,124},{4,123},{5,122},{6,121},{7,120},{8... | collective-permute-start | bytes 196616 | tf_op jit(solution)/shard_map/ppermute | solution.py:228
  107.7 7.3 %collective-permute-start.18 = (bf16[128,256]{1,0:T(8,128)(2,1)S(1)}, bf16[128,256]{1,0:T(8,128)(2,1)S(1)}, u32[]{:S(2)}, u32[]{:S(2)}) collective-permute-start(bf16[128,256]{1,0:T(8,128)(2,1)S(1)} %get-tuple-element.166), channel_id=1, source_target_pairs={{0,126},{1,127},{2,124},{3,125},{4,122},{5,123},{6,120},{7,121},{8... | collective-permute-start | bytes 196616 | tf_op jit(solution)/shard_map/ppermute | solution.py:228
  127.6 15.0 %collective-permute-start.25 = (f32[3,128,256]{2,1,0:T(8,128)S(1)}, f32[3,128,256]{2,1,0:T(8,128)S(1)}, u32[]{:S(2)}, u32[]{:S(2)}) collective-permute-start(f32[3,128,256]{2,1,0:T(8,128)S(1)} %get-tuple-element.189), channel_id=1, source_target_pairs={{0,124},{1,125},{2,126},{3,127},{4,120},{5,121},{6,122},{7,123},{8... | collective-permute-start | bytes 1179656 | tf_op jit(solution)/shard_map/ppermute | solution.py:228
  130.0 8.4 %collective-permute-start.24 = (bf16[128,256]{1,0:T(8,128)(2,1)S(1)}, bf16[128,256]{1,0:T(8,128)(2,1)S(1)}, u32[]{:S(2)}, u32[]{:S(2)}) collective-permute-start(bf16[128,256]{1,0:T(8,128)(2,1)S(1)} %get-tuple-element.180), channel_id=1, source_target_pairs={{0,127},{1,126},{2,125},{3,124},{4,123},{5,122},{6,121},{7,120},{8... | collective-permute-start | bytes 196616 | tf_op jit(solution)/shard_map/ppermute | solution.py:228
  133.3 7.3 %collective-permute-start.23 = (bf16[128,256]{1,0:T(8,128)(2,1)S(1)}, bf16[128,256]{1,0:T(8,128)(2,1)S(1)}, u32[]{:S(2)}, u32[]{:S(2)}) collective-permute-start(bf16[128,256]{1,0:T(8,128)(2,1)S(1)} %get-tuple-element.180), channel_id=1, source_target_pairs={{0,126},{1,127},{2,124},{3,125},{4,122},{5,123},{6,120},{7,121},{8... | collective-permute-start | bytes 196616 | tf_op jit(solution)/shard_map/ppermute | solution.py:228
  154.8 12.0 %collective-permute-start.30 = (f32[3,128,256]{2,1,0:T(8,128)S(1)}, f32[3,128,256]{2,1,0:T(8,128)S(1)}, u32[]{:S(2)}, u32[]{:S(2)}) collective-permute-start(f32[3,128,256]{2,1,0:T(8,128)S(1)} %get-tuple-element.203), channel_id=1, source_target_pairs={{0,124},{1,125},{2,126},{3,127},{4,120},{5,121},{6,122},{7,123},{8... | collective-permute-start | bytes 1179656 | tf_op jit(solution)/shard_map/ppermute | solution.py:228
  155.1 9.3 %collective-permute-start.29 = (bf16[128,256]{1,0:T(8,128)(2,1)S(1)}, bf16[128,256]{1,0:T(8,128)(2,1)S(1)}, u32[]{:S(2)}, u32[]{:S(2)}) collective-permute-start(bf16[128,256]{1,0:T(8,128)(2,1)S(1)} %get-tuple-element.194), channel_id=1, source_target_pairs={{0,127},{1,126},{2,125},{3,124},{4,123},{5,122},{6,121},{7,120},{8... | collective-permute-start | bytes 196616 | tf_op jit(solution)/shard_map/ppermute | solution.py:228
  157.6 7.8 %collective-permute-start.28 = (bf16[128,256]{1,0:T(8,128)(2,1)S(1)}, bf16[128,256]{1,0:T(8,128)(2,1)S(1)}, u32[]{:S(2)}, u32[]{:S(2)}) collective-permute-start(bf16[128,256]{1,0:T(8,128)(2,1)S(1)} %get-tuple-element.194), channel_id=1, source_target_pairs={{0,126},{1,127},{2,124},{3,125},{4,122},{5,123},{6,120},{7,121},{8... | collective-permute-start | bytes 196616 | tf_op jit(solution)/shard_map/ppermute | solution.py:228
  158.5 6.9 %collective-permute-start.27 = (bf16[128,256]{1,0:T(8,128)(2,1)S(1)}, bf16[128,256]{1,0:T(8,128)(2,1)S(1)}, u32[]{:S(2)}, u32[]{:S(2)}) collective-permute-start(bf16[128,256]{1,0:T(8,128)(2,1)S(1)} %get-tuple-element.194), channel_id=1, source_target_pairs={{0,125},{1,124},{2,127},{3,126},{4,121},{5,120},{6,123},{7,122},{8... | collective-permute-start | bytes 196616 | tf_op jit(solution)/shard_map/ppermute | solution.py:228
  178.8 12.0 %collective-permute-start.35 = (f32[3,128,256]{2,1,0:T(8,128)S(1)}, f32[3,128,256]{2,1,0:T(8,128)S(1)}, u32[]{:S(2)}, u32[]{:S(2)}) collective-permute-start(f32[3,128,256]{2,1,0:T(8,128)S(1)} %get-tuple-element.218), channel_id=1, source_target_pairs={{0,124},{1,125},{2,126},{3,127},{4,120},{5,121},{6,122},{7,123},{8... | collective-permute-start | bytes 1179656 | tf_op jit(solution)/shard_map/ppermute | solution.py:228
  178.9 9.5 %collective-permute-start.34 = (bf16[128,256]{1,0:T(8,128)(2,1)S(1)}, bf16[128,256]{1,0:T(8,128)(2,1)S(1)}, u32[]{:S(2)}, u32[]{:S(2)}) collective-permute-start(bf16[128,256]{1,0:T(8,128)(2,1)S(1)} %get-tuple-element.208), channel_id=1, source_target_pairs={{0,127},{1,126},{2,125},{3,124},{4,123},{5,122},{6,121},{7,120},{8... | collective-permute-start | bytes 196616 | tf_op jit(solution)/shard_map/ppermute | solution.py:228
  181.8 7.4 %collective-permute-start.33 = (bf16[128,256]{1,0:T(8,128)(2,1)S(1)}, bf16[128,256]{1,0:T(8,128)(2,1)S(1)}, u32[]{:S(2)}, u32[]{:S(2)}) collective-permute-start(bf16[128,256]{1,0:T(8,128)(2,1)S(1)} %get-tuple-element.208), channel_id=1, source_target_pairs={{0,126},{1,127},{2,124},{3,125},{4,122},{5,123},{6,120},{7,121},{8... | collective-permute-start | bytes 196616 | tf_op jit(solution)/shard_map/ppermute | solution.py:228
  (18 other events, 163.8 us)

commit v4 on v3

--- a/solution.py
+++ b/solution.py
@@ -11,6 +11,7 @@
 adam_eps = 1e-08
 EDGE = 128
 OWNERS = 4
+HOPS = (0, 2, 3, 1)
 VMEM = pltpu.VMEM
 F32 = jnp.float32
 BF16 = jnp.bfloat16
@@ -81,12 +82,14 @@
 def item_kernel(stratum, slots, meta, *refs):
     got = refs[:OWNERS]
     users, teacher, parts, residual, items = refs[OWNERS:]
-    shard = got[0].shape[0] // 2
+    shard = items.shape[0] // (2 * OWNERS)
     place = place_of(words(meta, stratum)[1])
-    for hop in range(OWNERS):
+    for hop, piece in zip(HOPS, got):
         start = pl.multiple_of((place ^ hop) * shard, shard)
-        items[pl.ds(start, shard), :] = got[hop][:shard, :]
-        items[pl.ds(start + OWNERS * shard, shard), :] = got[hop][shard:, :]
+        for side in range(2):
+            span = slice(side * shard, (side + 1) * shard)
+            values = piece[span, :] if hop else piece[0, span, :].astype(BF16)
+            items[pl.ds(start + side * OWNERS * shard, shard), :] = values
     slot_grads(stratum, slots, meta, items, users, teacher, residual, parts)
 
 
@@ -277,8 +280,6 @@
                 compiler_params=LIMIT,
                 name="item_grad",
             )(*in_vmem(meta, *got, user_bf, scores))
-        if stratum > 0:
-            parts, state = lax.optimization_barrier((parts, state))
         parts = lax.all_to_all(parts, "rep", 0, 0)
         scratch = [VMEM((user_rows // EDGE, EDGE, rank), F32)]
         if last:
@@ -315,8 +316,9 @@
                 name="owner_adam",
             )(*in_vmem(*[meta] * first, parts, *((own, other) if first else (state,))))
             residual, rounded, state = lax.optimization_barrier((residual, rounded, state))
+            got = [shifted(rounded, hop) if hop else None for hop in HOPS]
             state = shifted(state)
-            got = [shifted(rounded, hop) for hop in reversed(range(OWNERS))][::-1]
+            got[HOPS.index(0)] = state
             *users, user_bf = pl.pallas_call(
                 functools.partial(user_kernel, stratum, slots),
                 in_specs=vmem_specs(1 + 5),

time: 211 us -> 208 us (0.986)
  starting transfers between devices: 61.6 us -> 53.8 us
  waiting for transfers between devices: 30 us -> 33.6 us
    ppermute x36 -> x29, starting transfers between devices: 54.4 us -> 46.5 us  [shifted(): return lax.ppermute(value, ('blk', 'rep'), moves(hop))]
    ppermute x36 -> x29, waiting for transfers between devices: 27.6 us -> 31.2 us  [shifted(): return lax.ppermute(value, ('blk', 'rep'), moves(hop))]
  transfers between devices with their start and end apart: 38 -> 31, of which waited for: 22 -> 21; matrix products, arithmetic and copies ran while one was open for 2% -> 2% of each run, Pallas kernels for 8% -> 6%
where the time goes in v4:
time: 208 us; the launch traced here: 207 us
  blocking collectives  94.7 us (46%)
  starting transfers between devices  53.8 us (26%)
  waiting for transfers between devices  33.6 us (16%)
  Pallas kernels  19.8 us (10%)
  other arithmetic  3.56 us (2%)
    all_to_all x8, blocking collectives, on_device(): parts = lax.all_to_all(parts, 'rep', 0, 0)  94.7 us
    ppermute x29, starting transfers between devices, shifted(): return lax.ppermute(value, ('blk', 'rep'), moves(hop))  46.5 us
    ppermute x29, waiting for transfers between devices, shifted(): return lax.ppermute(value, ('blk', 'rep'), moves(hop))  31.2 us
    pallas_call x7, Pallas kernels, on_device(): pl.pallas_call(functools.partial(user_kernel, stratum, slots), in_specs=v...  8.78 us
    all_to_all x1, starting transfers between devices, on_device(): items = lax.all_to_all(copies, 'rep', 0, 0).reshape(item_rows, rank)  5.03 us
    pallas_call x7, Pallas kernels, on_device(): pl.pallas_call(functools.partial(item_kernel, stratum, slots), in_specs=v...  4.66 us
  transfers between devices with their start and end apart: 31, of which 21 were waited for; matrix products, arithmetic and copies ran while one was open for 2% of the time, Pallas kernels for 6%

profile of v4, /device:TPU:1, one launch (start us, length us, event | category | flops | bytes accessed | tf_op | source)
XLA Modules:
  0.0 207.4 jit_solution(15565812968811807803)
XLA Ops:
  4.7 5.0 %all-to-all-start = ((bf16[8,64,256]{2,1,0:T(8,128)(2,1)}), bf16[8,64,256]{2,1,0:T(8,128)(2,1)S(1)}, u32[]{:S(2)}, u32[]{:S(2)}) async-start(bf16[8,64,256]{2,1,0:T(8,128)(2,1)} %broadcast_in_dim.7), calls=%async_computation | async-start | bytes 524288 | tf_op jit(solution)/shard_map/all_to_all | solution.py:258
  13.4 2.4 %all-to-all-done = bf16[8,64,256]{2,1,0:T(8,128)(2,1)S(1)} async-done(((bf16[8,64,256]{2,1,0:T(8,128)(2,1)}), bf16[8,64,256]{2,1,0:T(8,128)(2,1)S(1)}, u32[]{:S(2)}, u32[]{:S(2)}) %all-to-all-start) | async-done | bytes 262176 | tf_op jit(solution)/shard_map/all_to_all | solution.py:258
  16.6 10.1 %all_to_all.45.parts = bf16[8,128,256]{2,1,0:T(8,128)(2,1)S(1)} all-to-all(bf16[8,128,256]{2,1,0:T(8,128)(2,1)S(1)} %get-tuple-element.109), channel_id=1, replica_groups=mesh['blk'=16,'rep'=8] {'rep'}, dimensions={0} | all-to-all | bytes 1048576 | tf_op jit(solution)/shard_map/all_to_all | solution.py:283
  26.9 3.6 %collective-permute-start.1 = (f32[3,128,256]{2,1,0:T(8,128)S(1)}, f32[3,128,256]{2,1,0:T(8,128)S(1)}, u32[]{:S(2)}, u32[]{:S(2)}) collective-permute-start(f32[3,128,256]{2,1,0:T(8,128)S(1)} %get-tuple-element.114), channel_id=1, source_target_pairs={{0,124},{1,125},{2,126},{3,127},{4,120},{5,121},{6,122},{7,123},{8... | collective-permute-start | bytes 1179656 | tf_op jit(solution)/shard_map/ppermute | solution.py:231
  32.5 5.1 %collective-permute-start.3 = (bf16[128,256]{1,0:T(8,128)(2,1)S(1)}, bf16[128,256]{1,0:T(8,128)(2,1)S(1)}, u32[]{:S(2)}, u32[]{:S(2)}) collective-permute-start(bf16[128,256]{1,0:T(8,128)(2,1)S(1)} %get-tuple-element.115), channel_id=1, source_target_pairs={{0,127},{1,126},{2,125},{3,124},{4,123},{5,122},{6,121},{7,120},{8... | collective-permute-start | bytes 196616 | tf_op jit(solution)/shard_map/ppermute | solution.py:231
  40.2 3.2 %collective-permute-done.4.refs_3_ = bf16[128,256]{1,0:T(8,128)(2,1)S(1)} collective-permute-done((bf16[128,256]{1,0:T(8,128)(2,1)S(1)}, bf16[128,256]{1,0:T(8,128)(2,1)S(1)}, u32[]{:S(2)}, u32[]{:S(2)}) %collective-permute-start.4) | collective-permute-done | bytes 65568 | tf_op jit(solution)/shard_map/ppermute | solution.py:231
  44.1 11.8 %all_to_all.46.parts = bf16[8,128,256]{2,1,0:T(8,128)(2,1)S(1)} all-to-all(bf16[8,128,256]{2,1,0:T(8,128)(2,1)S(1)} %get-tuple-element.119), channel_id=1, replica_groups=mesh['blk'=16,'rep'=8] {'rep'}, dimensions={0} | all-to-all | bytes 1048576 | tf_op jit(solution)/shard_map/all_to_all | solution.py:283
  63.2 2.8 %collective-permute-done.6.refs_1_ = bf16[128,256]{1,0:T(8,128)(2,1)S(1)} collective-permute-done((bf16[128,256]{1,0:T(8,128)(2,1)S(1)}, bf16[128,256]{1,0:T(8,128)(2,1)S(1)}, u32[]{:S(2)}, u32[]{:S(2)}) %collective-permute-start.6) | collective-permute-done | bytes 65568 | tf_op jit(solution)/shard_map/ppermute | solution.py:231
  67.3 12.5 %all_to_all.47.parts = bf16[8,128,256]{2,1,0:T(8,128)(2,1)S(1)} all-to-all(bf16[8,128,256]{2,1,0:T(8,128)(2,1)S(1)} %get-tuple-element.131), channel_id=1, replica_groups=mesh['blk'=16,'rep'=8] {'rep'}, dimensions={0} | all-to-all | bytes 1048576 | tf_op jit(solution)/shard_map/all_to_all | solution.py:283
  80.1 2.6 %collective-permute-start.10 = (bf16[128,256]{1,0:T(8,128)(2,1)S(1)}, bf16[128,256]{1,0:T(8,128)(2,1)S(1)}, u32[]{:S(2)}, u32[]{:S(2)}) collective-permute-start(bf16[128,256]{1,0:T(8,128)(2,1)S(1)} %get-tuple-element.135), channel_id=1, source_target_pairs={{0,126},{1,127},{2,124},{3,125},{4,122},{5,123},{6,120},{7,121},{8... | collective-permute-start | bytes 196616 | tf_op jit(solution)/shard_map/ppermute | solution.py:231
  86.8 3.3 %collective-permute-done.10.refs_1_ = bf16[128,256]{1,0:T(8,128)(2,1)S(1)} collective-permute-done((bf16[128,256]{1,0:T(8,128)(2,1)S(1)}, bf16[128,256]{1,0:T(8,128)(2,1)S(1)}, u32[]{:S(2)}, u32[]{:S(2)}) %collective-permute-start.10) | collective-permute-done | bytes 65568 | tf_op jit(solution)/shard_map/ppermute | solution.py:231
  91.2 12.3 %all_to_all.48.parts = bf16[8,128,256]{2,1,0:T(8,128)(2,1)S(1)} all-to-all(bf16[8,128,256]{2,1,0:T(8,128)(2,1)S(1)} %get-tuple-element.143), channel_id=1, replica_groups=mesh['blk'=16,'rep'=8] {'rep'}, dimensions={0} | all-to-all | bytes 1048576 | tf_op jit(solution)/shard_map/all_to_all | solution.py:283
  103.8 3.1 %collective-permute-start.14 = (bf16[128,256]{1,0:T(8,128)(2,1)S(1)}, bf16[128,256]{1,0:T(8,128)(2,1)S(1)}, u32[]{:S(2)}, u32[]{:S(2)}) collective-permute-start(bf16[128,256]{1,0:T(8,128)(2,1)S(1)} %get-tuple-element.147), channel_id=1, source_target_pairs={{0,126},{1,127},{2,124},{3,125},{4,122},{5,123},{6,120},{7,121},{8... | collective-permute-start | bytes 196616 | tf_op jit(solution)/shard_map/ppermute | solution.py:231
  110.6 3.3 %collective-permute-done.14.refs_1_ = bf16[128,256]{1,0:T(8,128)(2,1)S(1)} collective-permute-done((bf16[128,256]{1,0:T(8,128)(2,1)S(1)}, bf16[128,256]{1,0:T(8,128)(2,1)S(1)}, u32[]{:S(2)}, u32[]{:S(2)}) %collective-permute-start.14) | collective-permute-done | bytes 65568 | tf_op jit(solution)/shard_map/ppermute | solution.py:231
  115.4 11.9 %all_to_all.49.parts = bf16[8,128,256]{2,1,0:T(8,128)(2,1)S(1)} all-to-all(bf16[8,128,256]{2,1,0:T(8,128)(2,1)S(1)} %get-tuple-element.155), channel_id=1, replica_groups=mesh['blk'=16,'rep'=8] {'rep'}, dimensions={0} | all-to-all | bytes 1048576 | tf_op jit(solution)/shard_map/all_to_all | solution.py:283
  127.5 3.6 %collective-permute-start.18 = (bf16[128,256]{1,0:T(8,128)(2,1)S(1)}, bf16[128,256]{1,0:T(8,128)(2,1)S(1)}, u32[]{:S(2)}, u32[]{:S(2)}) collective-permute-start(bf16[128,256]{1,0:T(8,128)(2,1)S(1)} %get-tuple-element.159), channel_id=1, source_target_pairs={{0,126},{1,127},{2,124},{3,125},{4,122},{5,123},{6,120},{7,121},{8... | collective-permute-start | bytes 196616 | tf_op jit(solution)/shard_map/ppermute | solution.py:231
  134.5 2.9 %collective-permute-done.18.refs_1_ = bf16[128,256]{1,0:T(8,128)(2,1)S(1)} collective-permute-done((bf16[128,256]{1,0:T(8,128)(2,1)S(1)}, bf16[128,256]{1,0:T(8,128)(2,1)S(1)}, u32[]{:S(2)}, u32[]{:S(2)}) %collective-permute-start.18) | collective-permute-done | bytes 65568 | tf_op jit(solution)/shard_map/ppermute | solution.py:231
  139.6 11.9 %all_to_all.50.parts = bf16[8,128,256]{2,1,0:T(8,128)(2,1)S(1)} all-to-all(bf16[8,128,256]{2,1,0:T(8,128)(2,1)S(1)} %get-tuple-element.167), channel_id=1, replica_groups=mesh['blk'=16,'rep'=8] {'rep'}, dimensions={0} | all-to-all | bytes 1048576 | tf_op jit(solution)/shard_map/all_to_all | solution.py:283
  151.8 3.6 %collective-permute-start.22 = (bf16[128,256]{1,0:T(8,128)(2,1)S(1)}, bf16[128,256]{1,0:T(8,128)(2,1)S(1)}, u32[]{:S(2)}, u32[]{:S(2)}) collective-permute-start(bf16[128,256]{1,0:T(8,128)(2,1)S(1)} %get-tuple-element.171), channel_id=1, source_target_pairs={{0,126},{1,127},{2,124},{3,125},{4,122},{5,123},{6,120},{7,121},{8... | collective-permute-start | bytes 196616 | tf_op jit(solution)/shard_map/ppermute | solution.py:231
  163.8 11.9 %all_to_all.51.parts = bf16[8,128,256]{2,1,0:T(8,128)(2,1)S(1)} all-to-all(bf16[8,128,256]{2,1,0:T(8,128)(2,1)S(1)} %get-tuple-element.179), channel_id=1, replica_groups=mesh['blk'=16,'rep'=8] {'rep'}, dimensions={0} | all-to-all | bytes 1048576 | tf_op jit(solution)/shard_map/all_to_all | solution.py:283
  176.0 3.6 %collective-permute-start.26 = (bf16[128,256]{1,0:T(8,128)(2,1)S(1)}, bf16[128,256]{1,0:T(8,128)(2,1)S(1)}, u32[]{:S(2)}, u32[]{:S(2)}) collective-permute-start(bf16[128,256]{1,0:T(8,128)(2,1)S(1)} %get-tuple-element.183), channel_id=1, source_target_pairs={{0,126},{1,127},{2,124},{3,125},{4,122},{5,123},{6,120},{7,121},{8... | collective-permute-start | bytes 196616 | tf_op jit(solution)/shard_map/ppermute | solution.py:231
  188.0 12.1 %all_to_all.52.parts = bf16[8,128,256]{2,1,0:T(8,128)(2,1)S(1)} all-to-all(bf16[8,128,256]{2,1,0:T(8,128)(2,1)S(1)} %get-tuple-element.192), channel_id=1, replica_groups=mesh['blk'=16,'rep'=8] {'rep'}, dimensions={0} | all-to-all | bytes 1048576 | tf_op jit(solution)/shard_map/all_to_all | solution.py:283
  200.3 2.7 %last_user_adam.1 = (f32[1024,256]{1,0:T(8,128)}, f32[1024,256]{1,0:T(8,128)}, f32[1024,256]{1,0:T(8,128)}) custom-call(s32[8,2,128]{2,1,0:T(2,128)S(1)} %broadcast_in_dim.8.meta, bf16[512,256]{1,0:T(8,128)(2,1)S(1)} %get-tuple-element.190.items, bf16[8,128,128]{2,1,0:T(8,128)(2,1)S(1)} %get-tuple-element.193.residual, ...), custom_call_target="tpu_custom_call" | custom-call | flops 300000000 | bytes 8000000 | tf_op jit(solution)/shard_map/last_user_adam/pallas_call | solution.py:297
  203.0 3.6 %collective-permute-done.29.state = f32[3,64,256]{2,1,0:T(8,128)S(1)} collective-permute-done((f32[3,64,256]{2,1,0:T(8,128)S(1)}, f32[3,64,256]{2,1,0:T(8,128)S(1)}, u32[]{:S(2)}, u32[]{:S(2)}) %collective-permute-start.29) | collective-permute-done | bytes 196640 | tf_op jit(solution)/shard_map/ppermute | solution.py:231
  (91 shorter events, 57.0 us)
Async XLA Ops:
  1.7 11.6 %collective-permute-start = (f32[3,64,256]{2,1,0:T(8,128)S(1)}, f32[3,64,256]{2,1,0:T(8,128)S(1)}, u32[]{:S(2)}, u32[]{:S(2)}) collective-permute-start(f32[3,64,256]{2,1,0:T(8,128)S(1)} %start.1.own), channel_id=1, source_target_pairs={{0,4},{1,5},{2,6},{3,7},{4,0},{5,1},{6,2},{7,3},{8,12},{9,13},{10,... | collective-permute-start | bytes 589832 | tf_op jit(solution)/shard_map/ppermute | solution.py:256
  4.7 11.2 %all-to-all-start = ((bf16[8,64,256]{2,1,0:T(8,128)(2,1)}), bf16[8,64,256]{2,1,0:T(8,128)(2,1)S(1)}, u32[]{:S(2)}, u32[]{:S(2)}) async-start(bf16[8,64,256]{2,1,0:T(8,128)(2,1)} %broadcast_in_dim.7), calls=%async_computation | async-start | bytes 524288 | tf_op jit(solution)/shard_map/all_to_all | solution.py:258
  26.9 16.6 %collective-permute-start.1 = (f32[3,128,256]{2,1,0:T(8,128)S(1)}, f32[3,128,256]{2,1,0:T(8,128)S(1)}, u32[]{:S(2)}, u32[]{:S(2)}) collective-permute-start(f32[3,128,256]{2,1,0:T(8,128)S(1)} %get-tuple-element.114), channel_id=1, source_target_pairs={{0,124},{1,125},{2,126},{3,127},{4,120},{5,121},{6,122},{7,123},{8... | collective-permute-start | bytes 1179656 | tf_op jit(solution)/shard_map/ppermute | solution.py:231
  30.5 8.6 %collective-permute-start.2 = (bf16[128,256]{1,0:T(8,128)(2,1)S(1)}, bf16[128,256]{1,0:T(8,128)(2,1)S(1)}, u32[]{:S(2)}, u32[]{:S(2)}) collective-permute-start(bf16[128,256]{1,0:T(8,128)(2,1)S(1)} %get-tuple-element.115), channel_id=1, source_target_pairs={{0,126},{1,127},{2,124},{3,125},{4,122},{5,123},{6,120},{7,121},{8... | collective-permute-start | bytes 196616 | tf_op jit(solution)/shard_map/ppermute | solution.py:231
  32.5 7.7 %collective-permute-start.3 = (bf16[128,256]{1,0:T(8,128)(2,1)S(1)}, bf16[128,256]{1,0:T(8,128)(2,1)S(1)}, u32[]{:S(2)}, u32[]{:S(2)}) collective-permute-start(bf16[128,256]{1,0:T(8,128)(2,1)S(1)} %get-tuple-element.115), channel_id=1, source_target_pairs={{0,127},{1,126},{2,125},{3,124},{4,123},{5,122},{6,121},{7,120},{8... | collective-permute-start | bytes 196616 | tf_op jit(solution)/shard_map/ppermute | solution.py:231
  56.1 10.5 %collective-permute-start.5 = (f32[3,128,256]{2,1,0:T(8,128)S(1)}, f32[3,128,256]{2,1,0:T(8,128)S(1)}, u32[]{:S(2)}, u32[]{:S(2)}) collective-permute-start(f32[3,128,256]{2,1,0:T(8,128)S(1)} %get-tuple-element.122), channel_id=1, source_target_pairs={{0,124},{1,125},{2,126},{3,127},{4,120},{5,121},{6,122},{7,123},{8... | collective-permute-start | bytes 1179656 | tf_op jit(solution)/shard_map/ppermute | solution.py:231
  56.2 9.9 %collective-permute-start.6 = (bf16[128,256]{1,0:T(8,128)(2,1)S(1)}, bf16[128,256]{1,0:T(8,128)(2,1)S(1)}, u32[]{:S(2)}, u32[]{:S(2)}) collective-permute-start(bf16[128,256]{1,0:T(8,128)(2,1)S(1)} %get-tuple-element.123), channel_id=1, source_target_pairs={{0,126},{1,127},{2,124},{3,125},{4,122},{5,123},{6,120},{7,121},{8... | collective-permute-start | bytes 196616 | tf_op jit(solution)/shard_map/ppermute | solution.py:231
  58.5 8.1 %collective-permute-start.7 = (bf16[128,256]{1,0:T(8,128)(2,1)S(1)}, bf16[128,256]{1,0:T(8,128)(2,1)S(1)}, u32[]{:S(2)}, u32[]{:S(2)}) collective-permute-start(bf16[128,256]{1,0:T(8,128)(2,1)S(1)} %get-tuple-element.123), channel_id=1, source_target_pairs={{0,127},{1,126},{2,125},{3,124},{4,123},{5,122},{6,121},{7,120},{8... | collective-permute-start | bytes 196616 | tf_op jit(solution)/shard_map/ppermute | solution.py:231
  80.0 10.6 %collective-permute-start.9 = (f32[3,128,256]{2,1,0:T(8,128)S(1)}, f32[3,128,256]{2,1,0:T(8,128)S(1)}, u32[]{:S(2)}, u32[]{:S(2)}) collective-permute-start(f32[3,128,256]{2,1,0:T(8,128)S(1)} %get-tuple-element.134), channel_id=1, source_target_pairs={{0,124},{1,125},{2,126},{3,127},{4,120},{5,121},{6,122},{7,123},{8... | collective-permute-start | bytes 1179656 | tf_op jit(solution)/shard_map/ppermute | solution.py:231
  80.1 10.1 %collective-permute-start.10 = (bf16[128,256]{1,0:T(8,128)(2,1)S(1)}, bf16[128,256]{1,0:T(8,128)(2,1)S(1)}, u32[]{:S(2)}, u32[]{:S(2)}) collective-permute-start(bf16[128,256]{1,0:T(8,128)(2,1)S(1)} %get-tuple-element.135), channel_id=1, source_target_pairs={{0,126},{1,127},{2,124},{3,125},{4,122},{5,123},{6,120},{7,121},{8... | collective-permute-start | bytes 196616 | tf_op jit(solution)/shard_map/ppermute | solution.py:231
  82.7 7.8 %collective-permute-start.11 = (bf16[128,256]{1,0:T(8,128)(2,1)S(1)}, bf16[128,256]{1,0:T(8,128)(2,1)S(1)}, u32[]{:S(2)}, u32[]{:S(2)}) collective-permute-start(bf16[128,256]{1,0:T(8,128)(2,1)S(1)} %get-tuple-element.135), channel_id=1, source_target_pairs={{0,127},{1,126},{2,125},{3,124},{4,123},{5,122},{6,121},{7,120},{8... | collective-permute-start | bytes 196616 | tf_op jit(solution)/shard_map/ppermute | solution.py:231
  103.7 10.9 %collective-permute-start.13 = (f32[3,128,256]{2,1,0:T(8,128)S(1)}, f32[3,128,256]{2,1,0:T(8,128)S(1)}, u32[]{:S(2)}, u32[]{:S(2)}) collective-permute-start(f32[3,128,256]{2,1,0:T(8,128)S(1)} %get-tuple-element.146), channel_id=1, source_target_pairs={{0,124},{1,125},{2,126},{3,127},{4,120},{5,121},{6,122},{7,123},{8... | collective-permute-start | bytes 1179656 | tf_op jit(solution)/shard_map/ppermute | solution.py:231
  103.8 10.1 %collective-permute-start.14 = (bf16[128,256]{1,0:T(8,128)(2,1)S(1)}, bf16[128,256]{1,0:T(8,128)(2,1)S(1)}, u32[]{:S(2)}, u32[]{:S(2)}) collective-permute-start(bf16[128,256]{1,0:T(8,128)(2,1)S(1)} %get-tuple-element.147), channel_id=1, source_target_pairs={{0,126},{1,127},{2,124},{3,125},{4,122},{5,123},{6,120},{7,121},{8... | collective-permute-start | bytes 196616 | tf_op jit(solution)/shard_map/ppermute | solution.py:231
  106.9 7.4 %collective-permute-start.15 = (bf16[128,256]{1,0:T(8,128)(2,1)S(1)}, bf16[128,256]{1,0:T(8,128)(2,1)S(1)}, u32[]{:S(2)}, u32[]{:S(2)}) collective-permute-start(bf16[128,256]{1,0:T(8,128)(2,1)S(1)} %get-tuple-element.147), channel_id=1, source_target_pairs={{0,127},{1,126},{2,125},{3,124},{4,123},{5,122},{6,121},{7,120},{8... | collective-permute-start | bytes 196616 | tf_op jit(solution)/shard_map/ppermute | solution.py:231
  127.5 11.4 %collective-permute-start.17 = (f32[3,128,256]{2,1,0:T(8,128)S(1)}, f32[3,128,256]{2,1,0:T(8,128)S(1)}, u32[]{:S(2)}, u32[]{:S(2)}) collective-permute-start(f32[3,128,256]{2,1,0:T(8,128)S(1)} %get-tuple-element.158), channel_id=1, source_target_pairs={{0,124},{1,125},{2,126},{3,127},{4,120},{5,121},{6,122},{7,123},{8... | collective-permute-start | bytes 1179656 | tf_op jit(solution)/shard_map/ppermute | solution.py:231
  127.5 9.8 %collective-permute-start.18 = (bf16[128,256]{1,0:T(8,128)(2,1)S(1)}, bf16[128,256]{1,0:T(8,128)(2,1)S(1)}, u32[]{:S(2)}, u32[]{:S(2)}) collective-permute-start(bf16[128,256]{1,0:T(8,128)(2,1)S(1)} %get-tuple-element.159), channel_id=1, source_target_pairs={{0,126},{1,127},{2,124},{3,125},{4,122},{5,123},{6,120},{7,121},{8... | collective-permute-start | bytes 196616 | tf_op jit(solution)/shard_map/ppermute | solution.py:231
  131.2 7.0 %collective-permute-start.19 = (bf16[128,256]{1,0:T(8,128)(2,1)S(1)}, bf16[128,256]{1,0:T(8,128)(2,1)S(1)}, u32[]{:S(2)}, u32[]{:S(2)}) collective-permute-start(bf16[128,256]{1,0:T(8,128)(2,1)S(1)} %get-tuple-element.159), channel_id=1, source_target_pairs={{0,127},{1,126},{2,125},{3,124},{4,123},{5,122},{6,121},{7,120},{8... | collective-permute-start | bytes 196616 | tf_op jit(solution)/shard_map/ppermute | solution.py:231
  151.7 11.4 %collective-permute-start.21 = (f32[3,128,256]{2,1,0:T(8,128)S(1)}, f32[3,128,256]{2,1,0:T(8,128)S(1)}, u32[]{:S(2)}, u32[]{:S(2)}) collective-permute-start(f32[3,128,256]{2,1,0:T(8,128)S(1)} %get-tuple-element.170), channel_id=1, source_target_pairs={{0,124},{1,125},{2,126},{3,127},{4,120},{5,121},{6,122},{7,123},{8... | collective-permute-start | bytes 1179656 | tf_op jit(solution)/shard_map/ppermute | solution.py:231
  151.8 9.8 %collective-permute-start.22 = (bf16[128,256]{1,0:T(8,128)(2,1)S(1)}, bf16[128,256]{1,0:T(8,128)(2,1)S(1)}, u32[]{:S(2)}, u32[]{:S(2)}) collective-permute-start(bf16[128,256]{1,0:T(8,128)(2,1)S(1)} %get-tuple-element.171), channel_id=1, source_target_pairs={{0,126},{1,127},{2,124},{3,125},{4,122},{5,123},{6,120},{7,121},{8... | collective-permute-start | bytes 196616 | tf_op jit(solution)/shard_map/ppermute | solution.py:231
  155.4 7.0 %collective-permute-start.23 = (bf16[128,256]{1,0:T(8,128)(2,1)S(1)}, bf16[128,256]{1,0:T(8,128)(2,1)S(1)}, u32[]{:S(2)}, u32[]{:S(2)}) collective-permute-start(bf16[128,256]{1,0:T(8,128)(2,1)S(1)} %get-tuple-element.171), channel_id=1, source_target_pairs={{0,127},{1,126},{2,125},{3,124},{4,123},{5,122},{6,121},{7,120},{8... | collective-permute-start | bytes 196616 | tf_op jit(solution)/shard_map/ppermute | solution.py:231
  175.9 11.5 %collective-permute-start.25 = (f32[3,128,256]{2,1,0:T(8,128)S(1)}, f32[3,128,256]{2,1,0:T(8,128)S(1)}, u32[]{:S(2)}, u32[]{:S(2)}) collective-permute-start(f32[3,128,256]{2,1,0:T(8,128)S(1)} %get-tuple-element.182), channel_id=1, source_target_pairs={{0,124},{1,125},{2,126},{3,127},{4,120},{5,121},{6,122},{7,123},{8... | collective-permute-start | bytes 1179656 | tf_op jit(solution)/shard_map/ppermute | solution.py:231
  176.0 9.8 %collective-permute-start.26 = (bf16[128,256]{1,0:T(8,128)(2,1)S(1)}, bf16[128,256]{1,0:T(8,128)(2,1)S(1)}, u32[]{:S(2)}, u32[]{:S(2)}) collective-permute-start(bf16[128,256]{1,0:T(8,128)(2,1)S(1)} %get-tuple-element.183), channel_id=1, source_target_pairs={{0,126},{1,127},{2,124},{3,125},{4,122},{5,123},{6,120},{7,121},{8... | collective-permute-start | bytes 196616 | tf_op jit(solution)/shard_map/ppermute | solution.py:231
  179.6 7.0 %collective-permute-start.27 = (bf16[128,256]{1,0:T(8,128)(2,1)S(1)}, bf16[128,256]{1,0:T(8,128)(2,1)S(1)}, u32[]{:S(2)}, u32[]{:S(2)}) collective-permute-start(bf16[128,256]{1,0:T(8,128)(2,1)S(1)} %get-tuple-element.183), channel_id=1, source_target_pairs={{0,127},{1,126},{2,125},{3,124},{4,123},{5,122},{6,121},{7,120},{8... | collective-permute-start | bytes 196616 | tf_op jit(solution)/shard_map/ppermute | solution.py:231
  200.2 6.4 %collective-permute-start.29 = (f32[3,64,256]{2,1,0:T(8,128)S(1)}, f32[3,64,256]{2,1,0:T(8,128)S(1)}, u32[]{:S(2)}, u32[]{:S(2)}) collective-permute-start(f32[3,64,256]{2,1,0:T(8,128)S(1)} %owner_adam.15), channel_id=1, source_target_pairs={{0,124},{1,125},{2,126},{3,127},{4,120},{5,121},{6,122},{7,123},{8... | collective-permute-start | bytes 589832 | tf_op jit(solution)/shard_map/ppermute | solution.py:231
  (11 other events, 121.6 us)

commit v5 on v4

--- a/solution.py
+++ b/solution.py
@@ -11,6 +11,7 @@
 adam_eps = 1e-08
 EDGE = 128
 OWNERS = 4
+SUM_HOPS = (2, 3, 1)
 HOPS = (0, 2, 3, 1)
 VMEM = pltpu.VMEM
 F32 = jnp.float32
@@ -52,8 +53,7 @@
     return pl.ds(pl.multiple_of(index * EDGE, EDGE), EDGE)
 
 
-def slot_grads(stratum, slots, meta, items, users, teacher, residual, parts):
-    shard = parts.shape[1] // 2
+def slot_grads(stratum, slots, meta, items, users, teacher, residual, grad):
     rows, rest = words(meta, stratum)
     blocks = [users[block_at(row_of(rows, slot)), :] for slot in range(slots)]
     for slot, user_block in enumerate(blocks):
@@ -67,21 +67,29 @@
         hits = [
             jnp.where(field(rest, 2 * slot, 2) == block, residual[slot], jnp.zeros((), BF16)) for slot in range(slots)
         ]
-        grad = jnp.dot(jnp.concatenate(hits, axis=1), stacked, preferred_element_type=F32).astype(BF16)
-        for piece in range(EDGE // shard):
-            at = block * (EDGE // shard) + piece
-            span = slice(at // OWNERS * shard, (at // OWNERS + 1) * shard)
-            for owner in range(at % OWNERS, parts.shape[0], OWNERS):
-                parts[owner, span, :] = grad[piece * shard : (piece + 1) * shard, :]
-
-
-def first_item_kernel(stratum, slots, meta, items, users, teacher, parts, residual):
-    slot_grads(stratum, slots, meta, items, users, teacher, residual, parts)
+        grad[block * EDGE : (block + 1) * EDGE, :] = jnp.dot(
+            jnp.concatenate(hits, axis=1), stacked, preferred_element_type=F32
+        )
+
+
+def split_parts(place, grad, mine, *sent):
+    shard = mine.shape[0] // 2
+    for hop, part in zip((0, *SUM_HOPS), (mine, *sent)):
+        start = pl.multiple_of((place ^ hop) * shard, shard)
+        for side in range(2):
+            rows = grad[pl.ds(start + side * OWNERS * shard, shard), :]
+            part[side * shard : (side + 1) * shard, :] = rows.astype(part.dtype)
+
+
+def first_item_kernel(stratum, slots, meta, items, users, teacher, *refs):
+    *parts, residual, grad = refs
+    slot_grads(stratum, slots, meta, items, users, teacher, residual, grad)
+    split_parts(place_of(words(meta, stratum)[1]), grad, *parts)
 
 
 def item_kernel(stratum, slots, meta, *refs):
     got = refs[:OWNERS]
-    users, teacher, parts, residual, items = refs[OWNERS:]
+    users, teacher, *parts, residual, items, grad = refs[OWNERS:]
     shard = items.shape[0] // (2 * OWNERS)
     place = place_of(words(meta, stratum)[1])
     for hop, piece in zip(HOPS, got):
@@ -90,7 +98,8 @@
             span = slice(side * shard, (side + 1) * shard)
             values = piece[span, :] if hop else piece[0, span, :].astype(BF16)
             items[pl.ds(start + side * OWNERS * shard, shard), :] = values
-    slot_grads(stratum, slots, meta, items, users, teacher, residual, parts)
+    slot_grads(stratum, slots, meta, items, users, teacher, residual, grad)
+    split_parts(place, grad, *parts)
 
 
 def user_grads(stratum, slots, meta, items, residual, grad):
@@ -130,19 +139,30 @@
     )
 
 
-def owner_kernel(parts, state, state_out, rounded):
-    total = parts[0].astype(F32)
-    for part in range(1, parts.shape[0]):
-        total += parts[part].astype(F32)
+def sum_kernel(*refs):
+    *parts, total = refs
+    acc = parts[0][...]
+    for part in parts[1:]:
+        acc += part[...].astype(F32)
+    total[...] = acc.astype(total.dtype)
+
+
+def owner_kernel(mine, other, state, state_out, rounded):
+    total = mine[...].astype(F32) + other[...].astype(F32)
     new, state_out[1], state_out[2] = adam(state[0], state[1], state[2], total)
     state_out[0] = new
     rounded[...] = new.astype(BF16)
 
 
-def first_owner_kernel(slots, meta, parts, own, other, state_out, rounded):
-    total = parts[0].astype(F32)
-    for part in range(1, parts.shape[0]):
-        total += parts[part].astype(F32)
+def last_owner_kernel(stratum, slots, meta, mine, other, state, state_out):
+    shard = state.shape[1] // 2
+    rows = pl.ds(pl.multiple_of(field(words(meta, stratum)[1], 22, 1) * shard, shard), shard)
+    total = mine[rows, :].astype(F32) + other[rows, :].astype(F32)
+    state_out[0], state_out[1], state_out[2] = adam(state[0, rows, :], state[1, rows, :], state[2, rows, :], total)
+
+
+def first_owner_kernel(slots, meta, mine, other_part, own, other, state_out, rounded):
+    total = mine[...].astype(F32) + other_part[...].astype(F32)
 
     def update(low, high):
         columns = [jnp.concatenate([low[term], high[term]], axis=0) for term in range(3)]
@@ -159,15 +179,6 @@
     @pl.when(side == 1)
     def _():
         update(other, own)
-
-
-def last_owner_kernel(stratum, slots, meta, parts, state, state_out):
-    shard = state.shape[1] // 2
-    rows = pl.ds(pl.multiple_of(field(words(meta, stratum)[1], 22, 1) * shard, shard), shard)
-    total = parts[0, rows, :].astype(F32)
-    for part in range(1, parts.shape[0]):
-        total += parts[part, rows, :].astype(F32)
-    state_out[0], state_out[1], state_out[2] = adam(state[0, rows, :], state[1, rows, :], state[2, rows, :], total)
 
 
 def start_kernel(values, one, two, own, arrived):
@@ -258,39 +269,52 @@
     items = lax.all_to_all(copies, "rep", 0, 0).reshape(item_rows, rank)
     items, own, other, user_bf, meta = lax.optimization_barrier((items, own, other, user_bf, meta))
 
-    parts_shape = VMEM((reps, 2 * shard, rank), BF16)
+    parts_shape = [VMEM((2 * shard, rank), F32)] + [VMEM((2 * shard, rank), BF16)] * (OWNERS - 1)
+    item_scratch = [VMEM((item_rows, rank), F32)]
     residual_shape = VMEM((slots, EDGE, EDGE), BF16)
     for stratum in range(strata):
         last = stratum == strata - 1
         if stratum == 0:
-            parts, residual = pl.pallas_call(
+            *parts, residual = pl.pallas_call(
                 functools.partial(first_item_kernel, stratum, slots),
                 in_specs=vmem_specs(1 + 3),
-                out_specs=vmem_specs(2),
-                out_shape=[parts_shape, residual_shape],
+                out_specs=vmem_specs(OWNERS + 1),
+                out_shape=[*parts_shape, residual_shape],
+                scratch_shapes=item_scratch,
                 compiler_params=LIMIT,
                 name="item_grad",
             )(*in_vmem(meta, items, user_bf, scores))
         else:
-            parts, residual, items = pl.pallas_call(
+            *parts, residual, items = pl.pallas_call(
                 functools.partial(item_kernel, stratum, slots),
                 in_specs=vmem_specs(1 + OWNERS + 2),
-                out_specs=vmem_specs(3),
-                out_shape=[parts_shape, residual_shape, VMEM((item_rows, rank), BF16)],
+                out_specs=vmem_specs(OWNERS + 2),
+                out_shape=[*parts_shape, residual_shape, VMEM((item_rows, rank), BF16)],
+                scratch_shapes=item_scratch,
                 compiler_params=LIMIT,
                 name="item_grad",
             )(*in_vmem(meta, *got, user_bf, scores))
-        parts = lax.all_to_all(parts, "rep", 0, 0)
+        for at, hop in enumerate(SUM_HOPS):
+            parts[at + 1] = lax.ppermute(parts[at + 1], "rep", [(rep, rep ^ hop) for rep in range(reps)])
+        mine = pl.pallas_call(
+            sum_kernel,
+            in_specs=vmem_specs(OWNERS),
+            out_specs=vmem_specs(1)[0],
+            out_shape=VMEM((2 * shard, rank), BF16),
+            compiler_params=LIMIT,
+            name="sum_parts",
+        )(*in_vmem(*parts))
+        partner = lax.ppermute(mine, "rep", [(at, at ^ OWNERS) for at in range(reps)])
         scratch = [VMEM((user_rows // EDGE, EDGE, rank), F32)]
         if last:
             state = pl.pallas_call(
                 functools.partial(last_owner_kernel, stratum, slots),
-                in_specs=vmem_specs(1 + 2),
+                in_specs=vmem_specs(1 + 3),
                 out_specs=vmem_specs(1)[0],
                 out_shape=VMEM((3, shard, rank), F32),
                 compiler_params=LIMIT,
                 name="owner_adam",
-            )(*in_vmem(meta, parts, state))
+            )(*in_vmem(meta, mine, partner, state))
             residual, state = lax.optimization_barrier((residual, state))
             state = shifted(state)
             by_block = pl.BlockSpec((2 * EDGE, rank), lambda at: (at, 0))
@@ -309,12 +333,12 @@
             first = stratum == 0
             state, rounded = pl.pallas_call(
                 functools.partial(first_owner_kernel, slots) if first else owner_kernel,
-                in_specs=vmem_specs(4 if first else 2),
+                in_specs=vmem_specs(5 if first else 3),
                 out_specs=vmem_specs(2),
                 out_shape=[VMEM((3, 2 * shard, rank), F32), VMEM((2 * shard, rank), BF16)],
                 compiler_params=LIMIT,
                 name="owner_adam",
-            )(*in_vmem(*[meta] * first, parts, *((own, other) if first else (state,))))
+            )(*in_vmem(*[meta] * first, mine, partner, *((own, other) if first else (state,))))
             residual, rounded, state = lax.optimization_barrier((residual, rounded, state))
             got = [shifted(rounded, hop) if hop else None for hop in HOPS]
             state = shifted(state)

time: 208 us -> 206 us (level)
  blocking collectives: 94.7 us -> 0 us
  waiting for transfers between devices: 33.6 us -> 87.4 us
  starting transfers between devices: 53.8 us -> 88 us
    all_to_all x8 -> x0, blocking collectives: 94.7 us -> none  [on_device(): parts = lax.all_to_all(parts, 'rep', 0, 0)]
    ppermute x0 -> x32, waiting for transfers between devices: none -> 51.3 us  [the longest x24 27.4 us: on_device(): lax.ppermute(parts[at + 1], 'rep', [(rep, rep ^ hop) for rep in range(rep...]
    ppermute x0 -> x32, starting transfers between devices: none -> 27.9 us  [the longest x24 25.6 us: on_device(): lax.ppermute(parts[at + 1], 'rep', [(rep, rep ^ hop) for rep in range(rep...]
    ppermute x29, starting transfers between devices: 46.5 us -> 52.8 us  [shifted(): return lax.ppermute(value, ('blk', 'rep'), moves(hop))]
    ppermute x29, waiting for transfers between devices: 31.2 us -> 34.5 us  [shifted(): return lax.ppermute(value, ('blk', 'rep'), moves(hop))]
  transfers between devices with their start and end apart: 31 -> 63, of which waited for: 21 -> 49; matrix products, arithmetic and copies ran while one was open for 2% -> 3% of each run, Pallas kernels for 6% -> 6%
where the time goes in v5:
time: 206 us; the launch traced here: 205 us
  starting transfers between devices  88 us (43%)
  waiting for transfers between devices  87.4 us (42%)
  Pallas kernels  21.5 us (10%)
  other arithmetic  4.36 us (2%)
  local copies, waits for them, and re-layouts  2.82 us (1%)
    ppermute x29, starting transfers between devices, shifted(): return lax.ppermute(value, ('blk', 'rep'), moves(hop))  52.8 us
    ppermute x29, waiting for transfers between devices, shifted(): return lax.ppermute(value, ('blk', 'rep'), moves(hop))  34.5 us
    ppermute x24, waiting for transfers between devices, on_device(): lax.ppermute(parts[at + 1], 'rep', [(rep, rep ^ hop) for rep in range(rep...  27.4 us
    ppermute x24, starting transfers between devices, on_device(): lax.ppermute(parts[at + 1], 'rep', [(rep, rep ^ hop) for rep in range(rep...  25.6 us
    ppermute x8, waiting for transfers between devices, on_device(): lax.ppermute(mine, 'rep', [(at, at ^ OWNERS) for at in range(reps)])  23.9 us
    pallas_call x7, Pallas kernels, on_device(): pl.pallas_call(functools.partial(user_kernel, stratum, slots), in_specs=v...  8.76 us
    all_to_all x1, starting transfers between devices, on_device(): items = lax.all_to_all(copies, 'rep', 0, 0).reshape(item_rows, rank)  5.03 us
    pallas_call x7, Pallas kernels, on_device(): pl.pallas_call(functools.partial(item_kernel, stratum, slots), in_specs=v...  4.76 us
  transfers between devices with their start and end apart: 63, of which 49 were waited for; matrix products, arithmetic and copies ran while one was open for 3% of the time, Pallas kernels for 6%

profile of v5, /device:TPU:1, one launch (start us, length us, event | category | flops | bytes accessed | tf_op | source)
XLA Modules:
  0.0 205.2 jit_solution(12944280044639742439)
XLA Ops:
  6.2 5.0 %all-to-all-start = ((bf16[8,64,256]{2,1,0:T(8,128)(2,1)}), bf16[8,64,256]{2,1,0:T(8,128)(2,1)S(1)}, u32[]{:S(2)}, u32[]{:S(2)}) async-start(bf16[8,64,256]{2,1,0:T(8,128)(2,1)} %broadcast_in_dim.7), calls=%async_computation | async-start | bytes 524288 | tf_op jit(solution)/shard_map/all_to_all | solution.py:269
  29.9 4.5 %collective-permute-start.5 = (f32[3,128,256]{2,1,0:T(8,128)S(1)}, f32[3,128,256]{2,1,0:T(8,128)S(1)}, u32[]{:S(2)}, u32[]{:S(2)}) collective-permute-start(f32[3,128,256]{2,1,0:T(8,128)S(1)} %get-tuple-element.141), channel_id=1, source_target_pairs={{0,124},{1,125},{2,126},{3,127},{4,120},{5,121},{6,122},{7,123},{8... | collective-permute-start | bytes 1179656 | tf_op jit(solution)/shard_map/ppermute | solution.py:242
  35.9 5.4 %collective-permute-start.7 = (bf16[128,256]{1,0:T(8,128)(2,1)S(1)}, bf16[128,256]{1,0:T(8,128)(2,1)S(1)}, u32[]{:S(2)}, u32[]{:S(2)}) collective-permute-start(bf16[128,256]{1,0:T(8,128)(2,1)S(1)} %get-tuple-element.142), channel_id=1, source_target_pairs={{0,127},{1,126},{2,125},{3,124},{4,123},{5,122},{6,121},{7,120},{8... | collective-permute-start | bytes 196616 | tf_op jit(solution)/shard_map/ppermute | solution.py:242
  49.1 2.6 %collective-permute-start.9 = (bf16[128,256]{1,0:T(8,128)(2,1)S(1)}, bf16[128,256]{1,0:T(8,128)(2,1)S(1)}, u32[]{:S(2)}, u32[]{:S(2)}) collective-permute-start(bf16[128,256]{1,0:T(8,128)(2,1)S(1)} %get-tuple-element.147), channel_id=1, source_target_pairs={{0,2},{1,3},{2,0},{3,1},{4,6},{5,7},{6,4},{7,5},{8,10},{9,11},{10,... | collective-permute-start | bytes 196616 | tf_op jit(solution)/shard_map/ppermute | solution.py:298
  55.0 3.6 %collective-permute-done.12.other = bf16[128,256]{1,0:T(8,128)(2,1)S(1)} collective-permute-done((bf16[128,256]{1,0:T(8,128)(2,1)S(1)}, bf16[128,256]{1,0:T(8,128)(2,1)S(1)}, u32[]{:S(2)}, u32[]{:S(2)}) %collective-permute-start.12) | collective-permute-done | bytes 65568 | tf_op jit(solution)/shard_map/ppermute | solution.py:307
  59.5 3.3 %collective-permute-start.14 = (bf16[128,256]{1,0:T(8,128)(2,1)S(1)}, bf16[128,256]{1,0:T(8,128)(2,1)S(1)}, u32[]{:S(2)}, u32[]{:S(2)}) collective-permute-start(bf16[128,256]{1,0:T(8,128)(2,1)S(1)} %get-tuple-element.153), channel_id=1, source_target_pairs={{0,126},{1,127},{2,124},{3,125},{4,122},{5,123},{6,120},{7,121},{8... | collective-permute-start | bytes 196616 | tf_op jit(solution)/shard_map/ppermute | solution.py:242
  65.9 3.4 %collective-permute-done.14.refs_1_ = bf16[128,256]{1,0:T(8,128)(2,1)S(1)} collective-permute-done((bf16[128,256]{1,0:T(8,128)(2,1)S(1)}, bf16[128,256]{1,0:T(8,128)(2,1)S(1)}, u32[]{:S(2)}, u32[]{:S(2)}) %collective-permute-start.14) | collective-permute-done | bytes 65568 | tf_op jit(solution)/shard_map/ppermute | solution.py:242
  77.5 3.1 %collective-permute-done.20.other = bf16[128,256]{1,0:T(8,128)(2,1)S(1)} collective-permute-done((bf16[128,256]{1,0:T(8,128)(2,1)S(1)}, bf16[128,256]{1,0:T(8,128)(2,1)S(1)}, u32[]{:S(2)}, u32[]{:S(2)}) %collective-permute-start.20) | collective-permute-done | bytes 65568 | tf_op jit(solution)/shard_map/ppermute | solution.py:307
  82.3 2.9 %collective-permute-start.22 = (bf16[128,256]{1,0:T(8,128)(2,1)S(1)}, bf16[128,256]{1,0:T(8,128)(2,1)S(1)}, u32[]{:S(2)}, u32[]{:S(2)}) collective-permute-start(bf16[128,256]{1,0:T(8,128)(2,1)S(1)} %get-tuple-element.168), channel_id=1, source_target_pairs={{0,126},{1,127},{2,124},{3,125},{4,122},{5,123},{6,120},{7,121},{8... | collective-permute-start | bytes 196616 | tf_op jit(solution)/shard_map/ppermute | solution.py:242
  87.8 3.3 %collective-permute-done.22.refs_1_ = bf16[128,256]{1,0:T(8,128)(2,1)S(1)} collective-permute-done((bf16[128,256]{1,0:T(8,128)(2,1)S(1)}, bf16[128,256]{1,0:T(8,128)(2,1)S(1)}, u32[]{:S(2)}, u32[]{:S(2)}) %collective-permute-start.22) | collective-permute-done | bytes 65568 | tf_op jit(solution)/shard_map/ppermute | solution.py:242
  100.0 3.1 %collective-permute-done.28.other = bf16[128,256]{1,0:T(8,128)(2,1)S(1)} collective-permute-done((bf16[128,256]{1,0:T(8,128)(2,1)S(1)}, bf16[128,256]{1,0:T(8,128)(2,1)S(1)}, u32[]{:S(2)}, u32[]{:S(2)}) %collective-permute-start.28) | collective-permute-done | bytes 65568 | tf_op jit(solution)/shard_map/ppermute | solution.py:307
  104.8 4.3 %collective-permute-start.30 = (bf16[128,256]{1,0:T(8,128)(2,1)S(1)}, bf16[128,256]{1,0:T(8,128)(2,1)S(1)}, u32[]{:S(2)}, u32[]{:S(2)}) collective-permute-start(bf16[128,256]{1,0:T(8,128)(2,1)S(1)} %get-tuple-element.183), channel_id=1, source_target_pairs={{0,126},{1,127},{2,124},{3,125},{4,122},{5,123},{6,120},{7,121},{8... | collective-permute-start | bytes 196616 | tf_op jit(solution)/shard_map/ppermute | solution.py:242
  113.6 2.5 %collective-permute-done.31.refs_2_ = bf16[128,256]{1,0:T(8,128)(2,1)S(1)} collective-permute-done((bf16[128,256]{1,0:T(8,128)(2,1)S(1)}, bf16[128,256]{1,0:T(8,128)(2,1)S(1)}, u32[]{:S(2)}, u32[]{:S(2)}) %collective-permute-start.31) | collective-permute-done | bytes 65568 | tf_op jit(solution)/shard_map/ppermute | solution.py:242
  123.5 3.1 %collective-permute-done.36.other = bf16[128,256]{1,0:T(8,128)(2,1)S(1)} collective-permute-done((bf16[128,256]{1,0:T(8,128)(2,1)S(1)}, bf16[128,256]{1,0:T(8,128)(2,1)S(1)}, u32[]{:S(2)}, u32[]{:S(2)}) %collective-permute-start.36) | collective-permute-done | bytes 65568 | tf_op jit(solution)/shard_map/ppermute | solution.py:307
  128.3 4.3 %collective-permute-start.38 = (bf16[128,256]{1,0:T(8,128)(2,1)S(1)}, bf16[128,256]{1,0:T(8,128)(2,1)S(1)}, u32[]{:S(2)}, u32[]{:S(2)}) collective-permute-start(bf16[128,256]{1,0:T(8,128)(2,1)S(1)} %get-tuple-element.198), channel_id=1, source_target_pairs={{0,126},{1,127},{2,124},{3,125},{4,122},{5,123},{6,120},{7,121},{8... | collective-permute-start | bytes 196616 | tf_op jit(solution)/shard_map/ppermute | solution.py:242
  134.9 2.5 %collective-permute-done.38.refs_1_ = bf16[128,256]{1,0:T(8,128)(2,1)S(1)} collective-permute-done((bf16[128,256]{1,0:T(8,128)(2,1)S(1)}, bf16[128,256]{1,0:T(8,128)(2,1)S(1)}, u32[]{:S(2)}, u32[]{:S(2)}) %collective-permute-start.38) | collective-permute-done | bytes 65568 | tf_op jit(solution)/shard_map/ppermute | solution.py:242
  147.1 3.1 %collective-permute-done.44.other = bf16[128,256]{1,0:T(8,128)(2,1)S(1)} collective-permute-done((bf16[128,256]{1,0:T(8,128)(2,1)S(1)}, bf16[128,256]{1,0:T(8,128)(2,1)S(1)}, u32[]{:S(2)}, u32[]{:S(2)}) %collective-permute-start.44) | collective-permute-done | bytes 65568 | tf_op jit(solution)/shard_map/ppermute | solution.py:307
  152.0 4.3 %collective-permute-start.46 = (bf16[128,256]{1,0:T(8,128)(2,1)S(1)}, bf16[128,256]{1,0:T(8,128)(2,1)S(1)}, u32[]{:S(2)}, u32[]{:S(2)}) collective-permute-start(bf16[128,256]{1,0:T(8,128)(2,1)S(1)} %get-tuple-element.213), channel_id=1, source_target_pairs={{0,126},{1,127},{2,124},{3,125},{4,122},{5,123},{6,120},{7,121},{8... | collective-permute-start | bytes 196616 | tf_op jit(solution)/shard_map/ppermute | solution.py:242
  158.5 2.5 %collective-permute-done.46.refs_1_ = bf16[128,256]{1,0:T(8,128)(2,1)S(1)} collective-permute-done((bf16[128,256]{1,0:T(8,128)(2,1)S(1)}, bf16[128,256]{1,0:T(8,128)(2,1)S(1)}, u32[]{:S(2)}, u32[]{:S(2)}) %collective-permute-start.46) | collective-permute-done | bytes 65568 | tf_op jit(solution)/shard_map/ppermute | solution.py:242
  170.8 3.1 %collective-permute-done.52.other = bf16[128,256]{1,0:T(8,128)(2,1)S(1)} collective-permute-done((bf16[128,256]{1,0:T(8,128)(2,1)S(1)}, bf16[128,256]{1,0:T(8,128)(2,1)S(1)}, u32[]{:S(2)}, u32[]{:S(2)}) %collective-permute-start.52) | collective-permute-done | bytes 65568 | tf_op jit(solution)/shard_map/ppermute | solution.py:307
  175.6 4.3 %collective-permute-start.54 = (bf16[128,256]{1,0:T(8,128)(2,1)S(1)}, bf16[128,256]{1,0:T(8,128)(2,1)S(1)}, u32[]{:S(2)}, u32[]{:S(2)}) collective-permute-start(bf16[128,256]{1,0:T(8,128)(2,1)S(1)} %get-tuple-element.228), channel_id=1, source_target_pairs={{0,126},{1,127},{2,124},{3,125},{4,122},{5,123},{6,120},{7,121},{8... | collective-permute-start | bytes 196616 | tf_op jit(solution)/shard_map/ppermute | solution.py:242
  182.2 2.5 %collective-permute-done.54.refs_1_ = bf16[128,256]{1,0:T(8,128)(2,1)S(1)} collective-permute-done((bf16[128,256]{1,0:T(8,128)(2,1)S(1)}, bf16[128,256]{1,0:T(8,128)(2,1)S(1)}, u32[]{:S(2)}, u32[]{:S(2)}) %collective-permute-start.54) | collective-permute-done | bytes 65568 | tf_op jit(solution)/shard_map/ppermute | solution.py:242
  194.4 3.1 %collective-permute-done.60.other = bf16[128,256]{1,0:T(8,128)(2,1)S(1)} collective-permute-done((bf16[128,256]{1,0:T(8,128)(2,1)S(1)}, bf16[128,256]{1,0:T(8,128)(2,1)S(1)}, u32[]{:S(2)}, u32[]{:S(2)}) %collective-permute-start.60) | collective-permute-done | bytes 65568 | tf_op jit(solution)/shard_map/ppermute | solution.py:307
  199.2 2.7 %last_user_adam.1 = (f32[1024,256]{1,0:T(8,128)}, f32[1024,256]{1,0:T(8,128)}, f32[1024,256]{1,0:T(8,128)}) custom-call(s32[8,2,128]{2,1,0:T(2,128)S(1)} %broadcast_in_dim.8.meta, bf16[512,256]{1,0:T(8,128)(2,1)S(1)} %get-tuple-element.235.items, bf16[8,128,128]{2,1,0:T(8,128)(2,1)S(1)} %get-tuple-element.241.residual, ...), custom_call_target="tpu_custom_call" | custom-call | flops 300000000 | bytes 8000000 | tf_op jit(solution)/shard_map/last_user_adam/pallas_call | solution.py:321
  (157 shorter events, 121.5 us)
Async XLA Ops:
  2.4 13.3 %collective-permute-start = (f32[3,64,256]{2,1,0:T(8,128)}, f32[3,64,256]{2,1,0:T(8,128)}, u32[]{:S(2)}, u32[]{:S(2)}) collective-permute-start(f32[3,64,256]{2,1,0:T(8,128)} %start.1.own), channel_id=1, source_target_pairs={{0,4},{1,5},{2,6},{3,7},{4,0},{5,1},{6,2},{7,3},{8,12},{9,13},{10,... | collective-permute-start | bytes 589832 | tf_op jit(solution)/shard_map/ppermute | solution.py:267
  6.2 11.2 %all-to-all-start = ((bf16[8,64,256]{2,1,0:T(8,128)(2,1)}), bf16[8,64,256]{2,1,0:T(8,128)(2,1)S(1)}, u32[]{:S(2)}, u32[]{:S(2)}) async-start(bf16[8,64,256]{2,1,0:T(8,128)(2,1)} %broadcast_in_dim.7), calls=%async_computation | async-start | bytes 524288 | tf_op jit(solution)/shard_map/all_to_all | solution.py:269
  29.9 17.2 %collective-permute-start.5 = (f32[3,128,256]{2,1,0:T(8,128)S(1)}, f32[3,128,256]{2,1,0:T(8,128)S(1)}, u32[]{:S(2)}, u32[]{:S(2)}) collective-permute-start(f32[3,128,256]{2,1,0:T(8,128)S(1)} %get-tuple-element.141), channel_id=1, source_target_pairs={{0,124},{1,125},{2,126},{3,127},{4,120},{5,121},{6,122},{7,123},{8... | collective-permute-start | bytes 1179656 | tf_op jit(solution)/shard_map/ppermute | solution.py:242
  34.4 9.0 %collective-permute-start.6 = (bf16[128,256]{1,0:T(8,128)(2,1)S(1)}, bf16[128,256]{1,0:T(8,128)(2,1)S(1)}, u32[]{:S(2)}, u32[]{:S(2)}) collective-permute-start(bf16[128,256]{1,0:T(8,128)(2,1)S(1)} %get-tuple-element.142), channel_id=1, source_target_pairs={{0,126},{1,127},{2,124},{3,125},{4,122},{5,123},{6,120},{7,121},{8... | collective-permute-start | bytes 196616 | tf_op jit(solution)/shard_map/ppermute | solution.py:242
  35.9 8.8 %collective-permute-start.7 = (bf16[128,256]{1,0:T(8,128)(2,1)S(1)}, bf16[128,256]{1,0:T(8,128)(2,1)S(1)}, u32[]{:S(2)}, u32[]{:S(2)}) collective-permute-start(bf16[128,256]{1,0:T(8,128)(2,1)S(1)} %get-tuple-element.142), channel_id=1, source_target_pairs={{0,127},{1,126},{2,125},{3,124},{4,123},{5,122},{6,121},{7,120},{8... | collective-permute-start | bytes 196616 | tf_op jit(solution)/shard_map/ppermute | solution.py:242
  58.7 11.5 %collective-permute-start.13 = (f32[3,128,256]{2,1,0:T(8,128)S(1)}, f32[3,128,256]{2,1,0:T(8,128)S(1)}, u32[]{:S(2)}, u32[]{:S(2)}) collective-permute-start(f32[3,128,256]{2,1,0:T(8,128)S(1)} %get-tuple-element.152), channel_id=1, source_target_pairs={{0,124},{1,125},{2,126},{3,127},{4,120},{5,121},{6,122},{7,123},{8... | collective-permute-start | bytes 1179656 | tf_op jit(solution)/shard_map/ppermute | solution.py:242
  59.5 9.8 %collective-permute-start.14 = (bf16[128,256]{1,0:T(8,128)(2,1)S(1)}, bf16[128,256]{1,0:T(8,128)(2,1)S(1)}, u32[]{:S(2)}, u32[]{:S(2)}) collective-permute-start(bf16[128,256]{1,0:T(8,128)(2,1)S(1)} %get-tuple-element.153), channel_id=1, source_target_pairs={{0,126},{1,127},{2,124},{3,125},{4,122},{5,123},{6,120},{7,121},{8... | collective-permute-start | bytes 196616 | tf_op jit(solution)/shard_map/ppermute | solution.py:242
  62.8 7.1 %collective-permute-start.15 = (bf16[128,256]{1,0:T(8,128)(2,1)S(1)}, bf16[128,256]{1,0:T(8,128)(2,1)S(1)}, u32[]{:S(2)}, u32[]{:S(2)}) collective-permute-start(bf16[128,256]{1,0:T(8,128)(2,1)S(1)} %get-tuple-element.153), channel_id=1, source_target_pairs={{0,127},{1,126},{2,125},{3,124},{4,123},{5,122},{6,121},{7,120},{8... | collective-permute-start | bytes 196616 | tf_op jit(solution)/shard_map/ppermute | solution.py:242
  80.7 11.6 %collective-permute-start.21 = (f32[3,128,256]{2,1,0:T(8,128)S(1)}, f32[3,128,256]{2,1,0:T(8,128)S(1)}, u32[]{:S(2)}, u32[]{:S(2)}) collective-permute-start(f32[3,128,256]{2,1,0:T(8,128)S(1)} %get-tuple-element.167), channel_id=1, source_target_pairs={{0,124},{1,125},{2,126},{3,127},{4,120},{5,121},{6,122},{7,123},{8... | collective-permute-start | bytes 1179656 | tf_op jit(solution)/shard_map/ppermute | solution.py:242
  82.3 8.7 %collective-permute-start.22 = (bf16[128,256]{1,0:T(8,128)(2,1)S(1)}, bf16[128,256]{1,0:T(8,128)(2,1)S(1)}, u32[]{:S(2)}, u32[]{:S(2)}) collective-permute-start(bf16[128,256]{1,0:T(8,128)(2,1)S(1)} %get-tuple-element.168), channel_id=1, source_target_pairs={{0,126},{1,127},{2,124},{3,125},{4,122},{5,123},{6,120},{7,121},{8... | collective-permute-start | bytes 196616 | tf_op jit(solution)/shard_map/ppermute | solution.py:242
  85.2 7.0 %collective-permute-start.23 = (bf16[128,256]{1,0:T(8,128)(2,1)S(1)}, bf16[128,256]{1,0:T(8,128)(2,1)S(1)}, u32[]{:S(2)}, u32[]{:S(2)}) collective-permute-start(bf16[128,256]{1,0:T(8,128)(2,1)S(1)} %get-tuple-element.168), channel_id=1, source_target_pairs={{0,127},{1,126},{2,125},{3,124},{4,123},{5,122},{6,121},{7,120},{8... | collective-permute-start | bytes 196616 | tf_op jit(solution)/shard_map/ppermute | solution.py:242
  103.2 12.9 %collective-permute-start.29 = (f32[3,128,256]{2,1,0:T(8,128)S(1)}, f32[3,128,256]{2,1,0:T(8,128)S(1)}, u32[]{:S(2)}, u32[]{:S(2)}) collective-permute-start(f32[3,128,256]{2,1,0:T(8,128)S(1)} %get-tuple-element.182), channel_id=1, source_target_pairs={{0,124},{1,125},{2,126},{3,127},{4,120},{5,121},{6,122},{7,123},{8... | collective-permute-start | bytes 1179656 | tf_op jit(solution)/shard_map/ppermute | solution.py:242
  104.8 8.8 %collective-permute-start.30 = (bf16[128,256]{1,0:T(8,128)(2,1)S(1)}, bf16[128,256]{1,0:T(8,128)(2,1)S(1)}, u32[]{:S(2)}, u32[]{:S(2)}) collective-permute-start(bf16[128,256]{1,0:T(8,128)(2,1)S(1)} %get-tuple-element.183), channel_id=1, source_target_pairs={{0,126},{1,127},{2,124},{3,125},{4,122},{5,123},{6,120},{7,121},{8... | collective-permute-start | bytes 196616 | tf_op jit(solution)/shard_map/ppermute | solution.py:242
  109.1 7.0 %collective-permute-start.31 = (bf16[128,256]{1,0:T(8,128)(2,1)S(1)}, bf16[128,256]{1,0:T(8,128)(2,1)S(1)}, u32[]{:S(2)}, u32[]{:S(2)}) collective-permute-start(bf16[128,256]{1,0:T(8,128)(2,1)S(1)} %get-tuple-element.183), channel_id=1, source_target_pairs={{0,127},{1,126},{2,125},{3,124},{4,123},{5,122},{6,121},{7,120},{8... | collective-permute-start | bytes 196616 | tf_op jit(solution)/shard_map/ppermute | solution.py:242
  126.7 13.0 %collective-permute-start.37 = (f32[3,128,256]{2,1,0:T(8,128)S(1)}, f32[3,128,256]{2,1,0:T(8,128)S(1)}, u32[]{:S(2)}, u32[]{:S(2)}) collective-permute-start(f32[3,128,256]{2,1,0:T(8,128)S(1)} %get-tuple-element.197), channel_id=1, source_target_pairs={{0,124},{1,125},{2,126},{3,127},{4,120},{5,121},{6,122},{7,123},{8... | collective-permute-start | bytes 1179656 | tf_op jit(solution)/shard_map/ppermute | solution.py:242
  128.3 9.1 %collective-permute-start.38 = (bf16[128,256]{1,0:T(8,128)(2,1)S(1)}, bf16[128,256]{1,0:T(8,128)(2,1)S(1)}, u32[]{:S(2)}, u32[]{:S(2)}) collective-permute-start(bf16[128,256]{1,0:T(8,128)(2,1)S(1)} %get-tuple-element.198), channel_id=1, source_target_pairs={{0,126},{1,127},{2,124},{3,125},{4,122},{5,123},{6,120},{7,121},{8... | collective-permute-start | bytes 196616 | tf_op jit(solution)/shard_map/ppermute | solution.py:242
  132.7 7.0 %collective-permute-start.39 = (bf16[128,256]{1,0:T(8,128)(2,1)S(1)}, bf16[128,256]{1,0:T(8,128)(2,1)S(1)}, u32[]{:S(2)}, u32[]{:S(2)}) collective-permute-start(bf16[128,256]{1,0:T(8,128)(2,1)S(1)} %get-tuple-element.198), channel_id=1, source_target_pairs={{0,127},{1,126},{2,125},{3,124},{4,123},{5,122},{6,121},{7,120},{8... | collective-permute-start | bytes 196616 | tf_op jit(solution)/shard_map/ppermute | solution.py:242
  150.3 12.9 %collective-permute-start.45 = (f32[3,128,256]{2,1,0:T(8,128)S(1)}, f32[3,128,256]{2,1,0:T(8,128)S(1)}, u32[]{:S(2)}, u32[]{:S(2)}) collective-permute-start(f32[3,128,256]{2,1,0:T(8,128)S(1)} %get-tuple-element.212), channel_id=1, source_target_pairs={{0,124},{1,125},{2,126},{3,127},{4,120},{5,121},{6,122},{7,123},{8... | collective-permute-start | bytes 1179656 | tf_op jit(solution)/shard_map/ppermute | solution.py:242
  152.0 9.1 %collective-permute-start.46 = (bf16[128,256]{1,0:T(8,128)(2,1)S(1)}, bf16[128,256]{1,0:T(8,128)(2,1)S(1)}, u32[]{:S(2)}, u32[]{:S(2)}) collective-permute-start(bf16[128,256]{1,0:T(8,128)(2,1)S(1)} %get-tuple-element.213), channel_id=1, source_target_pairs={{0,126},{1,127},{2,124},{3,125},{4,122},{5,123},{6,120},{7,121},{8... | collective-permute-start | bytes 196616 | tf_op jit(solution)/shard_map/ppermute | solution.py:242
  156.3 7.0 %collective-permute-start.47 = (bf16[128,256]{1,0:T(8,128)(2,1)S(1)}, bf16[128,256]{1,0:T(8,128)(2,1)S(1)}, u32[]{:S(2)}, u32[]{:S(2)}) collective-permute-start(bf16[128,256]{1,0:T(8,128)(2,1)S(1)} %get-tuple-element.213), channel_id=1, source_target_pairs={{0,127},{1,126},{2,125},{3,124},{4,123},{5,122},{6,121},{7,120},{8... | collective-permute-start | bytes 196616 | tf_op jit(solution)/shard_map/ppermute | solution.py:242
  174.0 12.9 %collective-permute-start.53 = (f32[3,128,256]{2,1,0:T(8,128)S(1)}, f32[3,128,256]{2,1,0:T(8,128)S(1)}, u32[]{:S(2)}, u32[]{:S(2)}) collective-permute-start(f32[3,128,256]{2,1,0:T(8,128)S(1)} %get-tuple-element.227), channel_id=1, source_target_pairs={{0,124},{1,125},{2,126},{3,127},{4,120},{5,121},{6,122},{7,123},{8... | collective-permute-start | bytes 1179656 | tf_op jit(solution)/shard_map/ppermute | solution.py:242
  175.6 9.0 %collective-permute-start.54 = (bf16[128,256]{1,0:T(8,128)(2,1)S(1)}, bf16[128,256]{1,0:T(8,128)(2,1)S(1)}, u32[]{:S(2)}, u32[]{:S(2)}) collective-permute-start(bf16[128,256]{1,0:T(8,128)(2,1)S(1)} %get-tuple-element.228), channel_id=1, source_target_pairs={{0,126},{1,127},{2,124},{3,125},{4,122},{5,123},{6,120},{7,121},{8... | collective-permute-start | bytes 196616 | tf_op jit(solution)/shard_map/ppermute | solution.py:242
  179.9 7.0 %collective-permute-start.55 = (bf16[128,256]{1,0:T(8,128)(2,1)S(1)}, bf16[128,256]{1,0:T(8,128)(2,1)S(1)}, u32[]{:S(2)}, u32[]{:S(2)}) collective-permute-start(bf16[128,256]{1,0:T(8,128)(2,1)S(1)} %get-tuple-element.228), channel_id=1, source_target_pairs={{0,127},{1,126},{2,125},{3,124},{4,123},{5,122},{6,121},{7,120},{8... | collective-permute-start | bytes 196616 | tf_op jit(solution)/shard_map/ppermute | solution.py:242
  197.6 6.7 %collective-permute-start.61 = (f32[3,64,256]{2,1,0:T(8,128)S(1)}, f32[3,64,256]{2,1,0:T(8,128)S(1)}, u32[]{:S(2)}, u32[]{:S(2)}) collective-permute-start(f32[3,64,256]{2,1,0:T(8,128)S(1)} %owner_adam.15), channel_id=1, source_target_pairs={{0,124},{1,125},{2,126},{3,127},{4,120},{5,121},{6,122},{7,123},{8... | collective-permute-start | bytes 589832 | tf_op jit(solution)/shard_map/ppermute | solution.py:242
  (44 other events, 264.5 us)

commit v6 on v5

--- a/solution.py
+++ b/solution.py
@@ -252,7 +252,6 @@
 
     scores = teacher[0, 0]
     users = (user_factors, user_first, user_second)
-    user_bf = user_factors.astype(BF16)
 
     anywhere = pl.BlockSpec(memory_space=pl.ANY)
     own = pl.pallas_call(
@@ -267,7 +266,8 @@
     other = lax.ppermute(own, "rep", [(at, at ^ OWNERS) for at in range(reps)])
     copies = jnp.broadcast_to(own[0].astype(BF16)[None], (reps, shard, rank))
     items = lax.all_to_all(copies, "rep", 0, 0).reshape(item_rows, rank)
-    items, own, other, user_bf, meta = lax.optimization_barrier((items, own, other, user_bf, meta))
+    items, own, other, meta, factors = lax.optimization_barrier((items, own, other, meta, user_factors))
+    user_bf = factors.astype(BF16)
 
     parts_shape = [VMEM((2 * shard, rank), F32)] + [VMEM((2 * shard, rank), BF16)] * (OWNERS - 1)
     item_scratch = [VMEM((item_rows, rank), F32)]

time: 206 us -> 204 us (level)
    all_to_all x1, waiting for transfers between devices: 1.65 us -> 3.72 us  [on_device(): items = lax.all_to_all(copies, 'rep', 0, 0).reshape(item_rows, rank)]
  transfers between devices with their start and end apart: 63 -> 63, of which waited for: 49 -> 50; matrix products, arithmetic and copies ran while one was open for 3% -> 2% of each run, Pallas kernels for 6% -> 6%
where the time goes in v6:
time: 204 us; the launch traced here: 203 us
  waiting for transfers between devices  89.2 us (44%)
  starting transfers between devices  88.3 us (43%)
  Pallas kernels  19.9 us (10%)
  other arithmetic  3.57 us (2%)
    ppermute x29, starting transfers between devices, shifted(): return lax.ppermute(value, ('blk', 'rep'), moves(hop))  52.9 us
    ppermute x29, waiting for transfers between devices, shifted(): return lax.ppermute(value, ('blk', 'rep'), moves(hop))  34.3 us
    ppermute x24, waiting for transfers between devices, on_device(): lax.ppermute(parts[at + 1], 'rep', [(rep, rep ^ hop) for rep in range(rep...  27.3 us
    ppermute x24, starting transfers between devices, on_device(): lax.ppermute(parts[at + 1], 'rep', [(rep, rep ^ hop) for rep in range(rep...  25.8 us
    ppermute x8, waiting for transfers between devices, on_device(): lax.ppermute(mine, 'rep', [(at, at ^ OWNERS) for at in range(reps)])  23.9 us
    pallas_call x7, Pallas kernels, on_device(): pl.pallas_call(functools.partial(user_kernel, stratum, slots), in_specs=v...  8.76 us
    all_to_all x1, starting transfers between devices, on_device(): items = lax.all_to_all(copies, 'rep', 0, 0).reshape(item_rows, rank)  5.03 us
    pallas_call x7, Pallas kernels, on_device(): pl.pallas_call(functools.partial(item_kernel, stratum, slots), in_specs=v...  4.79 us
  transfers between devices with their start and end apart: 63, of which 50 were waited for; matrix products, arithmetic and copies ran while one was open for 2% of the time, Pallas kernels for 6%

profile of v6, /device:TPU:1, one launch (start us, length us, event | category | flops | bytes accessed | tf_op | source)
XLA Modules:
  0.0 203.0 jit_solution(14181327609172679046)
XLA Ops:
  4.7 5.0 %all-to-all-start = ((bf16[8,64,256]{2,1,0:T(8,128)(2,1)}), bf16[8,64,256]{2,1,0:T(8,128)(2,1)S(1)}, u32[]{:S(2)}, u32[]{:S(2)}) async-start(bf16[8,64,256]{2,1,0:T(8,128)(2,1)} %broadcast_in_dim.7), calls=%async_computation | async-start | bytes 524288 | tf_op jit(solution)/shard_map/all_to_all | solution.py:268
  12.1 3.7 %all-to-all-done = bf16[8,64,256]{2,1,0:T(8,128)(2,1)S(1)} async-done(((bf16[8,64,256]{2,1,0:T(8,128)(2,1)}), bf16[8,64,256]{2,1,0:T(8,128)(2,1)S(1)}, u32[]{:S(2)}, u32[]{:S(2)}) %all-to-all-start) | async-done | bytes 262176 | tf_op jit(solution)/shard_map/all_to_all | solution.py:268
  27.5 4.6 %collective-permute-start.5 = (f32[3,128,256]{2,1,0:T(8,128)S(1)}, f32[3,128,256]{2,1,0:T(8,128)S(1)}, u32[]{:S(2)}, u32[]{:S(2)}) collective-permute-start(f32[3,128,256]{2,1,0:T(8,128)S(1)} %get-tuple-element.141), channel_id=1, source_target_pairs={{0,124},{1,125},{2,126},{3,127},{4,120},{5,121},{6,122},{7,123},{8... | collective-permute-start | bytes 1179656 | tf_op jit(solution)/shard_map/ppermute | solution.py:242
  33.0 6.0 %collective-permute-start.7 = (bf16[128,256]{1,0:T(8,128)(2,1)S(1)}, bf16[128,256]{1,0:T(8,128)(2,1)S(1)}, u32[]{:S(2)}, u32[]{:S(2)}) collective-permute-start(bf16[128,256]{1,0:T(8,128)(2,1)S(1)} %get-tuple-element.142), channel_id=1, source_target_pairs={{0,127},{1,126},{2,125},{3,124},{4,123},{5,122},{6,121},{7,120},{8... | collective-permute-start | bytes 196616 | tf_op jit(solution)/shard_map/ppermute | solution.py:242
  42.2 2.6 %collective-permute-done.8.refs_3_ = bf16[128,256]{1,0:T(8,128)(2,1)S(1)} collective-permute-done((bf16[128,256]{1,0:T(8,128)(2,1)S(1)}, bf16[128,256]{1,0:T(8,128)(2,1)S(1)}, u32[]{:S(2)}, u32[]{:S(2)}) %collective-permute-start.8) | collective-permute-done | bytes 65568 | tf_op jit(solution)/shard_map/ppermute | solution.py:242
  46.7 2.7 %collective-permute-start.9 = (bf16[128,256]{1,0:T(8,128)(2,1)S(1)}, bf16[128,256]{1,0:T(8,128)(2,1)S(1)}, u32[]{:S(2)}, u32[]{:S(2)}) collective-permute-start(bf16[128,256]{1,0:T(8,128)(2,1)S(1)} %get-tuple-element.147), channel_id=1, source_target_pairs={{0,2},{1,3},{2,0},{3,1},{4,6},{5,7},{6,4},{7,5},{8,10},{9,11},{10,... | collective-permute-start | bytes 196616 | tf_op jit(solution)/shard_map/ppermute | solution.py:298
  52.7 3.5 %collective-permute-done.12.other = bf16[128,256]{1,0:T(8,128)(2,1)S(1)} collective-permute-done((bf16[128,256]{1,0:T(8,128)(2,1)S(1)}, bf16[128,256]{1,0:T(8,128)(2,1)S(1)}, u32[]{:S(2)}, u32[]{:S(2)}) %collective-permute-start.12) | collective-permute-done | bytes 65568 | tf_op jit(solution)/shard_map/ppermute | solution.py:307
  57.1 3.4 %collective-permute-start.14 = (bf16[128,256]{1,0:T(8,128)(2,1)S(1)}, bf16[128,256]{1,0:T(8,128)(2,1)S(1)}, u32[]{:S(2)}, u32[]{:S(2)}) collective-permute-start(bf16[128,256]{1,0:T(8,128)(2,1)S(1)} %get-tuple-element.153), channel_id=1, source_target_pairs={{0,126},{1,127},{2,124},{3,125},{4,122},{5,123},{6,120},{7,121},{8... | collective-permute-start | bytes 196616 | tf_op jit(solution)/shard_map/ppermute | solution.py:242
  63.6 3.4 %collective-permute-done.14.refs_1_ = bf16[128,256]{1,0:T(8,128)(2,1)S(1)} collective-permute-done((bf16[128,256]{1,0:T(8,128)(2,1)S(1)}, bf16[128,256]{1,0:T(8,128)(2,1)S(1)}, u32[]{:S(2)}, u32[]{:S(2)}) %collective-permute-start.14) | collective-permute-done | bytes 65568 | tf_op jit(solution)/shard_map/ppermute | solution.py:242
  75.2 3.1 %collective-permute-done.20.other = bf16[128,256]{1,0:T(8,128)(2,1)S(1)} collective-permute-done((bf16[128,256]{1,0:T(8,128)(2,1)S(1)}, bf16[128,256]{1,0:T(8,128)(2,1)S(1)}, u32[]{:S(2)}, u32[]{:S(2)}) %collective-permute-start.20) | collective-permute-done | bytes 65568 | tf_op jit(solution)/shard_map/ppermute | solution.py:307
  80.1 2.9 %collective-permute-start.22 = (bf16[128,256]{1,0:T(8,128)(2,1)S(1)}, bf16[128,256]{1,0:T(8,128)(2,1)S(1)}, u32[]{:S(2)}, u32[]{:S(2)}) collective-permute-start(bf16[128,256]{1,0:T(8,128)(2,1)S(1)} %get-tuple-element.168), channel_id=1, source_target_pairs={{0,126},{1,127},{2,124},{3,125},{4,122},{5,123},{6,120},{7,121},{8... | collective-permute-start | bytes 196616 | tf_op jit(solution)/shard_map/ppermute | solution.py:242
  85.5 3.3 %collective-permute-done.22.refs_1_ = bf16[128,256]{1,0:T(8,128)(2,1)S(1)} collective-permute-done((bf16[128,256]{1,0:T(8,128)(2,1)S(1)}, bf16[128,256]{1,0:T(8,128)(2,1)S(1)}, u32[]{:S(2)}, u32[]{:S(2)}) %collective-permute-start.22) | collective-permute-done | bytes 65568 | tf_op jit(solution)/shard_map/ppermute | solution.py:242
  97.7 3.1 %collective-permute-done.28.other = bf16[128,256]{1,0:T(8,128)(2,1)S(1)} collective-permute-done((bf16[128,256]{1,0:T(8,128)(2,1)S(1)}, bf16[128,256]{1,0:T(8,128)(2,1)S(1)}, u32[]{:S(2)}, u32[]{:S(2)}) %collective-permute-start.28) | collective-permute-done | bytes 65568 | tf_op jit(solution)/shard_map/ppermute | solution.py:307
  102.5 4.2 %collective-permute-start.30 = (bf16[128,256]{1,0:T(8,128)(2,1)S(1)}, bf16[128,256]{1,0:T(8,128)(2,1)S(1)}, u32[]{:S(2)}, u32[]{:S(2)}) collective-permute-start(bf16[128,256]{1,0:T(8,128)(2,1)S(1)} %get-tuple-element.183), channel_id=1, source_target_pairs={{0,126},{1,127},{2,124},{3,125},{4,122},{5,123},{6,120},{7,121},{8... | collective-permute-start | bytes 196616 | tf_op jit(solution)/shard_map/ppermute | solution.py:242
  121.3 3.1 %collective-permute-done.36.other = bf16[128,256]{1,0:T(8,128)(2,1)S(1)} collective-permute-done((bf16[128,256]{1,0:T(8,128)(2,1)S(1)}, bf16[128,256]{1,0:T(8,128)(2,1)S(1)}, u32[]{:S(2)}, u32[]{:S(2)}) %collective-permute-start.36) | collective-permute-done | bytes 65568 | tf_op jit(solution)/shard_map/ppermute | solution.py:307
  126.1 4.3 %collective-permute-start.38 = (bf16[128,256]{1,0:T(8,128)(2,1)S(1)}, bf16[128,256]{1,0:T(8,128)(2,1)S(1)}, u32[]{:S(2)}, u32[]{:S(2)}) collective-permute-start(bf16[128,256]{1,0:T(8,128)(2,1)S(1)} %get-tuple-element.198), channel_id=1, source_target_pairs={{0,126},{1,127},{2,124},{3,125},{4,122},{5,123},{6,120},{7,121},{8... | collective-permute-start | bytes 196616 | tf_op jit(solution)/shard_map/ppermute | solution.py:242
  132.7 2.5 %collective-permute-done.38.refs_1_ = bf16[128,256]{1,0:T(8,128)(2,1)S(1)} collective-permute-done((bf16[128,256]{1,0:T(8,128)(2,1)S(1)}, bf16[128,256]{1,0:T(8,128)(2,1)S(1)}, u32[]{:S(2)}, u32[]{:S(2)}) %collective-permute-start.38) | collective-permute-done | bytes 65568 | tf_op jit(solution)/shard_map/ppermute | solution.py:242
  144.9 3.1 %collective-permute-done.44.other = bf16[128,256]{1,0:T(8,128)(2,1)S(1)} collective-permute-done((bf16[128,256]{1,0:T(8,128)(2,1)S(1)}, bf16[128,256]{1,0:T(8,128)(2,1)S(1)}, u32[]{:S(2)}, u32[]{:S(2)}) %collective-permute-start.44) | collective-permute-done | bytes 65568 | tf_op jit(solution)/shard_map/ppermute | solution.py:307
  149.7 4.3 %collective-permute-start.46 = (bf16[128,256]{1,0:T(8,128)(2,1)S(1)}, bf16[128,256]{1,0:T(8,128)(2,1)S(1)}, u32[]{:S(2)}, u32[]{:S(2)}) collective-permute-start(bf16[128,256]{1,0:T(8,128)(2,1)S(1)} %get-tuple-element.213), channel_id=1, source_target_pairs={{0,126},{1,127},{2,124},{3,125},{4,122},{5,123},{6,120},{7,121},{8... | collective-permute-start | bytes 196616 | tf_op jit(solution)/shard_map/ppermute | solution.py:242
  168.5 3.1 %collective-permute-done.52.other = bf16[128,256]{1,0:T(8,128)(2,1)S(1)} collective-permute-done((bf16[128,256]{1,0:T(8,128)(2,1)S(1)}, bf16[128,256]{1,0:T(8,128)(2,1)S(1)}, u32[]{:S(2)}, u32[]{:S(2)}) %collective-permute-start.52) | collective-permute-done | bytes 65568 | tf_op jit(solution)/shard_map/ppermute | solution.py:307
  173.4 4.3 %collective-permute-start.54 = (bf16[128,256]{1,0:T(8,128)(2,1)S(1)}, bf16[128,256]{1,0:T(8,128)(2,1)S(1)}, u32[]{:S(2)}, u32[]{:S(2)}) collective-permute-start(bf16[128,256]{1,0:T(8,128)(2,1)S(1)} %get-tuple-element.228), channel_id=1, source_target_pairs={{0,126},{1,127},{2,124},{3,125},{4,122},{5,123},{6,120},{7,121},{8... | collective-permute-start | bytes 196616 | tf_op jit(solution)/shard_map/ppermute | solution.py:242
  179.9 2.5 %collective-permute-done.54.refs_1_ = bf16[128,256]{1,0:T(8,128)(2,1)S(1)} collective-permute-done((bf16[128,256]{1,0:T(8,128)(2,1)S(1)}, bf16[128,256]{1,0:T(8,128)(2,1)S(1)}, u32[]{:S(2)}, u32[]{:S(2)}) %collective-permute-start.54) | collective-permute-done | bytes 65568 | tf_op jit(solution)/shard_map/ppermute | solution.py:242
  192.1 3.1 %collective-permute-done.60.other = bf16[128,256]{1,0:T(8,128)(2,1)S(1)} collective-permute-done((bf16[128,256]{1,0:T(8,128)(2,1)S(1)}, bf16[128,256]{1,0:T(8,128)(2,1)S(1)}, u32[]{:S(2)}, u32[]{:S(2)}) %collective-permute-start.60) | collective-permute-done | bytes 65568 | tf_op jit(solution)/shard_map/ppermute | solution.py:307
  197.0 2.7 %last_user_adam.1 = (f32[1024,256]{1,0:T(8,128)}, f32[1024,256]{1,0:T(8,128)}, f32[1024,256]{1,0:T(8,128)}) custom-call(s32[8,2,128]{2,1,0:T(2,128)S(1)} %broadcast_in_dim.8.meta, bf16[512,256]{1,0:T(8,128)(2,1)S(1)} %get-tuple-element.235.items, bf16[8,128,128]{2,1,0:T(8,128)(2,1)S(1)} %get-tuple-element.241.residual, ...), custom_call_target="tpu_custom_call" | custom-call | flops 300000000 | bytes 8000000 | tf_op jit(solution)/shard_map/last_user_adam/pallas_call | solution.py:321
  (155 shorter events, 117.4 us)
Async XLA Ops:
  1.7 10.4 %collective-permute-start = (f32[3,64,256]{2,1,0:T(8,128)S(1)}, f32[3,64,256]{2,1,0:T(8,128)S(1)}, u32[]{:S(2)}, u32[]{:S(2)}) collective-permute-start(f32[3,64,256]{2,1,0:T(8,128)S(1)} %start.1.own), channel_id=1, source_target_pairs={{0,4},{1,5},{2,6},{3,7},{4,0},{5,1},{6,2},{7,3},{8,12},{9,13},{10,... | collective-permute-start | bytes 589832 | tf_op jit(solution)/shard_map/ppermute | solution.py:266
  4.7 11.2 %all-to-all-start = ((bf16[8,64,256]{2,1,0:T(8,128)(2,1)}), bf16[8,64,256]{2,1,0:T(8,128)(2,1)S(1)}, u32[]{:S(2)}, u32[]{:S(2)}) async-start(bf16[8,64,256]{2,1,0:T(8,128)(2,1)} %broadcast_in_dim.7), calls=%async_computation | async-start | bytes 524288 | tf_op jit(solution)/shard_map/all_to_all | solution.py:268
  27.5 17.3 %collective-permute-start.5 = (f32[3,128,256]{2,1,0:T(8,128)S(1)}, f32[3,128,256]{2,1,0:T(8,128)S(1)}, u32[]{:S(2)}, u32[]{:S(2)}) collective-permute-start(f32[3,128,256]{2,1,0:T(8,128)S(1)} %get-tuple-element.141), channel_id=1, source_target_pairs={{0,124},{1,125},{2,126},{3,127},{4,120},{5,121},{6,122},{7,123},{8... | collective-permute-start | bytes 1179656 | tf_op jit(solution)/shard_map/ppermute | solution.py:242
  32.1 9.0 %collective-permute-start.6 = (bf16[128,256]{1,0:T(8,128)(2,1)S(1)}, bf16[128,256]{1,0:T(8,128)(2,1)S(1)}, u32[]{:S(2)}, u32[]{:S(2)}) collective-permute-start(bf16[128,256]{1,0:T(8,128)(2,1)S(1)} %get-tuple-element.142), channel_id=1, source_target_pairs={{0,126},{1,127},{2,124},{3,125},{4,122},{5,123},{6,120},{7,121},{8... | collective-permute-start | bytes 196616 | tf_op jit(solution)/shard_map/ppermute | solution.py:242
  33.0 9.2 %collective-permute-start.7 = (bf16[128,256]{1,0:T(8,128)(2,1)S(1)}, bf16[128,256]{1,0:T(8,128)(2,1)S(1)}, u32[]{:S(2)}, u32[]{:S(2)}) collective-permute-start(bf16[128,256]{1,0:T(8,128)(2,1)S(1)} %get-tuple-element.142), channel_id=1, source_target_pairs={{0,127},{1,126},{2,125},{3,124},{4,123},{5,122},{6,121},{7,120},{8... | collective-permute-start | bytes 196616 | tf_op jit(solution)/shard_map/ppermute | solution.py:242
  56.3 11.6 %collective-permute-start.13 = (f32[3,128,256]{2,1,0:T(8,128)S(1)}, f32[3,128,256]{2,1,0:T(8,128)S(1)}, u32[]{:S(2)}, u32[]{:S(2)}) collective-permute-start(f32[3,128,256]{2,1,0:T(8,128)S(1)} %get-tuple-element.152), channel_id=1, source_target_pairs={{0,124},{1,125},{2,126},{3,127},{4,120},{5,121},{6,122},{7,123},{8... | collective-permute-start | bytes 1179656 | tf_op jit(solution)/shard_map/ppermute | solution.py:242
  57.1 9.9 %collective-permute-start.14 = (bf16[128,256]{1,0:T(8,128)(2,1)S(1)}, bf16[128,256]{1,0:T(8,128)(2,1)S(1)}, u32[]{:S(2)}, u32[]{:S(2)}) collective-permute-start(bf16[128,256]{1,0:T(8,128)(2,1)S(1)} %get-tuple-element.153), channel_id=1, source_target_pairs={{0,126},{1,127},{2,124},{3,125},{4,122},{5,123},{6,120},{7,121},{8... | collective-permute-start | bytes 196616 | tf_op jit(solution)/shard_map/ppermute | solution.py:242
  60.5 7.1 %collective-permute-start.15 = (bf16[128,256]{1,0:T(8,128)(2,1)S(1)}, bf16[128,256]{1,0:T(8,128)(2,1)S(1)}, u32[]{:S(2)}, u32[]{:S(2)}) collective-permute-start(bf16[128,256]{1,0:T(8,128)(2,1)S(1)} %get-tuple-element.153), channel_id=1, source_target_pairs={{0,127},{1,126},{2,125},{3,124},{4,123},{5,122},{6,121},{7,120},{8... | collective-permute-start | bytes 196616 | tf_op jit(solution)/shard_map/ppermute | solution.py:242
  78.5 11.6 %collective-permute-start.21 = (f32[3,128,256]{2,1,0:T(8,128)S(1)}, f32[3,128,256]{2,1,0:T(8,128)S(1)}, u32[]{:S(2)}, u32[]{:S(2)}) collective-permute-start(f32[3,128,256]{2,1,0:T(8,128)S(1)} %get-tuple-element.167), channel_id=1, source_target_pairs={{0,124},{1,125},{2,126},{3,127},{4,120},{5,121},{6,122},{7,123},{8... | collective-permute-start | bytes 1179656 | tf_op jit(solution)/shard_map/ppermute | solution.py:242
  80.1 8.7 %collective-permute-start.22 = (bf16[128,256]{1,0:T(8,128)(2,1)S(1)}, bf16[128,256]{1,0:T(8,128)(2,1)S(1)}, u32[]{:S(2)}, u32[]{:S(2)}) collective-permute-start(bf16[128,256]{1,0:T(8,128)(2,1)S(1)} %get-tuple-element.168), channel_id=1, source_target_pairs={{0,126},{1,127},{2,124},{3,125},{4,122},{5,123},{6,120},{7,121},{8... | collective-permute-start | bytes 196616 | tf_op jit(solution)/shard_map/ppermute | solution.py:242
  83.0 7.0 %collective-permute-start.23 = (bf16[128,256]{1,0:T(8,128)(2,1)S(1)}, bf16[128,256]{1,0:T(8,128)(2,1)S(1)}, u32[]{:S(2)}, u32[]{:S(2)}) collective-permute-start(bf16[128,256]{1,0:T(8,128)(2,1)S(1)} %get-tuple-element.168), channel_id=1, source_target_pairs={{0,127},{1,126},{2,125},{3,124},{4,123},{5,122},{6,121},{7,120},{8... | collective-permute-start | bytes 196616 | tf_op jit(solution)/shard_map/ppermute | solution.py:242
  100.9 12.9 %collective-permute-start.29 = (f32[3,128,256]{2,1,0:T(8,128)S(1)}, f32[3,128,256]{2,1,0:T(8,128)S(1)}, u32[]{:S(2)}, u32[]{:S(2)}) collective-permute-start(f32[3,128,256]{2,1,0:T(8,128)S(1)} %get-tuple-element.182), channel_id=1, source_target_pairs={{0,124},{1,125},{2,126},{3,127},{4,120},{5,121},{6,122},{7,123},{8... | collective-permute-start | bytes 1179656 | tf_op jit(solution)/shard_map/ppermute | solution.py:242
  102.5 9.0 %collective-permute-start.30 = (bf16[128,256]{1,0:T(8,128)(2,1)S(1)}, bf16[128,256]{1,0:T(8,128)(2,1)S(1)}, u32[]{:S(2)}, u32[]{:S(2)}) collective-permute-start(bf16[128,256]{1,0:T(8,128)(2,1)S(1)} %get-tuple-element.183), channel_id=1, source_target_pairs={{0,126},{1,127},{2,124},{3,125},{4,122},{5,123},{6,120},{7,121},{8... | collective-permute-start | bytes 196616 | tf_op jit(solution)/shard_map/ppermute | solution.py:242
  106.8 7.0 %collective-permute-start.31 = (bf16[128,256]{1,0:T(8,128)(2,1)S(1)}, bf16[128,256]{1,0:T(8,128)(2,1)S(1)}, u32[]{:S(2)}, u32[]{:S(2)}) collective-permute-start(bf16[128,256]{1,0:T(8,128)(2,1)S(1)} %get-tuple-element.183), channel_id=1, source_target_pairs={{0,127},{1,126},{2,125},{3,124},{4,123},{5,122},{6,121},{7,120},{8... | collective-permute-start | bytes 196616 | tf_op jit(solution)/shard_map/ppermute | solution.py:242
  124.5 12.9 %collective-permute-start.37 = (f32[3,128,256]{2,1,0:T(8,128)S(1)}, f32[3,128,256]{2,1,0:T(8,128)S(1)}, u32[]{:S(2)}, u32[]{:S(2)}) collective-permute-start(f32[3,128,256]{2,1,0:T(8,128)S(1)} %get-tuple-element.197), channel_id=1, source_target_pairs={{0,124},{1,125},{2,126},{3,127},{4,120},{5,121},{6,122},{7,123},{8... | collective-permute-start | bytes 1179656 | tf_op jit(solution)/shard_map/ppermute | solution.py:242
  126.1 9.0 %collective-permute-start.38 = (bf16[128,256]{1,0:T(8,128)(2,1)S(1)}, bf16[128,256]{1,0:T(8,128)(2,1)S(1)}, u32[]{:S(2)}, u32[]{:S(2)}) collective-permute-start(bf16[128,256]{1,0:T(8,128)(2,1)S(1)} %get-tuple-element.198), channel_id=1, source_target_pairs={{0,126},{1,127},{2,124},{3,125},{4,122},{5,123},{6,120},{7,121},{8... | collective-permute-start | bytes 196616 | tf_op jit(solution)/shard_map/ppermute | solution.py:242
  130.4 7.0 %collective-permute-start.39 = (bf16[128,256]{1,0:T(8,128)(2,1)S(1)}, bf16[128,256]{1,0:T(8,128)(2,1)S(1)}, u32[]{:S(2)}, u32[]{:S(2)}) collective-permute-start(bf16[128,256]{1,0:T(8,128)(2,1)S(1)} %get-tuple-element.198), channel_id=1, source_target_pairs={{0,127},{1,126},{2,125},{3,124},{4,123},{5,122},{6,121},{7,120},{8... | collective-permute-start | bytes 196616 | tf_op jit(solution)/shard_map/ppermute | solution.py:242
  148.1 12.9 %collective-permute-start.45 = (f32[3,128,256]{2,1,0:T(8,128)S(1)}, f32[3,128,256]{2,1,0:T(8,128)S(1)}, u32[]{:S(2)}, u32[]{:S(2)}) collective-permute-start(f32[3,128,256]{2,1,0:T(8,128)S(1)} %get-tuple-element.212), channel_id=1, source_target_pairs={{0,124},{1,125},{2,126},{3,127},{4,120},{5,121},{6,122},{7,123},{8... | collective-permute-start | bytes 1179656 | tf_op jit(solution)/shard_map/ppermute | solution.py:242
  149.7 9.0 %collective-permute-start.46 = (bf16[128,256]{1,0:T(8,128)(2,1)S(1)}, bf16[128,256]{1,0:T(8,128)(2,1)S(1)}, u32[]{:S(2)}, u32[]{:S(2)}) collective-permute-start(bf16[128,256]{1,0:T(8,128)(2,1)S(1)} %get-tuple-element.213), channel_id=1, source_target_pairs={{0,126},{1,127},{2,124},{3,125},{4,122},{5,123},{6,120},{7,121},{8... | collective-permute-start | bytes 196616 | tf_op jit(solution)/shard_map/ppermute | solution.py:242
  154.0 7.0 %collective-permute-start.47 = (bf16[128,256]{1,0:T(8,128)(2,1)S(1)}, bf16[128,256]{1,0:T(8,128)(2,1)S(1)}, u32[]{:S(2)}, u32[]{:S(2)}) collective-permute-start(bf16[128,256]{1,0:T(8,128)(2,1)S(1)} %get-tuple-element.213), channel_id=1, source_target_pairs={{0,127},{1,126},{2,125},{3,124},{4,123},{5,122},{6,121},{7,120},{8... | collective-permute-start | bytes 196616 | tf_op jit(solution)/shard_map/ppermute | solution.py:242
  171.7 12.9 %collective-permute-start.53 = (f32[3,128,256]{2,1,0:T(8,128)S(1)}, f32[3,128,256]{2,1,0:T(8,128)S(1)}, u32[]{:S(2)}, u32[]{:S(2)}) collective-permute-start(f32[3,128,256]{2,1,0:T(8,128)S(1)} %get-tuple-element.227), channel_id=1, source_target_pairs={{0,124},{1,125},{2,126},{3,127},{4,120},{5,121},{6,122},{7,123},{8... | collective-permute-start | bytes 1179656 | tf_op jit(solution)/shard_map/ppermute | solution.py:242
  173.4 9.0 %collective-permute-start.54 = (bf16[128,256]{1,0:T(8,128)(2,1)S(1)}, bf16[128,256]{1,0:T(8,128)(2,1)S(1)}, u32[]{:S(2)}, u32[]{:S(2)}) collective-permute-start(bf16[128,256]{1,0:T(8,128)(2,1)S(1)} %get-tuple-element.228), channel_id=1, source_target_pairs={{0,126},{1,127},{2,124},{3,125},{4,122},{5,123},{6,120},{7,121},{8... | collective-permute-start | bytes 196616 | tf_op jit(solution)/shard_map/ppermute | solution.py:242
  177.6 7.0 %collective-permute-start.55 = (bf16[128,256]{1,0:T(8,128)(2,1)S(1)}, bf16[128,256]{1,0:T(8,128)(2,1)S(1)}, u32[]{:S(2)}, u32[]{:S(2)}) collective-permute-start(bf16[128,256]{1,0:T(8,128)(2,1)S(1)} %get-tuple-element.228), channel_id=1, source_target_pairs={{0,127},{1,126},{2,125},{3,124},{4,123},{5,122},{6,121},{7,120},{8... | collective-permute-start | bytes 196616 | tf_op jit(solution)/shard_map/ppermute | solution.py:242
  195.3 6.7 %collective-permute-start.61 = (f32[3,64,256]{2,1,0:T(8,128)S(1)}, f32[3,64,256]{2,1,0:T(8,128)S(1)}, u32[]{:S(2)}, u32[]{:S(2)}) collective-permute-start(f32[3,64,256]{2,1,0:T(8,128)S(1)} %owner_adam.15), channel_id=1, source_target_pairs={{0,124},{1,125},{2,126},{3,127},{4,120},{5,121},{6,122},{7,123},{8... | collective-permute-start | bytes 589832 | tf_op jit(solution)/shard_map/ppermute | solution.py:242
  (43 other events, 257.7 us)
